TPU v7x, 512 devices: a whole 4x8x8 slice. The times are simulated.
512 devices in a mesh: grp: 16 (over y, core), exp: 32 (over x, z).
Axes of the slice: x: 4, y: 8, z: 8, core: 2. Of those that a mesh axis runs over, the one named last changes fastest.
Arguments:
- tokens: bfloat16 [67584, 4096], P(('grp', 'exp')), may hold values from -6 to 6
- routes: int32 [67584, 2], P(('grp', 'exp')), may hold values from 0 to 63, as said below
- gate_values: float32 [67584, 2], P(('grp', 'exp')), may hold values from 0.1 to 1
- dense_up: bfloat16 [4, 4096, 2688], P(None, ('grp', 'exp')), may hold values from -0.09375 to 0.09375
- dense_down: bfloat16 [4, 4096, 2688], P(None, ('grp', 'exp')), may hold values from -0.125 to 0.125
- up_noise: bfloat16 [4096, 10752], P(None, 'exp'), may hold values from -0.046875 to 0.046875
Outputs:
- mixed: bfloat16 [67584, 4096], P(('grp', 'exp'))
Inputs may be any that keep to these rules, and one draw needn't show every extreme that they name: `routes`: each row names two different experts. The rows of one device name no expert more than 11 times, and in every group some expert below 4 is named exactly 11 times by each of the group's devices.
All inputs are finite; a program needn't handle non-finite values.
Results may differ from a plain program's by a relative error of at most 0.0067.
Values may be sent and summed in bfloat16 or wider, within the bound.
No kernel may reach another device: no remote copies, remote signals or barrier semaphores. Data moves between devices by JAX's collectives and lax.ppermute only.
A program may use at most 128 MiB of HBM per device.

v0:
```python
import jax
import jax.numpy as jnp
from jax import lax
from jax.sharding import PartitionSpec as P


def spread(weights, blocks, unit_count):
    flight, row_count, unit_total = weights.shape
    reshaped = weights.reshape(flight, row_count, blocks, unit_count).transpose(0, 2, 1, 3)
    return reshaped.reshape(flight * blocks, row_count, unit_count)


def regroup(pieces, groups):
    owners, row_count, unit_total = pieces.shape
    reshaped = pieces.reshape(owners, groups, row_count // groups, unit_total).transpose(1, 0, 2, 3)
    return reshaped.reshape(owners * row_count, unit_total)


def on_device(tokens, routes, gate_values, dense_up, dense_down, up_noise):
    groups = lax.axis_size("grp")
    owners = lax.axis_size("exp")
    flight = dense_up.shape[0]
    blocks = owners // flight
    model_width = tokens.shape[1]
    tok_rows = tokens.shape[0]
    unit_count = up_noise.shape[1]
    slot_total = tok_rows // 12
    full_up, full_down = (
        lax.all_gather(dense_up, "grp", axis=1, tiled=True),
        lax.all_gather(dense_down, "grp", axis=1, tiled=True),
    )
    got_up, got_down = (
        lax.all_to_all(
            spread(full_up, blocks, unit_count), "exp", split_axis=0, concat_axis=0, tiled=True
        ),
        lax.all_to_all(
            spread(full_down, blocks, unit_count), "exp", split_axis=0, concat_axis=0, tiled=True
        ),
    )
    base_up = regroup(got_up, groups)
    base_down = regroup(got_down, groups)
    up_weight = (base_up.astype(jnp.float32) + up_noise.astype(jnp.float32)).astype(jnp.bfloat16)
    labels = jnp.arange(flight, dtype=jnp.int32)
    chosen = routes[:, :, None] == labels[None, None, :]
    present = jnp.any(chosen, axis=1).astype(jnp.int32)
    before = jnp.cumsum(present, axis=0) - present
    slot_ids = jnp.arange(slot_total, dtype=jnp.int32)
    placed = present[:, :, None] * (before[:, :, None] == slot_ids[None, None, :]).astype(jnp.int32)
    selector = placed.reshape(tok_rows, flight * slot_total).astype(jnp.bfloat16)
    outgoing = lax.dot_general(
        selector, tokens, (((0,), (0,)), ((), ())), preferred_element_type=jnp.float32
    ).astype(jnp.bfloat16)
    copies = jnp.broadcast_to(
        outgoing.reshape(flight, 1, slot_total, model_width),
        (flight, blocks, slot_total, model_width),
    ).reshape(owners, slot_total, model_width)
    rows_in = lax.all_to_all(copies, "exp", split_axis=0, concat_axis=0, tiled=True)
    source_count, slot_count, _ = rows_in.shape
    flat_rows = rows_in.reshape(source_count * slot_count, model_width)
    preact = jnp.dot(flat_rows, up_weight, preferred_element_type=jnp.float32)
    hidden = jnp.square(jnp.maximum(preact, 0.0)).astype(jnp.bfloat16)
    partial_value = lax.dot_general(
        hidden, base_down, (((1,), (1,)), ((), ())), preferred_element_type=jnp.float32
    )
    block_parts = partial_value.astype(jnp.bfloat16).reshape(source_count, slot_count, model_width)
    received = lax.all_to_all(block_parts, "exp", split_axis=0, concat_axis=0, tiled=True)
    totals = jnp.sum(
        received.astype(jnp.float32).reshape(flight, blocks, slot_total, model_width), axis=1
    )
    totals = totals.reshape(flight * slot_total, model_width)
    weights = jnp.sum(jnp.where(chosen, gate_values[:, :, None], jnp.float32(0.0)), axis=1)
    mixing = (placed.astype(jnp.float32) * weights[:, :, None]).reshape(
        tok_rows, flight * slot_total
    )
    mixed = jnp.dot(
        mixing, totals, precision=lax.Precision.HIGHEST, preferred_element_type=jnp.float32
    )
    return mixed.astype(jnp.bfloat16)


def solution(mesh):
    return jax.shard_map(
        on_device,
        mesh=mesh,
        in_specs=(
            P(("grp", "exp"), None),
            P(("grp", "exp"), None),
            P(("grp", "exp"), None),
            P(None, ("grp", "exp"), None),
            P(None, ("grp", "exp"), None),
            P(None, "exp"),
        ),
        out_specs=P(("grp", "exp"), None),
        check_vma=False,
    )
```

profile of v0, /device:TPU:32, one launch (start us, length us, event | category | flops | bytes accessed | tf_op | source)
XLA Modules:
  0.0 405.4 jit_solution(15057521329213488610)
XLA Ops:
  6.5 0.0 copy-start
  6.5 0.8 fusion.14
  7.4 1.2 reduce-window.6
  8.6 0.1 slice.12
  8.7 0.1 copy.45
  8.8 0.1 copy.46
  8.9 0.1 add_bitcast_fusion
  9.1 0.1 eq.45
  9.1 0.0 copy-done
  9.1 0.4 convolution_convert_fusion.1
  9.5 0.1 broadcast_in_dim.28
  9.7 2.5 broadcast_in_dim.29
  12.2 13.4 %all-to-all-start = ((bf16[32,11,4096]{2,1,0:T(8,128)(2,1)}), bf16[32,11,4096]{2,1,0:T(8,128)(2,1)}, u32[]{:S(2)}, u32[]{:S(2)}) async-start(bf16[32,11,4096]{2,1,0:T(8,128)(2,1)} %bitcast.49), calls=%async_computation | async-start | bytes 8388608 | tf_op jit(solution)/shard_map/all_to_all | solution.py:57
  25.6 0.0 all-gather.3.cloned.1.call-start
  25.7 0.0 copy-done.3
  25.7 0.7 copy.47
  26.4 0.0 all-gather.3.cloned.1.call-update
  26.4 43.4 %all-gather.3.cloned.1.call-done = bf16[4,128,2688]{2,0,1:T(4,128)(2,1)} async-done(((bf16[4,8,2688]{2,0,1:T(4,128)(2,1)}), bf16[4,128,2688]{2,0,1:T(4,128)(2,1)}) %all-gather.3.cloned.1.call-update) | async-done | bytes 2752528 | tf_op jit(solution)/shard_map/all_gather | solution.py:29
  69.9 6.0 %copy.48 = bf16[4,128,2688]{1,2,0:T(8,128)(2,1)} copy(bf16[4,128,2688]{2,0,1:T(4,128)(2,1)} %all-gather.3.cloned.1.call-done) | data formatting | bytes 5505024 | tf_op jit(solution)/shard_map/all_gather | solution.py:29
  75.8 47.0 %all-to-all-done = bf16[32,11,4096]{2,1,0:T(8,128)(2,1)} async-done(((bf16[32,11,4096]{2,1,0:T(8,128)(2,1)}), bf16[32,11,4096]{2,1,0:T(8,128)(2,1)}, u32[]{:S(2)}, u32[]{:S(2)}) %all-to-all-start) | async-done | bytes 2883616 | tf_op jit(solution)/shard_map/all_to_all | solution.py:57
  122.8 5.0 %all-to-all-start.1 = ((bf16[32,128,336]{1,2,0:T(8,128)(2,1)}), bf16[32,128,336]{1,2,0:T(8,128)(2,1)}, u32[]{:S(2)}, u32[]{:S(2)}) async-start(bf16[32,128,336]{1,2,0:T(8,128)(2,1)} %bitcast.51), calls=%async_computation.1 | async-start | bytes 5505024 | tf_op jit(solution)/shard_map/all_to_all | solution.py:33
  127.9 0.0 all-gather.5.cloned.1.call-start
  127.9 0.0 copy-done.4
  127.9 0.7 copy.52
  128.7 0.0 all-gather.5.cloned.1.call-update
  128.7 43.5 %all-gather.5.cloned.1.call-done = bf16[4,128,2688]{2,0,1:T(4,128)(2,1)} async-done(((bf16[4,8,2688]{2,0,1:T(4,128)(2,1)}), bf16[4,128,2688]{2,0,1:T(4,128)(2,1)}) %all-gather.5.cloned.1.call-update) | async-done | bytes 2752528 | tf_op jit(solution)/shard_map/all_gather | solution.py:30
  172.1 5.9 %copy.53 = bf16[4,128,2688]{1,2,0:T(8,128)(2,1)} copy(bf16[4,128,2688]{2,0,1:T(4,128)(2,1)} %all-gather.5.cloned.1.call-done) | data formatting | bytes 5505024 | tf_op jit(solution)/shard_map/all_gather | solution.py:30
  178.1 15.9 %all-to-all-done.1 = bf16[32,128,336]{1,2,0:T(8,128)(2,1)} async-done(((bf16[32,128,336]{1,2,0:T(8,128)(2,1)}), bf16[32,128,336]{1,2,0:T(8,128)(2,1)}, u32[]{:S(2)}, u32[]{:S(2)}) %all-to-all-start.1) | async-done | bytes 2752544 | tf_op jit(solution)/shard_map/all_to_all | solution.py:33
  193.9 4.8 %all-to-all-start.2 = ((bf16[32,128,336]{1,2,0:T(8,128)(2,1)}), bf16[32,128,336]{1,2,0:T(8,128)(2,1)}, u32[]{:S(2)}, u32[]{:S(2)}) async-start(bf16[32,128,336]{1,2,0:T(8,128)(2,1)} %bitcast.52), calls=%async_computation.2 | async-start | bytes 5505024 | tf_op jit(solution)/shard_map/all_to_all | solution.py:36
  198.7 4.7 %copy.51 = bf16[4096,336]{1,0:T(8,128)(2,1)} copy(bf16[4096,336]{0,1:T(8,128)(2,1)} %param.11) | data formatting | bytes 5505024 | tf_op args[5]
  203.4 4.9 %reshape.68 = bf16[352,4096]{1,0:T(8,128)(2,1)} reshape(bf16[32,11,4096]{2,1,0:T(8,128)(2,1)} %all-to-all-done) | data formatting | bytes 5767168 | tf_op jit(solution)/shard_map/reshape | solution.py:59
  208.3 5.3 %copy.49 = f32[32,128,336]{2,1,0:T(8,128)} copy(bf16[32,128,336]{1,2,0:T(8,128)(2,1)} %all-to-all-done.1) | data formatting | bytes 8257536 | tf_op jit(solution)/shard_map/convert_element_type | solution.py:42
  213.5 6.1 %copy.50 = f32[16,32,8,336]{3,2,1,0:T(8,128)} copy(f32[16,32,8,336]{3,2,0,1:T(8,128)} %bitcast.48) | data formatting | bytes 11010048 | tf_op jit(solution)/shard_map/convert_element_type | solution.py:42
  219.6 44.6 %all-to-all-done.2 = bf16[32,128,336]{1,2,0:T(8,128)(2,1)} async-done(((bf16[32,128,336]{1,2,0:T(8,128)(2,1)}), bf16[32,128,336]{1,2,0:T(8,128)(2,1)}, u32[]{:S(2)}, u32[]{:S(2)}) %all-to-all-start.2) | async-done | bytes 2752544 | tf_op jit(solution)/shard_map/all_to_all | solution.py:36
  264.3 4.6 %copy.54 = bf16[32,128,336]{2,1,0:T(8,128)(2,1)} copy(bf16[32,128,336]{1,2,0:T(8,128)(2,1)} %all-to-all-done.2) | data formatting | bytes 5505024 | tf_op jit(solution)/shard_map/all_to_all | solution.py:36
  268.9 4.2 %copy.55 = bf16[16,32,8,336]{3,2,1,0:T(8,128)(2,1)} copy(bf16[16,32,8,336]{3,2,0,1:T(8,128)(2,1)} %bitcast.50) | data formatting | bytes 5505024 | tf_op jit(solution)/shard_map/transpose | solution.py:15
  273.1 0.0 copy-done.2
  273.1 4.6 %fusion = bf16[4096,336]{1,0:T(8,128)(2,1)} fusion(f32[16,32,8,336]{3,2,1,0:T(8,128)S(1)} %copy-done.2, bf16[4096,336]{1,0:T(8,128)(2,1)} %copy.51), kind=kLoop, calls=%fused_computation.2 | loop fusion | flops 4128768 | bytes 11010048 | tf_op jit(solution)/shard_map/convert_element_type | solution.py:42
  277.8 8.6 %convolution_convert_fusion = bf16[352,4096]{1,0:T(8,128)(2,1)} fusion(bf16[4096,336]{1,0:T(8,128)(2,1)} %bitcast.53, bf16[352,4096]{1,0:T(8,128)(2,1)} %reshape.68, bf16[4096,336]{1,0:T(8,128)(2,1)} %fusion), kind=kOutput, calls=%fused_computation.3 | convolution fusion | flops 1939565056 | bytes 11272192 | tf_op jit(solution)/shard_map/dot_general | solution.py:62
  286.3 4.8 %reshape.75 = bf16[32,11,4096]{2,1,0:T(8,128)(2,1)} reshape(bf16[352,4096]{1,0:T(8,128)(2,1)} %convolution_convert_fusion) | data formatting | bytes 5767168 | tf_op jit(solution)/shard_map/reshape | solution.py:65
  291.1 5.2 %all-to-all-start.3 = ((bf16[32,11,4096]{2,1,0:T(8,128)(2,1)}), bf16[32,11,4096]{2,1,0:T(8,128)(2,1)}, u32[]{:S(2)}, u32[]{:S(2)}) async-start(bf16[32,11,4096]{2,1,0:T(8,128)(2,1)} %reshape.75), calls=%async_computation.3 | async-start | bytes 8388608 | tf_op jit(solution)/shard_map/all_to_all | solution.py:66
  296.3 0.0 copy-done.5
  296.3 0.0 copy-done.6
  296.3 0.0 copy-start.1
  296.3 96.2 %all-to-all-done.3 = bf16[32,11,4096]{2,1,0:T(8,128)(2,1)} async-done(((bf16[32,11,4096]{2,1,0:T(8,128)(2,1)}), bf16[32,11,4096]{2,1,0:T(8,128)(2,1)}, u32[]{:S(2)}, u32[]{:S(2)}) %all-to-all-start.3) | async-done | bytes 2883616 | tf_op jit(solution)/shard_map/all_to_all | solution.py:66
  392.6 3.0 convert_reduce_fusion
  395.6 2.9 fusion.1
  398.5 0.0 copy-done.1
  (18 shorter events, 0.1 us)
Async XLA Ops:
  6.5 2.6 copy-start
  12.2 13.5 %copy-start.3 = (bf16[4,8,2688]{2,1,0:T(8,128)(2,1)S(1)}, bf16[4,8,2688]{2,1,0:T(8,128)(2,1)}, u32[]{:S(2)}) copy-start(bf16[4,8,2688]{2,1,0:T(8,128)(2,1)} %param.9) | copy-start | bytes 516100
  12.2 110.6 %all-to-all-start = ((bf16[32,11,4096]{2,1,0:T(8,128)(2,1)}), bf16[32,11,4096]{2,1,0:T(8,128)(2,1)}, u32[]{:S(2)}, u32[]{:S(2)}) async-start(bf16[32,11,4096]{2,1,0:T(8,128)(2,1)} %bitcast.49), calls=%async_computation | async-start | bytes 8388608 | tf_op jit(solution)/shard_map/all_to_all | solution.py:57
  25.6 44.3 %all-gather.3.cloned.1.call-start = ((), (), s32[]{:S(2)}) async-start(), calls=%async_computation.4 | async-start | bytes 2924544 | tf_op jit(solution)/shard_map/all_gather | solution.py:29
  75.8 52.1 %copy-start.4 = (bf16[4,8,2688]{2,1,0:T(8,128)(2,1)S(1)}, bf16[4,8,2688]{2,1,0:T(8,128)(2,1)}, u32[]{:S(2)}) copy-start(bf16[4,8,2688]{2,1,0:T(8,128)(2,1)} %param.10) | copy-start | bytes 516100
  122.8 71.1 %all-to-all-start.1 = ((bf16[32,128,336]{1,2,0:T(8,128)(2,1)}), bf16[32,128,336]{1,2,0:T(8,128)(2,1)}, u32[]{:S(2)}, u32[]{:S(2)}) async-start(bf16[32,128,336]{1,2,0:T(8,128)(2,1)} %bitcast.51), calls=%async_computation.1 | async-start | bytes 5505024 | tf_op jit(solution)/shard_map/all_to_all | solution.py:33
  127.9 44.3 %all-gather.5.cloned.1.call-start = ((), (), s32[]{:S(2)}) async-start(), calls=%async_computation.5 | async-start | bytes 2924544 | tf_op jit(solution)/shard_map/all_gather | solution.py:30
  193.9 70.3 %all-to-all-start.2 = ((bf16[32,128,336]{1,2,0:T(8,128)(2,1)}), bf16[32,128,336]{1,2,0:T(8,128)(2,1)}, u32[]{:S(2)}, u32[]{:S(2)}) async-start(bf16[32,128,336]{1,2,0:T(8,128)(2,1)} %bitcast.52), calls=%async_computation.2 | async-start | bytes 5505024 | tf_op jit(solution)/shard_map/all_to_all | solution.py:36
  268.9 4.3 %copy-start.2 = (f32[16,32,8,336]{3,2,1,0:T(8,128)S(1)}, f32[16,32,8,336]{3,2,1,0:T(8,128)}, u32[]{:S(2)}) copy-start(f32[16,32,8,336]{3,2,1,0:T(8,128)} %copy.50) | copy-start | bytes 16515076
  291.1 5.2 %copy-start.5 = (s32[132,2]{0,1:T(2,128)S(1)}, s32[132,2]{0,1:T(2,128)}, u32[]{:S(2)}) copy-start(s32[132,2]{0,1:T(2,128)} %param.7) | copy-start | bytes 3172
  291.1 5.2 %copy-start.6 = (f32[132,2]{0,1:T(2,128)S(1)}, f32[132,2]{0,1:T(2,128)}, u32[]{:S(2)}) copy-start(f32[132,2]{0,1:T(2,128)} %param.8) | copy-start | bytes 3172
  291.1 101.5 %all-to-all-start.3 = ((bf16[32,11,4096]{2,1,0:T(8,128)(2,1)}), bf16[32,11,4096]{2,1,0:T(8,128)(2,1)}, u32[]{:S(2)}, u32[]{:S(2)}) async-start(bf16[32,11,4096]{2,1,0:T(8,128)(2,1)} %reshape.75), calls=%async_computation.3 | async-start | bytes 8388608 | tf_op jit(solution)/shard_map/all_to_all | solution.py:66
  296.3 102.2 %copy-start.1 = (bf16[132,4096]{1,0:T(8,128)(2,1)S(1)}, bf16[132,4096]{1,0:T(8,128)(2,1)}, u32[]{:S(2)}) copy-start(bf16[132,4096]{1,0:T(8,128)(2,1)} %param.6) | copy-start | bytes 3244036
Sparse Core Ops, SparseCore 0:
  28.6 41.2 all-gather.2
  130.8 41.2 all-gather.4
where the time goes:
time: 406 us; the launch traced here: 405 us
  waiting for transfers between devices  291 us (72%)
  local copies, waits for them, and re-layouts  51 us (13%)
  starting transfers between devices  28.5 us (7%)
  between operations  13.6 us (3%)
  matrix products  11.9 us (3%)
  other arithmetic  9.81 us (2%)
    all_to_all x1, waiting for transfers between devices, on_device(): lax.all_to_all(block_parts, 'exp', split_axis=0, concat_axis=0, tiled=True)  96.2 us
    all_to_all x1, waiting for transfers between devices, on_device(): lax.all_to_all(copies, 'exp', split_axis=0, concat_axis=0, tiled=True)  47 us
    all_to_all x1, waiting for transfers between devices, on_device(): lax.all_to_all(spread(full_down, blocks, unit_count), 'exp', split_axis=0...  44.6 us
    all_gather x1, waiting for transfers between devices, on_device(): lax.all_gather(dense_down, 'grp', axis=1, tiled=True)  43.5 us
    all_gather x1, waiting for transfers between devices, on_device(): lax.all_gather(dense_up, 'grp', axis=1, tiled=True)  43.4 us
    all_to_all x1, waiting for transfers between devices, on_device(): lax.all_to_all(spread(full_up, blocks, unit_count), 'exp', split_axis=0,...  15.9 us
    all_to_all x1, starting transfers between devices, on_device(): lax.all_to_all(copies, 'exp', split_axis=0, concat_axis=0, tiled=True)  13.4 us
    convert_element_type x2, local copies, waits for them, and re-layouts, on_device(): base_up.astype(jnp.float32) + up_noise.astype(jnp.float32)  11.4 us
  transfers between devices with their start and end apart: 6, of which 6 were waited for; matrix products, arithmetic and copies ran while one was open for 8% of the time, Pallas kernels for 0%

commit v1 on v0

v1 whole, which is shorter than its diff:
```python
import jax
import jax.numpy as jnp
from jax import lax
from jax.sharding import Mesh, PartitionSpec as P

SLOTS = 11


def on_device(tokens, routes, gate_values, dense_up, dense_down, up_noise):
    flight, rows, _ = dense_up.shape
    units = up_noise.shape[1]
    width = tokens.shape[1]
    toks = tokens.shape[0]
    blocks = dense_up.shape[2] // units

    def spread(w):
        return w.reshape(flight, rows, blocks, units).transpose(0, 2, 1, 3).reshape(flight * blocks, rows, units)

    pieces = jnp.concatenate([spread(dense_up), spread(dense_down)], axis=1)
    got = lax.all_to_all(pieces, ("x", "z"), 0, 0, tiled=True)
    owners = got.shape[0]
    span = owners * rows
    mine = lax.axis_index("y") * lax.axis_size("core") + lax.axis_index("core")
    noise = lax.dynamic_slice_in_dim(up_noise, mine * span, span, axis=0)
    up = got[:, :rows].reshape(span, units).astype(jnp.float32) + noise.astype(jnp.float32)
    up = up.astype(jnp.bfloat16)
    down = got[:, rows:].reshape(span, units)
    shard = jnp.stack([up.T, down.T])
    weights = lax.all_gather(shard, ("y", "core"))

    labels = jnp.arange(flight, dtype=jnp.int32)
    chosen = routes[:, :, None] == labels[None, None, :]
    present = jnp.any(chosen, axis=1).astype(jnp.int32)
    before = jnp.cumsum(present, axis=0) - present
    slot_ids = jnp.arange(SLOTS, dtype=jnp.int32)
    placed = present[:, :, None] * (before[:, :, None] == slot_ids[None, None, :]).astype(jnp.int32)
    selector = placed.reshape(toks, flight * SLOTS).astype(jnp.bfloat16)
    outgoing = lax.dot_general(
        selector, tokens, (((0,), (0,)), ((), ())), preferred_element_type=jnp.float32
    ).astype(jnp.bfloat16)
    routed = lax.all_to_all(outgoing.reshape(flight, SLOTS, width), "x", 0, 0, tiled=True)
    routed = routed.reshape(flight * SLOTS, width)
    everyone = lax.all_gather(routed, "z", axis=0, tiled=True)

    preact = jnp.einsum(
        "rgc,guc->ru", everyone.reshape(-1, weights.shape[0], span), weights[:, 0], preferred_element_type=jnp.float32
    )
    hidden = jnp.square(jnp.maximum(preact, 0.0)).astype(jnp.bfloat16)
    part = jnp.einsum("ru,guc->rgc", hidden, weights[:, 1], preferred_element_type=jnp.float32)
    part = part.astype(jnp.bfloat16).reshape(-1, flight * SLOTS, width)
    total = lax.psum_scatter(part, "z", scatter_dimension=0, tiled=False)
    home = lax.all_to_all(total.reshape(flight, SLOTS, width), "x", 0, 0, tiled=True)
    home = home.reshape(flight * SLOTS, width)
    gates = jnp.sum(jnp.where(chosen, gate_values[:, :, None], jnp.float32(0.0)), axis=1)
    mixing = (placed.astype(jnp.float32) * gates[:, :, None]).reshape(toks, flight * SLOTS)
    mixed = jnp.dot(mixing, home.astype(jnp.float32), precision=lax.Precision.HIGHEST, preferred_element_type=jnp.float32)
    return mixed.astype(jnp.bfloat16)


def solution(mesh):
    split = Mesh(mesh.devices.reshape(8, 2, 4, 8), ("y", "core", "x", "z"))
    every = ("y", "core", "x", "z")
    return jax.shard_map(
        on_device,
        mesh=split,
        in_specs=(
            P(every, None),
            P(every, None),
            P(every, None),
            P(None, every, None),
            P(None, every, None),
            P(None, ("x", "z")),
        ),
        out_specs=P(every, None),
        check_vma=False,
    )
```

time: 406 us -> 221 us (0.54)
  the two profiles are of different devices: /device:TPU:32 before, /device:TPU:8 now
where the time goes in v1:
time: 221 us
  waiting for transfers between devices  139 us (63%)
  local copies, waits for them, and re-layouts  22.9 us (10%)
  starting transfers between devices  15.7 us (7%)
  blocking collectives  13.7 us (6%)
  between operations  13.3 us (6%)
  matrix products  13.2 us (6%)
  other arithmetic  3.15 us (1%)
    reduce_scatter x1, waiting for transfers between devices, on_device(): total = lax.psum_scatter(part, 'z', scatter_dimension=0, tiled=False)  49.2 us
    all_gather x1, waiting for transfers between devices, on_device(): weights = lax.all_gather(shard, ('y', 'core'))  42.5 us
    all_gather x1, waiting for transfers between devices, on_device(): everyone = lax.all_gather(routed, 'z', axis=0, tiled=True)  24.5 us
    all_to_all x1, waiting for transfers between devices, on_device(): got = lax.all_to_all(pieces, ('x', 'z'), 0, 0, tiled=True)  14.6 us
    all_to_all x1, blocking collectives, on_device(): lax.all_to_all(outgoing.reshape(flight, SLOTS, width), 'x', 0, 0, tiled=T...  13.7 us
    all_to_all x1, starting transfers between devices, on_device(): got = lax.all_to_all(pieces, ('x', 'z'), 0, 0, tiled=True)  11.3 us
    dot_general x1, matrix products, on_device(): jnp.einsum('ru,guc->rgc', hidden, weights[:, 1], preferred_element_type=j...  8.7 us
    all_to_all x1, waiting for transfers between devices, on_device(): lax.all_to_all(total.reshape(flight, SLOTS, width), 'x', 0, 0, tiled=True)  8.06 us
  transfers between devices with their start and end apart: 5, of which 5 were waited for; matrix products, arithmetic and copies ran while one was open for 4% of the time, Pallas kernels for 0%

profile of v1, /device:TPU:8, one launch (start us, length us, event | category | flops | bytes accessed | tf_op | source)
XLA Modules:
  0.0 220.8 jit_solution(17008936871597060669)
XLA Ops:
  6.5 0.0 copy-start
  6.5 0.0 copy-start.1
  6.5 0.0 all-gather.7.cloned.1.call-start
  6.5 0.9 fusion.34
  7.4 1.2 reduce-window.6
  8.7 0.1 slice.28
  8.7 0.1 copy.35
  8.9 0.1 copy.36
  9.0 0.1 add_bitcast_fusion
  9.1 0.1 eq.45
  9.2 2.4 %convolution_convert_fusion = bf16[44,4096]{1,0:T(8,128)(2,1)} fusion(bf16[132,4096]{1,0:T(8,128)(2,1)} %param.6, s32[132,44]{0,1:T(8,128)S(1)} %mul.30, s32[132,44]{0,1:T(8,128)S(1)} %eq.43, s32[44]{0:T(128)S(1)} %eq.45), kind=kOutput, calls=%fused_computation.2 | convolution fusion | flops 47776784 | bytes 1488432 | tf_op jit(solution)/shard_map/dot_general | solution.py:38
  11.6 1.1 reshape.56
  12.7 13.7 %all_to_all.15 = bf16[4,11,4096]{2,1,0:T(8,128)(2,1)} all-to-all(bf16[4,11,4096]{2,1,0:T(8,128)(2,1)S(1)} %reshape.56), channel_id=1, replica_groups=mesh['y'=8,'core'=2,'x'=4,'z'=8] {'x'}, dimensions={0} | all-to-all | bytes 720896 | tf_op jit(solution)/shard_map/all_to_all | solution.py:41
  26.4 1.9 reshape.68
  28.3 0.0 all-gather.7.cloned.1.call-update
  28.4 0.0 copy-done.1
  28.4 0.3 reshape.59
  28.7 1.2 reshape.61
  29.9 0.8 pad_maximum_fusion
  30.7 11.3 %all-to-all-start.1 = ((bf16[32,16,336]{2,1,0:T(8,128)(2,1)}), bf16[32,16,336]{2,1,0:T(8,128)(2,1)S(1)}, u32[]{:S(2)}, u32[]{:S(2)}) async-start(bf16[32,16,336]{2,1,0:T(8,128)(2,1)} %pad_maximum_fusion), calls=%async_computation.1 | async-start | bytes 786432 | tf_op jit(solution)/shard_map/all_to_all | solution.py:20
  42.0 0.0 all-gather.5.cloned.1.call-start
  42.1 0.0 copy-done
  42.1 0.2 copy.45
  42.3 14.6 %all-to-all-done.1 = bf16[32,16,336]{2,1,0:T(8,128)(2,1)S(1)} async-done(((bf16[32,16,336]{2,1,0:T(8,128)(2,1)}), bf16[32,16,336]{2,1,0:T(8,128)(2,1)S(1)}, u32[]{:S(2)}, u32[]{:S(2)}) %all-to-all-start.1) | async-done | bytes 344096 | tf_op jit(solution)/shard_map/all_to_all | solution.py:20
  56.9 0.1 fusion.24
  57.0 0.1 pad_maximum_fusion.1
  57.1 0.9 copy.40
  58.0 0.0 all-gather.5.cloned.1.call-update
  58.0 0.0 reduce-scatter.2.cloned.1.call-start
  58.1 24.5 %all-gather.7.cloned.1.call-done = bf16[8,44,4096]{2,1,0:T(8,128)(2,1)} async-done(((bf16[1,44,4096]{2,1,0:T(8,128)(2,1)}), bf16[8,44,4096]{2,1,0:T(8,128)(2,1)}) %all-gather.7.cloned.1.call-update) | async-done | bytes 2883600 | tf_op jit(solution)/shard_map/all_gather | solution.py:43
  82.6 4.9 %reshape.58 = bf16[352,16,256]{2,1,0:T(8,128)(2,1)} reshape(bf16[8,44,4096]{2,1,0:T(8,128)(2,1)} %all-gather.7.cloned.1.call-done) | data formatting | bytes 5767168 | tf_op jit(solution)/shard_map/reshape | solution.py:46
  87.5 42.5 %all-gather.5.cloned.1.call-done = bf16[32,336,256]{2,1,0:T(8,128)(2,1)} async-done(((bf16[2,336,256]{2,1,0:T(8,128)(2,1)}), bf16[32,336,256]{2,1,0:T(8,128)(2,1)}) %all-gather.5.cloned.1.call-update) | async-done | bytes 5505040 | tf_op jit(solution)/shard_map/all_gather | solution.py:29
  130.1 8.7 %fusion.4 = bf16[352,16,256]{2,0,1:T(8,128)(2,1)} fusion(bf16[16,2,336,256]{3,2,1,0:T(8,128)(2,1)} %bitcast.87, bf16[352,16,256]{2,1,0:T(8,128)(2,1)} %reshape.58), kind=kOutput, calls=%fused_computation.8 | convolution fusion | flops 1939565056 | bytes 11272192 | tf_op jit(solution)/shard_map/ru,guc->rgc/dot_general | solution.py:49
  138.8 5.1 %copy.44 = bf16[352,16,256]{2,1,0:T(8,128)(2,1)} copy(bf16[352,16,256]{2,0,1:T(8,128)(2,1)} %fusion.4) | data formatting | bytes 5767168 | tf_op jit(solution)/shard_map/convert_element_type | solution.py:50
  143.9 4.8 %reshape.64 = bf16[8,44,4096]{2,1,0:T(8,128)(2,1)} reshape(bf16[352,16,256]{2,1,0:T(8,128)(2,1)} %copy.44) | data formatting | bytes 5767168 | tf_op jit(solution)/shard_map/reshape | solution.py:50
  148.7 0.0 copy-start.2
  148.7 0.0 copy-start.3
  148.7 0.0 reduce-scatter.2.cloned.1.call-update
  148.7 49.2 %reduce-scatter.2.cloned.1.call-done = bf16[1,44,4096]{2,1,0:T(8,128)(2,1)} async-done(((bf16[8,44,4096]{2,1,0:T(8,128)(2,1)}), bf16[1,44,4096]{2,1,0:T(8,128)(2,1)}) %reduce-scatter.2.cloned.1.call-update) | async-done | bytes 360464 | tf_op jit(solution)/shard_map/reduce_scatter | solution.py:51
  197.9 1.9 reshape_reduce_scatter.3
  199.8 4.3 %all-to-all-start.2 = ((bf16[4,11,4096]{2,1,0:T(8,128)(2,1)}), bf16[4,11,4096]{2,1,0:T(8,128)(2,1)S(1)}, u32[]{:S(2)}, u32[]{:S(2)}) async-start(bf16[4,11,4096]{2,1,0:T(8,128)(2,1)} %reshape_reduce_scatter.3), calls=%async_computation.3 | async-start | bytes 1048576 | tf_op jit(solution)/shard_map/all_to_all | solution.py:52
  204.1 0.0 copy-done.2
  204.1 0.0 copy-done.3
  204.1 8.1 %all-to-all-done.2 = bf16[4,11,4096]{2,1,0:T(8,128)(2,1)S(1)} async-done(((bf16[4,11,4096]{2,1,0:T(8,128)(2,1)}), bf16[4,11,4096]{2,1,0:T(8,128)(2,1)S(1)}, u32[]{:S(2)}, u32[]{:S(2)}) %all-to-all-start.2) | async-done | bytes 360480 | tf_op jit(solution)/shard_map/all_to_all | solution.py:52
  212.2 2.1 fusion
  (17 shorter events, 0.2 us)
Async XLA Ops:
  6.5 35.6 %copy-start = (bf16[4096,336]{0,1:T(8,128)(2,1)S(1)}, bf16[4096,336]{0,1:T(8,128)(2,1)}, u32[]{:S(2)}) copy-start(bf16[4096,336]{0,1:T(8,128)(2,1)} %param.11) | copy-start | bytes 8257540
  6.5 21.8 %copy-start.1 = (bf16[4,8,2688]{2,1,0:T(8,128)(2,1)S(1)}, bf16[4,8,2688]{2,1,0:T(8,128)(2,1)}, u32[]{:S(2)}) copy-start(bf16[4,8,2688]{2,1,0:T(8,128)(2,1)} %param.9) | copy-start | bytes 516100
  6.5 76.1 %all-gather.7.cloned.1.call-start = ((), (), s32[]{:S(2)}) async-start(), calls=%async_computation.6 | async-start | bytes 3538944 | tf_op jit(solution)/shard_map/all_gather | solution.py:43
  30.7 26.2 %all-to-all-start.1 = ((bf16[32,16,336]{2,1,0:T(8,128)(2,1)}), bf16[32,16,336]{2,1,0:T(8,128)(2,1)S(1)}, u32[]{:S(2)}, u32[]{:S(2)}) async-start(bf16[32,16,336]{2,1,0:T(8,128)(2,1)} %pad_maximum_fusion), calls=%async_computation.1 | async-start | bytes 786432 | tf_op jit(solution)/shard_map/all_to_all | solution.py:20
  42.0 88.0 %all-gather.5.cloned.1.call-start = ((), (), s32[]{:S(2)}) async-start(), calls=%async_computation.5 | async-start | bytes 5849088 | tf_op jit(solution)/shard_map/all_gather | solution.py:29
  58.0 139.8 %reduce-scatter.2.cloned.1.call-start = ((), (), s32[]{:S(2)}) async-start(), calls=%async_computation.4 | async-start | bytes 3538944 | tf_op jit(solution)/shard_map/reduce_scatter | solution.py:51
  148.7 55.4 %copy-start.2 = (s32[132,2]{0,1:T(2,128)S(1)}, s32[132,2]{0,1:T(2,128)}, u32[]{:S(2)}) copy-start(s32[132,2]{0,1:T(2,128)} %param.7) | copy-start | bytes 3172
  148.7 55.4 %copy-start.3 = (f32[132,2]{0,1:T(2,128)S(1)}, f32[132,2]{0,1:T(2,128)}, u32[]{:S(2)}) copy-start(f32[132,2]{0,1:T(2,128)} %param.8) | copy-start | bytes 3172
  199.8 12.4 %all-to-all-start.2 = ((bf16[4,11,4096]{2,1,0:T(8,128)(2,1)}), bf16[4,11,4096]{2,1,0:T(8,128)(2,1)S(1)}, u32[]{:S(2)}, u32[]{:S(2)}) async-start(bf16[4,11,4096]{2,1,0:T(8,128)(2,1)} %reshape_reduce_scatter.3), calls=%async_computation.3 | async-start | bytes 1048576 | tf_op jit(solution)/shard_map/all_to_all | solution.py:52
Sparse Core Ops, SparseCore 0:
  28.5 54.0 all-gather.6
  84.7 45.2 all-gather.4
  148.8 49.0 reduce-scatter.1

commit v2 on v1

v2 whole, which is shorter than its diff:
```python
import jax, jax.numpy as jnp
from jax import lax
from jax.experimental import pallas as pl
from jax.experimental.pallas import tpu as pltpu
from jax.sharding import Mesh, PartitionSpec as P

F32, BF16 = jnp.float32, jnp.bfloat16
SLOTS, PITCH, FLIGHT = 11, 12, 4
VMEM_LIMIT = 48 * 1024 * 1024


def place(routes):
    toks = routes.shape[1]
    rows = FLIGHT * PITCH
    slot = lax.broadcasted_iota(jnp.int32, (rows, toks), 0)
    expert = sum((slot >= PITCH * e).astype(jnp.int32) for e in range(1, FLIGHT))
    slot = slot - PITCH * expert
    first, second = routes[0:1] == expert, routes[1:2] == expert
    present = jnp.logical_or(first, second)
    earlier = lax.broadcasted_iota(jnp.int32, (toks, toks), 0) < lax.broadcasted_iota(jnp.int32, (toks, toks), 1)
    before = jnp.dot(
        present.astype(F32).astype(BF16), earlier.astype(F32).astype(BF16), preferred_element_type=F32
    )
    taken = jnp.logical_and(present, before == slot.astype(F32))
    return taken, first, second


def dispatch_kernel(routes_ref, tokens_ref, out_ref, shrink_ref, *, dtype):
    taken, _, _ = place(routes_ref[...])
    picked = jnp.dot(taken.astype(F32).astype(BF16), tokens_ref[...], preferred_element_type=F32)
    top = jnp.max(jnp.abs(picked), axis=1, keepdims=True)
    grow, shrink = jnp.ones_like(top), jnp.ones_like(top)
    for bits in (32, 16, 8, 4, 2, 1):
        low = top * (2.0**bits) < 16384.0
        factor = jnp.where(low, 2.0**bits, 1.0)
        top, grow = top * factor, grow * factor
        shrink = shrink * jnp.where(low, 2.0**-bits, 1.0)
    shrink_ref[...] = shrink
    picked = (picked * grow).astype(dtype)
    for e in range(FLIGHT):
        out_ref[e] = picked[e * PITCH : (e + 1) * PITCH]


def dispatch(routes_t, tokens, dtype):
    toks, width = tokens.shape
    return pl.pallas_call(
        lambda *r: dispatch_kernel(*r, dtype=dtype),
        out_shape=(
            jax.ShapeDtypeStruct((FLIGHT, PITCH, width), dtype),
            jax.ShapeDtypeStruct((FLIGHT * PITCH, 1), F32),
        ),
        compiler_params=pltpu.CompilerParams(vmem_limit_bytes=VMEM_LIMIT),
    )(routes_t, tokens)


def prepare_kernel(mine_ref, got_ref, noise_ref, out_ref):
    units, span = out_ref.shape[1:]
    rows = span // got_ref.shape[0]
    got = got_ref[...].reshape(2 * span, units)
    src = lax.broadcasted_iota(jnp.int32, (2 * span, span), 0)
    dst = lax.broadcasted_iota(jnp.int32, (2 * span, span), 1)
    dst = dst + (dst & ~(rows - 1))
    ups = (src == dst).astype(F32).astype(BF16)
    downs = (src == dst + rows).astype(F32).astype(BF16)
    up = lax.dot_general(ups, got, (((0,), (0,)), ((), ())), preferred_element_type=F32)
    up = (up + noise_ref[...].astype(F32)).astype(BF16)
    same = lax.broadcasted_iota(jnp.int32, (span, span), 0) == lax.broadcasted_iota(jnp.int32, (span, span), 1)
    same = same.astype(F32).astype(BF16)
    turn = (((0,), (0,)), ((), ()))
    out_ref[0] = lax.dot_general(up, same, turn, preferred_element_type=F32).astype(BF16)
    out_ref[1] = lax.dot_general(got, downs, turn, preferred_element_type=F32).astype(BF16)


def prepare(mine, got, noise):
    owners, both, units = got.shape
    span = owners * both // 2
    return pl.pallas_call(
        prepare_kernel,
        grid_spec=pltpu.PrefetchScalarGridSpec(
            num_scalar_prefetch=1,
            grid=(1,),
            in_specs=[
                pl.BlockSpec((owners, both, units), lambda i, m: (0, 0, 0)),
                pl.BlockSpec((span, units), lambda i, m: (m[0], 0)),
            ],
            out_specs=pl.BlockSpec((2, units, span), lambda i, m: (0, 0, 0)),
        ),
        out_shape=jax.ShapeDtypeStruct((2, units, span), BF16),
        compiler_params=pltpu.CompilerParams(vmem_limit_bytes=VMEM_LIMIT),
    )(mine, got, noise)


def expert_kernel(half, x_ref, w_ref, out_ref, acc_ref, hid_ref):
    step = pl.program_id(0)
    group, _, units, span = w_ref.shape

    @pl.when(step < half)
    def _():
        total = None
        for g in range(group):
            x = x_ref[:, g * span : (g + 1) * span].astype(F32).astype(BF16)
            term = lax.dot_general(x, w_ref[g, 0], (((1,), (1,)), ((), ())), preferred_element_type=F32)
            total = term if total is None else total + term

        @pl.when(step == 0)
        def _():
            acc_ref[...] = total

        @pl.when(step > 0)
        def _():
            acc_ref[...] += total

        @pl.when(step == half - 1)
        def _():
            hid_ref[...] = jnp.square(jnp.maximum(acc_ref[...], 0.0)).astype(BF16)

    @pl.when(step >= half)
    def _():
        for g in range(group):
            out_ref[:, g * span : (g + 1) * span] = jnp.dot(
                hid_ref[...], w_ref[g, 0], preferred_element_type=F32
            ).astype(BF16)


def expert(x, w, group=4):
    rows, width = x.shape
    members, _, units, span = w.shape
    half = members // group
    cols = group * span
    return pl.pallas_call(
        lambda *r: expert_kernel(half, *r),
        grid=(2 * half,),
        in_specs=[
            pl.BlockSpec((rows, cols), lambda i: (0, jnp.minimum(i, half - 1))),
            pl.BlockSpec((group, 1, units, span), lambda i: (i % half, i // half, 0, 0)),
        ],
        out_specs=pl.BlockSpec((rows, cols), lambda i: (0, jnp.maximum(i - half, 0))),
        out_shape=jax.ShapeDtypeStruct((rows, width), BF16),
        scratch_shapes=[pltpu.VMEM((rows, units), F32), pltpu.VMEM((rows, units), BF16)],
        compiler_params=pltpu.CompilerParams(vmem_limit_bytes=VMEM_LIMIT),
        cost_estimate=pl.CostEstimate(flops=4 * rows * width * units, bytes_accessed=4 * rows * width + 4 * width * units, transcendentals=0),
    )(x, w)


def mix_kernel(routes_ref, gates_ref, shrink_ref, home_ref, out_ref):
    taken, first, second = place(routes_ref[...])
    gates = gates_ref[...]
    weight = jnp.where(first, gates[0:1], 0.0) + jnp.where(second, gates[1:2], 0.0)
    weight = jnp.where(taken, weight, 0.0) * shrink_ref[...]
    high = weight.astype(BF16)
    rest = weight - high.astype(F32)
    middle = rest.astype(BF16)
    low = (rest - middle.astype(F32)).astype(BF16)
    home = jnp.concatenate([home_ref[e].astype(F32) for e in range(FLIGHT)], axis=0)
    home = (home * shrink_ref[...]).astype(BF16)
    turn = (((0,), (0,)), ((), ()))
    total = None
    for part in (low, middle, high):
        term = lax.dot_general(part, home, turn, preferred_element_type=F32)
        total = term if total is None else total + term
    out_ref[...] = total.astype(BF16)


def mix(routes_t, gates_t, shrink, home):
    toks, width = routes_t.shape[1], home.shape[2]
    return pl.pallas_call(
        mix_kernel,
        out_shape=jax.ShapeDtypeStruct((toks, width), BF16),
        compiler_params=pltpu.CompilerParams(vmem_limit_bytes=VMEM_LIMIT),
    )(routes_t, gates_t, shrink, home)


def on_device(tokens, routes, gate_values, dense_up, dense_down, up_noise):
    flight, rows, _ = dense_up.shape
    units = up_noise.shape[1]
    width = tokens.shape[1]
    blocks = dense_up.shape[2] // units

    def spread(w):
        return w.reshape(flight, rows, blocks, units).transpose(0, 2, 1, 3).reshape(flight * blocks, rows, units)

    pieces = jnp.concatenate([spread(dense_up), spread(dense_down)], axis=1)
    got = lax.all_to_all(pieces, ("x", "z"), 0, 0, tiled=True)
    mine = lax.axis_index("y") * lax.axis_size("core") + lax.axis_index("core")
    shard = prepare(mine.reshape(1), got, up_noise)

    outgoing, shrink = dispatch(routes.T, tokens, BF16)
    shard, outgoing = lax.optimization_barrier((shard, outgoing))
    weights = lax.all_gather(shard, ("y", "core"))
    routed = lax.all_to_all(outgoing, "x", 0, 0, tiled=True)
    routed = routed.reshape(flight * PITCH, width).astype(jnp.float16)
    everyone = lax.all_gather(routed, "z", axis=0, tiled=True).astype(BF16)

    part = expert(everyone, weights, 8)
    total = lax.psum_scatter(part, "z", scatter_dimension=0, tiled=True)
    home = lax.all_to_all(total.reshape(flight, PITCH, width), "x", 0, 0, tiled=True)
    return mix(routes.T, gate_values.T, shrink, home)


def solution(mesh):
    split = Mesh(mesh.devices.reshape(8, 2, 4, 8), ("y", "core", "x", "z"))
    every = ("y", "core", "x", "z")
    return jax.shard_map(
        on_device,
        mesh=split,
        in_specs=(
            P(every, None),
            P(every, None),
            P(every, None),
            P(None, every, None),
            P(None, every, None),
            P(None, ("x", "z")),
        ),
        out_specs=P(every, None),
        check_vma=False,
    )
```

time: 221 us -> 165 us (0.75)
  waiting for transfers between devices: 139 us -> 54.9 us
  blocking collectives: 13.7 us -> 58.3 us
  matrix products: 13.2 us -> 0 us
  local copies, waits for them, and re-layouts: 22.9 us -> 10.4 us
  Pallas kernels: 0 us -> 11 us
  starting transfers between devices: 15.7 us -> 13.2 us
    all_gather x1, waiting for transfers between devices: 42.5 us -> 0.01 us  [on_device(): weights = lax.all_gather(shard, ('y', 'core'))]
    all_gather x0 -> x1, blocking collectives: none -> 34.5 us  [on_device(): everyone = lax.all_gather(routed, 'z', axis=0, tiled=True).astype(BF16)]
    all_gather x1 -> x0, waiting for transfers between devices: 24.5 us -> none  [on_device(): everyone = lax.all_gather(routed, 'z', axis=0, tiled=True)]
    dot_general x3 -> x0, matrix products: 13.2 us -> none  [the longest x1 8.7 us: on_device(): jnp.einsum('ru,guc->rgc', hidden, weights[:, 1], preferred_element_type=j...]
    pallas_call x0 -> x4, Pallas kernels: none -> 11 us  [the longest x1 7.49 us: expert(): pl.pallas_call(lambda *r: expert_kernel(half, *r), grid=(2 * half,), in_s...]
    all_to_all x1 -> x2, blocking collectives: 13.7 us -> 23.8 us  [the longest x1 12.3 us: on_device(): lax.all_to_all(total.reshape(flight, PITCH, width), 'x', 0, 0, tiled=True)]
    reshape x3 -> x1, local copies, waits for them, and re-layouts: 10.9 us -> 1.09 us  [on_device(): total.reshape(flight, PITCH, width)]
    all_to_all x1 -> x0, waiting for transfers between devices: 8.06 us -> none  [on_device(): lax.all_to_all(total.reshape(flight, SLOTS, width), 'x', 0, 0, tiled=True)]
  transfers between devices with their start and end apart: 5 -> 3, of which waited for: 5 -> 2; matrix products, arithmetic and copies ran while one was open for 4% -> 4% of each run, Pallas kernels for 0% -> 0%
where the time goes in v2:
time: 165 us
  blocking collectives  58.3 us (35%)
  waiting for transfers between devices  54.9 us (33%)
  between operations  13.5 us (8%)
  starting transfers between devices  13.2 us (8%)
  Pallas kernels  11 us (7%)
  local copies, waits for them, and re-layouts  10.4 us (6%)
  other arithmetic  3.28 us (2%)
    reduce_scatter x1, waiting for transfers between devices, on_device(): total = lax.psum_scatter(part, 'z', scatter_dimension=0, tiled=True)  47.1 us
    all_gather x1, blocking collectives, on_device(): everyone = lax.all_gather(routed, 'z', axis=0, tiled=True).astype(BF16)  34.5 us
    all_to_all x1, starting transfers between devices, on_device(): got = lax.all_to_all(pieces, ('x', 'z'), 0, 0, tiled=True)  13.2 us
    all_to_all x1, blocking collectives, on_device(): lax.all_to_all(total.reshape(flight, PITCH, width), 'x', 0, 0, tiled=True)  12.3 us
    all_to_all x1, blocking collectives, on_device(): routed = lax.all_to_all(outgoing, 'x', 0, 0, tiled=True)  11.5 us
    all_to_all x1, waiting for transfers between devices, on_device(): got = lax.all_to_all(pieces, ('x', 'z'), 0, 0, tiled=True)  7.83 us
    pallas_call x1, Pallas kernels, expert(): pl.pallas_call(lambda *r: expert_kernel(half, *r), grid=(2 * half,), in_s...  7.49 us
    unnamed x15, local copies, waits for them, and re-layouts  6.73 us
  transfers between devices with their start and end apart: 3, of which 2 were waited for; matrix products, arithmetic and copies ran while one was open for 4% of the time, Pallas kernels for 0%

profile of v2, /device:TPU:8, one launch (start us, length us, event | category | flops | bytes accessed | tf_op | source)
XLA Modules:
  0.0 164.7 jit_solution(2646742535261457267)
XLA Ops:
  6.5 1.2 reshape.21
  7.8 1.2 reshape.23
  9.0 0.8 pad_maximum_fusion
  9.8 13.2 %all-to-all-start = ((bf16[32,16,336]{2,1,0:T(8,128)(2,1)}), bf16[32,16,336]{2,1,0:T(8,128)(2,1)S(1)}, u32[]{:S(2)}, u32[]{:S(2)}) async-start(bf16[32,16,336]{2,1,0:T(8,128)(2,1)} %pad_maximum_fusion), calls=%async_computation | async-start | bytes 786432 | tf_op jit(solution)/shard_map/all_to_all | solution.py:183
  23.0 0.0 copy-start.5
  23.0 0.0 all-gather.4.cloned.1.call-start
  23.0 3.3 %copy.15.noise_ref = bf16[4096,336]{1,0:T(8,128)(2,1)S(1)} copy(bf16[4096,336]{0,1:T(8,128)(2,1)} %param.11) | data formatting | bytes 5505024 | tf_op args[5]
  26.4 0.0 copy-done.5
  26.4 0.0 copy-start.1
  26.4 1.2 copy-done.1
  27.6 0.6 shard_map.64
  28.3 0.0 copy-start.2
  28.3 0.8 copy-done.2
  29.1 0.0 copy-start.3
  29.1 0.6 copy-done.3
  29.7 7.8 %all-to-all-done.got_ref = bf16[32,16,336]{2,1,0:T(8,128)(2,1)S(1)} async-done(((bf16[32,16,336]{2,1,0:T(8,128)(2,1)}), bf16[32,16,336]{2,1,0:T(8,128)(2,1)S(1)}, u32[]{:S(2)}, u32[]{:S(2)}) %all-to-all-start) | async-done | bytes 344096 | tf_op jit(solution)/shard_map/all_to_all | solution.py:183
  37.5 0.7 shard_map.65
  38.1 0.0 copy-start
  38.2 0.7 copy-done
  38.9 0.0 all-gather.4.cloned.1.call-update
  38.9 0.0 reduce-scatter.2.cloned.1.call-start
  39.0 11.5 %all_to_all.15 = bf16[4,12,4096]{2,1,0:T(8,128)(2,1)S(1)} all-to-all(bf16[4,12,4096]{2,1,0:T(8,128)(2,1)} %copy-done.2), channel_id=1, replica_groups=mesh['y'=8,'core'=2,'x'=4,'z'=8] {'x'}, dimensions={0} | all-to-all | bytes 786432 | tf_op jit(solution)/shard_map/all_to_all | solution.py:190
  50.5 0.1 convert_element_type.9
  50.6 0.1 convert_element_type.10
  50.7 34.5 %all-gather.5 = f16[384,4096]{1,0:T(8,128)(2,1)S(1)} all-gather(f16[48,4096]{1,0:T(8,128)(2,1)S(1)} %convert_element_type.10), channel_id=1, replica_groups=mesh['y'=8,'core'=2,'x'=4,'z'=8] {'z'}, dimensions={0}, use_global_device_ids=true | all-gather | bytes 3538944 | tf_op jit(solution)/shard_map/all_gather | solution.py:192
  85.2 2.4 %convert_element_type.11.r_0_ = bf16[384,4096]{1,0:T(8,128)(2,1)} convert(f16[384,4096]{1,0:T(8,128)(2,1)S(1)} %all-gather.5) | non-fusion elementwise | flops 1572864 | bytes 6291456 | tf_op jit(solution)/shard_map/convert_element_type | solution.py:192
  87.6 0.0 all-gather.4.cloned.1.call-done
  87.6 7.5 %shard_map.66 = bf16[384,4096]{1,0:T(8,128)(2,1)} custom-call(bf16[384,4096]{1,0:T(8,128)(2,1)} %convert_element_type.11.r_0_, bf16[16,2,336,256]{3,2,1,0:T(8,128)(2,1)} %bitcast.13), custom_call_target="tpu_custom_call" | custom-call | flops 2113929216 | bytes 11796480 | tf_op jit(solution)/shard_map/pallas_call | solution.py:130
  95.1 0.0 copy-start.4
  95.1 0.0 copy-start.6
  95.1 0.0 reduce-scatter.2.cloned.1.call-update
  95.1 47.1 %reduce-scatter.2.cloned.1.call-done = bf16[48,4096]{1,0:T(8,128)(2,1)} async-done(((bf16[384,4096]{1,0:T(8,128)(2,1)}), bf16[48,4096]{1,0:T(8,128)(2,1)}) %reduce-scatter.2.cloned.1.call-update) | async-done | bytes 393232 | tf_op jit(solution)/shard_map/reduce_scatter | solution.py:195
  142.2 1.1 reshape.25
  143.3 12.3 %all_to_all.16.home_ref = bf16[4,12,4096]{2,1,0:T(8,128)(2,1)S(1)} all-to-all(bf16[4,12,4096]{2,1,0:T(8,128)(2,1)S(1)} %reshape.25), channel_id=1, replica_groups=mesh['y'=8,'core'=2,'x'=4,'z'=8] {'x'}, dimensions={0} | all-to-all | bytes 786432 | tf_op jit(solution)/shard_map/all_to_all | solution.py:196
  155.6 0.0 copy-done.4
  155.6 0.0 copy-done.6
  155.6 2.3 %shard_map.67 = bf16[132,4096]{1,0:T(8,128)(2,1)} custom-call(s32[2,132]{1,0:T(2,128)S(1)} %bitcast.11, f32[2,132]{1,0:T(2,128)S(1)} %bitcast.12, f32[48,1]{1,0:T(8,128)S(1)} %copy-done.4, bf16[4,12,4096]{2,1,0:T(8,128)(2,1)S(1)} %all_to_all.16.home_ref), custom_call_target="tpu_custom_call" | custom-call | tf_op jit(solution)/shard_map/pallas_call | solution.py:166
  (2 shorter events, 0.1 us)
Async XLA Ops:
  9.8 27.7 %all-to-all-start = ((bf16[32,16,336]{2,1,0:T(8,128)(2,1)}), bf16[32,16,336]{2,1,0:T(8,128)(2,1)S(1)}, u32[]{:S(2)}, u32[]{:S(2)}) async-start(bf16[32,16,336]{2,1,0:T(8,128)(2,1)} %pad_maximum_fusion), calls=%async_computation | async-start | bytes 786432 | tf_op jit(solution)/shard_map/all_to_all | solution.py:183
  23.0 3.4 %copy-start.5 = (s32[132,2]{0,1:T(2,128)S(1)}, s32[132,2]{0,1:T(2,128)}, u32[]{:S(2)}) copy-start(s32[132,2]{0,1:T(2,128)} %param.7) | copy-start | bytes 3172
  23.0 64.7 %all-gather.4.cloned.1.call-start = ((), (), s32[]{:S(2)}) async-start(), calls=%async_computation.5 | async-start | bytes 5849088 | tf_op jit(solution)/shard_map/all_gather | solution.py:189
  26.4 1.3 copy-start.1
  28.3 0.8 copy-start.2
  29.1 0.6 copy-start.3
  38.1 0.8 copy-start
  38.9 103.3 %reduce-scatter.2.cloned.1.call-start = ((), (), s32[]{:S(2)}) async-start(), calls=%async_computation.4 | async-start | bytes 3538944 | tf_op jit(solution)/shard_map/reduce_scatter | solution.py:195
  95.1 60.5 %copy-start.4 = (f32[48,1]{1,0:T(8,128)S(1)}, f32[48,1]{1,0:T(8,128)}, u32[]{:S(2)}) copy-start(f32[48,1]{1,0:T(8,128)} %copy-done.3) | copy-start | bytes 580
  95.1 60.5 %copy-start.6 = (f32[132,2]{0,1:T(2,128)S(1)}, f32[132,2]{0,1:T(2,128)}, u32[]{:S(2)}) copy-start(f32[132,2]{0,1:T(2,128)} %param.8) | copy-start | bytes 3172
Sparse Core Ops, SparseCore 0:
  39.1 43.0 all-gather.3
  95.3 46.9 reduce-scatter.1

commit v3 on v2

--- a/solution.py
+++ b/solution.py
@@ -53,6 +53,25 @@
     )(routes_t, tokens)
 
 
+def split_kernel(up_ref, down_ref, out_ref):
+    flight = up_ref.shape[0]
+    units = out_ref.shape[2]
+    blocks = out_ref.shape[0] // flight
+    for e in range(flight):
+        both = jnp.concatenate([up_ref[e].astype(F32), down_ref[e].astype(F32)], axis=0).astype(BF16)
+        for b in range(blocks):
+            out_ref[e * blocks + b] = both[:, b * units : (b + 1) * units]
+
+
+def split(up, down, units):
+    flight, rows, total = up.shape
+    return pl.pallas_call(
+        split_kernel,
+        out_shape=jax.ShapeDtypeStruct((flight * total // units, 2 * rows, units), BF16),
+        compiler_params=pltpu.CompilerParams(vmem_limit_bytes=VMEM_LIMIT),
+    )(up, down)
+
+
 def prepare_kernel(mine_ref, got_ref, noise_ref, out_ref):
     units, span = out_ref.shape[1:]
     rows = span // got_ref.shape[0]
@@ -62,16 +81,13 @@
     dst = dst + (dst & ~(rows - 1))
     ups = (src == dst).astype(F32).astype(BF16)
     downs = (src == dst + rows).astype(F32).astype(BF16)
-    up = lax.dot_general(ups, got, (((0,), (0,)), ((), ())), preferred_element_type=F32)
-    up = (up + noise_ref[...].astype(F32)).astype(BF16)
-    same = lax.broadcasted_iota(jnp.int32, (span, span), 0) == lax.broadcasted_iota(jnp.int32, (span, span), 1)
-    same = same.astype(F32).astype(BF16)
     turn = (((0,), (0,)), ((), ()))
-    out_ref[0] = lax.dot_general(up, same, turn, preferred_element_type=F32).astype(BF16)
+    up = lax.dot_general(got, ups, turn, preferred_element_type=F32)
+    out_ref[0] = (up + noise_ref[...].astype(F32)).astype(BF16)
     out_ref[1] = lax.dot_general(got, downs, turn, preferred_element_type=F32).astype(BF16)
 
 
-def prepare(mine, got, noise):
+def prepare(mine, got, noise_t):
     owners, both, units = got.shape
     span = owners * both // 2
     return pl.pallas_call(
@@ -81,13 +97,13 @@
             grid=(1,),
             in_specs=[
                 pl.BlockSpec((owners, both, units), lambda i, m: (0, 0, 0)),
-                pl.BlockSpec((span, units), lambda i, m: (m[0], 0)),
+                pl.BlockSpec((units, span), lambda i, m: (0, m[0])),
             ],
             out_specs=pl.BlockSpec((2, units, span), lambda i, m: (0, 0, 0)),
         ),
         out_shape=jax.ShapeDtypeStruct((2, units, span), BF16),
         compiler_params=pltpu.CompilerParams(vmem_limit_bytes=VMEM_LIMIT),
-    )(mine, got, noise)
+    )(mine, got, noise_t)
 
 
 def expert_kernel(half, x_ref, w_ref, out_ref, acc_ref, hid_ref):
@@ -171,24 +187,26 @@
 
 
 def on_device(tokens, routes, gate_values, dense_up, dense_down, up_noise):
-    flight, rows, _ = dense_up.shape
+    flight = dense_up.shape[0]
     units = up_noise.shape[1]
     width = tokens.shape[1]
-    blocks = dense_up.shape[2] // units
-
-    def spread(w):
-        return w.reshape(flight, rows, blocks, units).transpose(0, 2, 1, 3).reshape(flight * blocks, rows, units)
-
-    pieces = jnp.concatenate([spread(dense_up), spread(dense_down)], axis=1)
-    got = lax.all_to_all(pieces, ("x", "z"), 0, 0, tiled=True)
+
+    got = lax.all_to_all(split(dense_up, dense_down, units), ("x", "z"), 0, 0, tiled=True)
     mine = lax.axis_index("y") * lax.axis_size("core") + lax.axis_index("core")
-    shard = prepare(mine.reshape(1), got, up_noise)
+    shard = prepare(mine.reshape(1), got, up_noise.T)
 
     outgoing, shrink = dispatch(routes.T, tokens, BF16)
-    shard, outgoing = lax.optimization_barrier((shard, outgoing))
+    here = lax.axis_index("x")
+    near = []
+    for s in range(flight):
+        block = lax.dynamic_index_in_dim(outgoing, (here + s) % flight, 0, keepdims=False)
+        near.append(lax.ppermute(block, "x", [(i, (i + s) % flight) for i in range(flight)]) if s else block)
+    shard, near = lax.optimization_barrier((shard, near))
     weights = lax.all_gather(shard, ("y", "core"))
-    routed = lax.all_to_all(outgoing, "x", 0, 0, tiled=True)
-    routed = routed.reshape(flight * PITCH, width).astype(jnp.float16)
+    routed = [
+        lax.select_n(here, *[near[(x - k) % flight] for x in range(flight)]) for k in range(flight)
+    ]
+    routed = jnp.concatenate(routed, axis=0).astype(jnp.float16)
     everyone = lax.all_gather(routed, "z", axis=0, tiled=True).astype(BF16)
 
     part = expert(everyone, weights, 8)

time: 165 us -> 168 us (1.018)
  blocking collectives: 58.3 us -> 47.5 us
  starting transfers between devices: 13.2 us -> 23.7 us
  waiting for transfers between devices: 54.9 us -> 60.9 us
  local copies, waits for them, and re-layouts: 10.4 us -> 5.78 us
    all_to_all x1 -> x0, blocking collectives: 11.5 us -> none  [on_device(): routed = lax.all_to_all(outgoing, 'x', 0, 0, tiled=True)]
    ppermute x0 -> x3, starting transfers between devices: none -> 10.4 us  [on_device(): lax.ppermute(block, 'x', [(i, (i + s) % flight) for i in range(flight)])]
    all_to_all x1, waiting for transfers between devices: 7.83 us -> 0.63 us  [on_device(): lax.all_to_all(split(dense_up, dense_down, units), ('x', 'z'), 0, 0, tile...]
    all_gather x1, waiting for transfers between devices: 0.01 us -> 6.72 us  [on_device(): weights = lax.all_gather(shard, ('y', 'core'))]
    ppermute x0 -> x3, waiting for transfers between devices: none -> 4.33 us  [on_device(): lax.ppermute(block, 'x', [(i, (i + s) % flight) for i in range(flight)])]
    unnamed x15 -> x14, local copies, waits for them, and re-layouts: 6.73 us -> 3.92 us
    reshape x4 -> x0, local copies, waits for them, and re-layouts: 2.43 us -> none  [spread(): w.reshape(flight, rows, blocks, units).transpose(0, 2, 1, 3)]
    reduce_scatter x1, waiting for transfers between devices: 47.1 us -> 49.1 us  [on_device(): total = lax.psum_scatter(part, 'z', scatter_dimension=0, tiled=True)]
  transfers between devices with their start and end apart: 3 -> 6, of which waited for: 2 -> 5; matrix products, arithmetic and copies ran while one was open for 4% -> 3% of each run, Pallas kernels for 0% -> 1%
where the time goes in v3:
time: 168 us
  waiting for transfers between devices  60.9 us (36%)
  blocking collectives  47.5 us (28%)
  starting transfers between devices  23.7 us (14%)
  between operations  13.6 us (8%)
  Pallas kernels  12.6 us (8%)
  local copies, waits for them, and re-layouts  5.78 us (3%)
  other arithmetic  3.51 us (2%)
    reduce_scatter x1, waiting for transfers between devices, on_device(): total = lax.psum_scatter(part, 'z', scatter_dimension=0, tiled=True)  49.1 us
    all_gather x1, blocking collectives, on_device(): everyone = lax.all_gather(routed, 'z', axis=0, tiled=True).astype(BF16)  35.3 us
    all_to_all x1, starting transfers between devices, on_device(): lax.all_to_all(split(dense_up, dense_down, units), ('x', 'z'), 0, 0, tile...  13.2 us
    all_to_all x1, blocking collectives, on_device(): lax.all_to_all(total.reshape(flight, PITCH, width), 'x', 0, 0, tiled=True)  12.2 us
    ppermute x3, starting transfers between devices, on_device(): lax.ppermute(block, 'x', [(i, (i + s) % flight) for i in range(flight)])  10.4 us
    pallas_call x1, Pallas kernels, expert(): pl.pallas_call(lambda *r: expert_kernel(half, *r), grid=(2 * half,), in_s...  7.68 us
    all_gather x1, waiting for transfers between devices, on_device(): weights = lax.all_gather(shard, ('y', 'core'))  6.72 us
    ppermute x3, waiting for transfers between devices, on_device(): lax.ppermute(block, 'x', [(i, (i + s) % flight) for i in range(flight)])  4.33 us
  transfers between devices with their start and end apart: 6, of which 5 were waited for; matrix products, arithmetic and copies ran while one was open for 3% of the time, Pallas kernels for 1%

profile of v3, /device:TPU:8, one launch (start us, length us, event | category | flops | bytes accessed | tf_op | source)
XLA Modules:
  0.0 167.5 jit_solution(13090306989690236913)
XLA Ops:
  6.5 0.0 copy-start
  6.5 0.0 copy-start.2
  6.5 1.1 copy-done.2
  7.6 0.0 copy-start.3
  7.6 0.9 copy-done.3
  8.5 0.9 shard_map.65
  9.5 13.2 %all-to-all-start = ((bf16[32,16,336]{2,1,0:T(8,128)(2,1)}), bf16[32,16,336]{2,1,0:T(8,128)(2,1)S(1)}, u32[]{:S(2)}, u32[]{:S(2)}) async-start(bf16[32,16,336]{2,1,0:T(8,128)(2,1)} %shard_map.65), calls=%async_computation | async-start | bytes 786432 | tf_op jit(solution)/shard_map/all_to_all | solution.py:194
  22.6 0.0 all-gather.4.cloned.1.call-start
  22.7 0.0 copy-start.1
  22.8 1.2 copy-done.1
  24.0 0.0 copy-start.4
  24.0 0.7 copy-done.4
  24.7 0.6 shard_map.64
  25.3 0.8 dynamic-slice_bitcast_fusion
  26.1 4.9 %collective-permute-start.2 = (bf16[12,4096]{1,0:T(8,128)(2,1)}, bf16[12,4096]{1,0:T(8,128)(2,1)S(1)}, u32[]{:S(2)}, u32[]{:S(2)}) collective-permute-start(bf16[12,4096]{1,0:T(8,128)(2,1)} %get-tuple-element.23), channel_id=1, source_target_pairs={{0,24},{8,0},{16,8},{24,16},{1,25},{9,1},{17,9},{25,17},{2,26},{10... | collective-permute-start | bytes 294920 | tf_op jit(solution)/shard_map/ppermute | solution.py:203
  31.0 2.7 %collective-permute-start.1 = (bf16[12,4096]{1,0:T(8,128)(2,1)}, bf16[12,4096]{1,0:T(8,128)(2,1)}, u32[]{:S(2)}, u32[]{:S(2)}) collective-permute-start(bf16[12,4096]{1,0:T(8,128)(2,1)} %get-tuple-element.24), channel_id=1, source_target_pairs={{0,16},{8,24},{16,0},{24,8},{1,17},{9,25},{17,1},{25,9},{2,18},{10... | collective-permute-start | bytes 294920 | tf_op jit(solution)/shard_map/ppermute | solution.py:203
  33.8 2.8 %collective-permute-start = (bf16[12,4096]{1,0:T(8,128)(2,1)}, bf16[12,4096]{1,0:T(8,128)(2,1)}, u32[]{:S(2)}, u32[]{:S(2)}) collective-permute-start(bf16[12,4096]{1,0:T(8,128)(2,1)} %get-tuple-element.25), channel_id=1, source_target_pairs={{0,8},{8,16},{16,24},{24,0},{1,9},{9,17},{17,25},{25,1},{2,10},{10... | collective-permute-start | bytes 294920 | tf_op jit(solution)/shard_map/ppermute | solution.py:203
  36.5 0.6 all-to-all-done.got_ref
  37.2 0.0 copy-done
  37.2 1.1 shard_map.66
  38.3 0.0 collective-permute-done.2
  38.3 2.9 %collective-permute-done.1 = bf16[12,4096]{1,0:T(8,128)(2,1)} collective-permute-done((bf16[12,4096]{1,0:T(8,128)(2,1)}, bf16[12,4096]{1,0:T(8,128)(2,1)}, u32[]{:S(2)}, u32[]{:S(2)}) %collective-permute-start.1) | collective-permute-done | bytes 98336 | tf_op jit(solution)/shard_map/ppermute | solution.py:203
  41.2 1.4 collective-permute-done
  42.6 0.0 all-gather.4.cloned.1.call-update
  42.6 0.0 reduce-scatter.2.cloned.1.call-start
  42.7 1.0 select_select_fusion.3
  43.7 0.2 maximum_convert_fusion
  43.9 35.3 %all-gather.5 = f16[384,4096]{1,0:T(8,128)(2,1)S(1)} all-gather(f16[48,4096]{1,0:T(8,128)(2,1)S(1)} %maximum_convert_fusion), channel_id=1, replica_groups=mesh['y'=8,'core'=2,'x'=4,'z'=8] {'z'}, dimensions={0}, use_global_device_ids=true | all-gather | bytes 3538944 | tf_op jit(solution)/shard_map/all_gather | solution.py:210
  79.2 2.3 %convert_element_type.7.r_0_ = bf16[384,4096]{1,0:T(8,128)(2,1)} convert(f16[384,4096]{1,0:T(8,128)(2,1)S(1)} %all-gather.5) | non-fusion elementwise | flops 1572864 | bytes 6291456 | tf_op jit(solution)/shard_map/convert_element_type | solution.py:210
  81.5 6.7 %all-gather.4.cloned.1.call-done = bf16[32,336,256]{2,1,0:T(8,128)(2,1)} async-done(((bf16[2,336,256]{2,1,0:T(8,128)(2,1)}), bf16[32,336,256]{2,1,0:T(8,128)(2,1)}) %all-gather.4.cloned.1.call-update) | async-done | bytes 5505040 | tf_op jit(solution)/shard_map/all_gather | solution.py:205
  88.3 7.7 %shard_map.67 = bf16[384,4096]{1,0:T(8,128)(2,1)} custom-call(bf16[384,4096]{1,0:T(8,128)(2,1)} %convert_element_type.7.r_0_, bf16[16,2,336,256]{3,2,1,0:T(8,128)(2,1)} %bitcast.17), custom_call_target="tpu_custom_call" | custom-call | flops 2113929216 | bytes 11796480 | tf_op jit(solution)/shard_map/pallas_call | solution.py:146
  96.0 0.0 copy-start.5
  96.0 0.0 copy-start.6
  96.0 0.0 reduce-scatter.2.cloned.1.call-update
  96.0 49.1 %reduce-scatter.2.cloned.1.call-done = bf16[48,4096]{1,0:T(8,128)(2,1)} async-done(((bf16[384,4096]{1,0:T(8,128)(2,1)}), bf16[48,4096]{1,0:T(8,128)(2,1)}) %reduce-scatter.2.cloned.1.call-update) | async-done | bytes 393232 | tf_op jit(solution)/shard_map/reduce_scatter | solution.py:213
  145.1 1.1 reshape.7
  146.2 12.2 %all_to_all.10.home_ref = bf16[4,12,4096]{2,1,0:T(8,128)(2,1)S(1)} all-to-all(bf16[4,12,4096]{2,1,0:T(8,128)(2,1)S(1)} %reshape.7), channel_id=1, replica_groups=mesh['y'=8,'core'=2,'x'=4,'z'=8] {'x'}, dimensions={0} | all-to-all | bytes 786432 | tf_op jit(solution)/shard_map/all_to_all | solution.py:214
  158.4 0.0 copy-done.5
  158.4 0.0 copy-done.6
  158.4 2.3 %shard_map.68 = bf16[132,4096]{1,0:T(8,128)(2,1)} custom-call(s32[2,132]{1,0:T(2,128)S(1)} %bitcast.15, f32[2,132]{1,0:T(2,128)S(1)} %bitcast.16, f32[48,1]{1,0:T(8,128)S(1)} %get-tuple-element.12.shrink_ref, bf16[4,12,4096]{2,1,0:T(8,128)(2,1)S(1)} %all_to_all.10.home_ref), custom_call_target="tpu_custom_call" | custom-call | tf_op jit(solution)/shard_map/pallas_call | solution.py:182
Async XLA Ops:
  6.5 30.6 %copy-start = (bf16[4096,336]{0,1:T(8,128)(2,1)S(1)}, bf16[4096,336]{0,1:T(8,128)(2,1)}, u32[]{:S(2)}) copy-start(bf16[4096,336]{0,1:T(8,128)(2,1)} %param.11) | copy-start | bytes 8257540
  6.5 1.1 copy-start.2
  7.6 0.9 copy-start.3
  9.5 27.7 %all-to-all-start = ((bf16[32,16,336]{2,1,0:T(8,128)(2,1)}), bf16[32,16,336]{2,1,0:T(8,128)(2,1)S(1)}, u32[]{:S(2)}, u32[]{:S(2)}) async-start(bf16[32,16,336]{2,1,0:T(8,128)(2,1)} %shard_map.65), calls=%async_computation | async-start | bytes 786432 | tf_op jit(solution)/shard_map/all_to_all | solution.py:194
  22.6 65.6 %all-gather.4.cloned.1.call-start = ((), (), s32[]{:S(2)}) async-start(), calls=%async_computation.4 | async-start | bytes 5849088 | tf_op jit(solution)/shard_map/all_gather | solution.py:205
  22.7 1.3 copy-start.1
  24.0 0.7 copy-start.4
  26.1 12.2 %collective-permute-start.2 = (bf16[12,4096]{1,0:T(8,128)(2,1)}, bf16[12,4096]{1,0:T(8,128)(2,1)S(1)}, u32[]{:S(2)}, u32[]{:S(2)}) collective-permute-start(bf16[12,4096]{1,0:T(8,128)(2,1)} %get-tuple-element.23), channel_id=1, source_target_pairs={{0,24},{8,0},{16,8},{24,16},{1,25},{9,1},{17,9},{25,17},{2,26},{10... | collective-permute-start | bytes 294920 | tf_op jit(solution)/shard_map/ppermute | solution.py:203
  31.0 10.1 %collective-permute-start.1 = (bf16[12,4096]{1,0:T(8,128)(2,1)}, bf16[12,4096]{1,0:T(8,128)(2,1)}, u32[]{:S(2)}, u32[]{:S(2)}) collective-permute-start(bf16[12,4096]{1,0:T(8,128)(2,1)} %get-tuple-element.24), channel_id=1, source_target_pairs={{0,16},{8,24},{16,0},{24,8},{1,17},{9,25},{17,1},{25,9},{2,18},{10... | collective-permute-start | bytes 294920 | tf_op jit(solution)/shard_map/ppermute | solution.py:203
  33.8 8.9 %collective-permute-start = (bf16[12,4096]{1,0:T(8,128)(2,1)}, bf16[12,4096]{1,0:T(8,128)(2,1)}, u32[]{:S(2)}, u32[]{:S(2)}) collective-permute-start(bf16[12,4096]{1,0:T(8,128)(2,1)} %get-tuple-element.25), channel_id=1, source_target_pairs={{0,8},{8,16},{16,24},{24,0},{1,9},{9,17},{17,25},{25,1},{2,10},{10... | collective-permute-start | bytes 294920 | tf_op jit(solution)/shard_map/ppermute | solution.py:203
  42.6 102.5 %reduce-scatter.2.cloned.1.call-start = ((), (), s32[]{:S(2)}) async-start(), calls=%async_computation.3 | async-start | bytes 3538944 | tf_op jit(solution)/shard_map/reduce_scatter | solution.py:213
  96.0 62.5 %copy-start.5 = (s32[132,2]{0,1:T(2,128)S(1)}, s32[132,2]{0,1:T(2,128)}, u32[]{:S(2)}) copy-start(s32[132,2]{0,1:T(2,128)} %param.7) | copy-start | bytes 3172
  96.0 62.5 %copy-start.6 = (f32[132,2]{0,1:T(2,128)S(1)}, f32[132,2]{0,1:T(2,128)}, u32[]{:S(2)}) copy-start(f32[132,2]{0,1:T(2,128)} %param.8) | copy-start | bytes 3172
Sparse Core Ops, SparseCore 0:
  42.7 45.4 all-gather.3
  96.1 48.9 reduce-scatter.1

commit v4 on v3

v4 whole, which is shorter than its diff:
```python
import jax, jax.numpy as jnp
from jax import lax
from jax.experimental import pallas as pl
from jax.experimental.pallas import tpu as pltpu
from jax.sharding import Mesh, PartitionSpec as P

F32, BF16 = jnp.float32, jnp.bfloat16
PITCH, FLIGHT = 12, 4
HID_LANES, UP_ROWS = 384, 344
VMEM_LIMIT = 48 * 1024 * 1024


def place(routes):
    toks = routes.shape[1]
    rows = FLIGHT * PITCH
    slot = lax.broadcasted_iota(jnp.int32, (rows, toks), 0)
    expert = sum((slot >= PITCH * e).astype(jnp.int32) for e in range(1, FLIGHT))
    slot = slot - PITCH * expert
    first, second = routes[0:1] == expert, routes[1:2] == expert
    present = jnp.logical_or(first, second)
    earlier = lax.broadcasted_iota(jnp.int32, (toks, toks), 0) < lax.broadcasted_iota(jnp.int32, (toks, toks), 1)
    before = jnp.dot(
        present.astype(F32).astype(BF16), earlier.astype(F32).astype(BF16), preferred_element_type=F32
    )
    taken = jnp.logical_and(present, before == slot.astype(F32))
    return taken, first, second


def rescale(top):
    factor, power = jnp.ones_like(top), jnp.zeros_like(top)
    for bits in (32, 16, 8, 4, 2, 1):
        high = top * (2.0**-bits) >= 8192.0
        scale = jnp.where(high, 2.0**-bits, 1.0)
        top, factor = top * scale, factor * scale
        power = power - jnp.where(high, float(bits), 0.0)
    for bits in (32, 16, 8, 4, 2, 1):
        low = top * (2.0**bits) < 16384.0
        scale = jnp.where(low, 2.0**bits, 1.0)
        top, factor = top * scale, factor * scale
        power = power + jnp.where(low, float(bits), 0.0)
    return factor, power


def dispatch_kernel(routes_ref, tokens_ref, out_ref):
    taken, _, _ = place(routes_ref[...])
    picked = jnp.dot(taken.astype(F32).astype(BF16), tokens_ref[...], preferred_element_type=F32).astype(BF16)
    for e in range(FLIGHT):
        out_ref[e] = picked[e * PITCH : (e + 1) * PITCH]


def dispatch(routes_t, tokens):
    return pl.pallas_call(
        dispatch_kernel,
        out_shape=jax.ShapeDtypeStruct((FLIGHT, PITCH, tokens.shape[1]), BF16),
        compiler_params=pltpu.CompilerParams(vmem_limit_bytes=VMEM_LIMIT),
    )(routes_t, tokens)


def split_kernel(up_ref, out_ref):
    flight = up_ref.shape[0]
    units = out_ref.shape[2]
    blocks = out_ref.shape[0] // flight
    for e in range(flight):
        for b in range(blocks):
            out_ref[e * blocks + b] = up_ref[e, :, b * units : (b + 1) * units]


def split(up, units):
    flight, rows, total = up.shape
    return pl.pallas_call(
        split_kernel,
        out_shape=jax.ShapeDtypeStruct((flight * total // units, rows, units), BF16),
        compiler_params=pltpu.CompilerParams(vmem_limit_bytes=VMEM_LIMIT),
    )(up)


def prepare_kernel(mine_ref, got_ref, noise_ref, out_ref):
    owners, rows, units = got_ref.shape
    span = owners * rows
    got = got_ref[...].astype(F32).reshape(span, units).astype(BF16)
    same = lax.broadcasted_iota(jnp.int32, (span, span), 0) == lax.broadcasted_iota(jnp.int32, (span, span), 1)
    same = same.astype(F32).astype(BF16)
    up = lax.dot_general(got, same, (((0,), (0,)), ((), ())), preferred_element_type=F32)
    up = (up + noise_ref[...].astype(F32)).astype(BF16).astype(F32)
    top = jnp.max(jnp.max(jnp.abs(up), axis=1, keepdims=True), axis=0, keepdims=True)
    factor, power = rescale(top)
    power = jnp.broadcast_to(power, (out_ref.shape[0] - units, span))
    out_ref[...] = jnp.concatenate([up * factor, power], axis=0).astype(BF16)


def prepare(mine, got, noise_t):
    owners, rows, units = got.shape
    span = owners * rows
    return pl.pallas_call(
        prepare_kernel,
        grid_spec=pltpu.PrefetchScalarGridSpec(
            num_scalar_prefetch=1,
            grid=(1,),
            in_specs=[
                pl.BlockSpec((owners, rows, units), lambda i, m: (0, 0, 0)),
                pl.BlockSpec((units, span), lambda i, m: (0, m[0])),
            ],
            out_specs=pl.BlockSpec((UP_ROWS, span), lambda i, m: (0, 0)),
        ),
        out_shape=jax.ShapeDtypeStruct((UP_ROWS, span), BF16),
        compiler_params=pltpu.CompilerParams(vmem_limit_bytes=VMEM_LIMIT),
    )(mine, got, noise_t)


def up_kernel(x_ref, w_ref, out_ref, acc_ref):
    step = pl.program_id(0)
    group, units, span = w_ref.shape
    total = None
    for g in range(group):
        x = x_ref[:, g * span : (g + 1) * span]
        term = lax.dot_general(x, w_ref[g], (((1,), (1,)), ((), ())), preferred_element_type=F32)
        total = term if total is None else total + term

    @pl.when(step == 0)
    def _():
        acc_ref[...] = total

    @pl.when(step > 0)
    def _():
        acc_ref[...] += total

    @pl.when(step == pl.num_programs(0) - 1)
    def _():
        hidden = jnp.square(jnp.maximum(acc_ref[...], 0.0))
        factor, power = rescale(jnp.max(hidden, axis=1, keepdims=True))
        hidden = hidden.astype(BF16).astype(F32) * factor
        power = jnp.broadcast_to(power, (power.shape[0], out_ref.shape[1] - units))
        out_ref[...] = jnp.concatenate([hidden, power], axis=1).astype(BF16)


def up_project(x, w, group=8):
    rows, width = x.shape
    members, units, span = w.shape
    return pl.pallas_call(
        up_kernel,
        grid=(members // group,),
        in_specs=[
            pl.BlockSpec((rows, group * span), lambda i: (0, i)),
            pl.BlockSpec((group, units, span), lambda i: (i, 0, 0)),
        ],
        out_specs=pl.BlockSpec((rows, HID_LANES), lambda i: (0, 0)),
        out_shape=jax.ShapeDtypeStruct((rows, HID_LANES), BF16),
        scratch_shapes=[pltpu.VMEM((rows, units), F32)],
        compiler_params=pltpu.CompilerParams(vmem_limit_bytes=VMEM_LIMIT),
        cost_estimate=pl.CostEstimate(flops=2 * rows * width * units, bytes_accessed=2 * width * (rows + units), transcendentals=0),
    )(x, w)


def down_kernel(units, hid_ref, w_ref, out_ref):
    blocks = hid_ref.shape[0]
    hidden = []
    for b in range(blocks):
        h = hid_ref[b].astype(F32)
        hidden.append(h[:, :units] * jnp.exp2(-h[:, units : units + 1]))
    hidden = jnp.concatenate(hidden, axis=1).astype(BF16)
    w = w_ref[...].reshape(-1, w_ref.shape[2])
    out = lax.dot_general(hidden, w, (((1,), (1,)), ((), ())), preferred_element_type=F32).astype(BF16)
    for z in range(blocks):
        for x in range(FLIGHT):
            first = (z * FLIGHT + x) * PITCH
            out_ref[x * blocks + z] = out[first : first + PITCH]


def down_project(hid, w, units):
    blocks, rows, lanes = hid.shape
    members, count, total = w.shape
    cols = members * count
    return pl.pallas_call(
        lambda *r: down_kernel(units, *r),
        out_shape=jax.ShapeDtypeStruct((rows // PITCH, PITCH, cols), BF16),
        compiler_params=pltpu.CompilerParams(vmem_limit_bytes=VMEM_LIMIT),
        cost_estimate=pl.CostEstimate(flops=2 * rows * cols * total, bytes_accessed=2 * cols * total + 2 * blocks * rows * lanes, transcendentals=0),
    )(hid, w)


def mix_kernel(rows, routes_ref, gates_ref, home_ref, out_ref):
    taken, first, second = place(routes_ref[...])
    gates = gates_ref[...]
    weight = jnp.where(first, gates[0:1], 0.0) + jnp.where(second, gates[1:2], 0.0)
    weight = jnp.where(taken, weight, 0.0)
    high = weight.astype(BF16)
    rest = weight - high.astype(F32)
    middle = rest.astype(BF16)
    low = (rest - middle.astype(F32)).astype(BF16)
    owners, _, cols = home_ref.shape
    blocks = owners // FLIGHT
    home = []
    for b in range(blocks):
        home.append(jnp.concatenate([home_ref[e * blocks + b].astype(F32) for e in range(FLIGHT)], axis=0))
    piece = cols // blocks
    src = lax.broadcasted_iota(jnp.int32, (cols, cols), 0)
    dst = lax.broadcasted_iota(jnp.int32, (cols, cols), 1)
    block, rem = src // piece, src % piece
    order = (dst == rem // rows * (blocks * rows) + block * rows + rem % rows).astype(F32).astype(BF16)
    turn = (((0,), (0,)), ((), ()))
    for q in range(blocks):
        chunk = jnp.concatenate([h[:, q * piece : (q + 1) * piece] for h in home], axis=1).astype(BF16)
        chunk = jnp.dot(chunk, order, preferred_element_type=F32).astype(BF16)
        total = None
        for part in (low, middle, high):
            term = lax.dot_general(part, chunk, turn, preferred_element_type=F32)
            total = term if total is None else total + term
        out_ref[:, q * cols : (q + 1) * cols] = total.astype(BF16)


def mix(routes_t, gates_t, home, rows):
    toks = routes_t.shape[1]
    owners, _, cols = home.shape
    return pl.pallas_call(
        lambda *r: mix_kernel(rows, *r),
        out_shape=jax.ShapeDtypeStruct((toks, owners // FLIGHT * cols), BF16),
        compiler_params=pltpu.CompilerParams(vmem_limit_bytes=VMEM_LIMIT),
    )(routes_t, gates_t, home)


def on_device(tokens, routes, gate_values, dense_up, dense_down, up_noise):
    flight, rows, total = dense_up.shape
    units = up_noise.shape[1]
    blocks = total // units
    width = tokens.shape[1]
    here = lax.axis_index("x")
    mine = lax.axis_index("y") * lax.axis_size("core") + lax.axis_index("core")

    outgoing = dispatch(routes.T, tokens)
    routed = lax.all_to_all(outgoing, "x", 0, 0, tiled=True).reshape(flight * PITCH, width)
    everyone = lax.all_gather(routed, "z", axis=0, tiled=True)

    pieces, _ = lax.optimization_barrier((split(dense_up, units), routed))
    got = lax.all_to_all(pieces, ("x", "z"), 0, 0, tiled=True)
    near = []
    for s in range(flight):
        block = lax.dynamic_index_in_dim(dense_down, (here + s) % flight, 0, keepdims=False)
        near.append(lax.ppermute(block, "x", [(i, (i + s) % flight) for i in range(flight)]) if s else block)
    got, near = lax.optimization_barrier((got, near))
    shard = prepare(mine.reshape(1), got, up_noise.T).astype(jnp.float16)
    up = lax.all_gather(shard, ("y", "core"))
    power = up[:, units : units + 1, :1].astype(F32)
    up = (up[:, :units].astype(F32) * jnp.exp2(-power)).astype(BF16)
    down = [lax.select_n(here, *[near[(x - k) % flight] for x in range(flight)]) for k in range(flight)]
    down = lax.all_gather(jnp.concatenate(down, axis=0), ("y", "core"))

    hidden = up_project(everyone, up).astype(jnp.float16)
    hidden = lax.all_gather(hidden, "z", axis=0, tiled=True).astype(BF16)
    out = down_project(hidden.reshape(blocks, -1, HID_LANES), down, units)
    home = lax.all_to_all(out, ("x", "z"), 0, 0, tiled=True)
    return mix(routes.T, gate_values.T, home, rows)


def solution(mesh):
    split = Mesh(mesh.devices.reshape(8, 2, 4, 8), ("y", "core", "x", "z"))
    every = ("y", "core", "x", "z")
    return jax.shard_map(
        on_device,
        mesh=split,
        in_specs=(
            P(every, None),
            P(every, None),
            P(every, None),
            P(None, every, None),
            P(None, every, None),
            P(None, ("x", "z")),
        ),
        out_specs=P(every, None),
        check_vma=False,
    )
```

time: 168 us -> 160 us (0.952)
  the two profiles are of different devices: /device:TPU:8 before, /device:TPU:64 now
where the time goes in v4:
time: 160 us; the launch traced here: 159 us
  blocking collectives  100 us (62%)
  starting transfers between devices  22.1 us (14%)
  between operations  13.6 us (8%)
  Pallas kernels  9.91 us (6%)
  local copies, waits for them, and re-layouts  7.31 us (5%)
  waiting for transfers between devices  3.65 us (2%)
  other arithmetic  2.47 us (2%)
    all_gather x1, blocking collectives, on_device(): hidden = lax.all_gather(hidden, 'z', axis=0, tiled=True).astype(BF16)  31.4 us
    all_to_all x1, blocking collectives, on_device(): home = lax.all_to_all(out, ('x', 'z'), 0, 0, tiled=True)  28.2 us
    all_gather x1, blocking collectives, on_device(): up = lax.all_gather(shard, ('y', 'core'))  27 us
    all_to_all x1, blocking collectives, on_device(): lax.all_to_all(outgoing, 'x', 0, 0, tiled=True)  13.7 us
    ppermute x3, starting transfers between devices, on_device(): lax.ppermute(block, 'x', [(i, (i + s) % flight) for i in range(flight)])  11.3 us
    all_to_all x1, starting transfers between devices, on_device(): got = lax.all_to_all(pieces, ('x', 'z'), 0, 0, tiled=True)  10.7 us
    unnamed x16, local copies, waits for them, and re-layouts  5.6 us
    pallas_call x1, Pallas kernels, mix(): pl.pallas_call(lambda *r: mix_kernel(rows, *r), out_shape=jax.ShapeDtypeS...  3.62 us
  transfers between devices with their start and end apart: 6, of which 2 were waited for; matrix products, arithmetic and copies ran while one was open for 2% of the time, Pallas kernels for 3%

profile of v4, /device:TPU:64, one launch (start us, length us, event | category | flops | bytes accessed | tf_op | source)
XLA Modules:
  0.0 159.4 jit_solution(6793314133596152091)
XLA Ops:
  6.5 0.0 all-gather.7.cloned.1.call-start
  6.5 0.0 copy-start.3
  6.5 1.2 copy-done.3
  7.8 0.0 copy-start.5
  7.8 0.7 copy-done.5
  8.5 0.0 copy-start.4
  8.5 0.0 copy-start.2
  8.5 0.4 shard_map.64
  8.9 13.7 %all_to_all.15 = bf16[4,12,4096]{2,1,0:T(8,128)(2,1)S(1)} all-to-all(bf16[4,12,4096]{2,1,0:T(8,128)(2,1)S(1)} %shard_map.64), channel_id=1, replica_groups=mesh['y'=8,'core'=2,'x'=4,'z'=8] {'x'}, dimensions={0} | all-to-all | bytes 786432 | tf_op jit(solution)/shard_map/all_to_all | solution.py:230
  22.6 0.8 reshape.9
  23.5 0.0 all-gather.7.cloned.1.call-update
  23.5 0.0 copy-done.4
  23.5 0.8 shard_map.65
  24.4 10.7 %all-to-all-start.1 = ((bf16[32,8,336]{2,1,0:T(8,128)(2,1)}), bf16[32,8,336]{2,1,0:T(8,128)(2,1)S(1)}, u32[]{:S(2)}, u32[]{:S(2)}) async-start(bf16[32,8,336]{2,1,0:T(8,128)(2,1)} %shard_map.65), calls=%async_computation.1 | async-start | bytes 393216 | tf_op jit(solution)/shard_map/all_to_all | solution.py:234
  35.1 0.0 all-gather.9.cloned.1.call-start
  35.1 0.9 dynamic-slice_bitcast_fusion
  36.0 3.4 %collective-permute-start = (bf16[8,2688]{1,0:T(8,128)(2,1)S(1)}, bf16[8,2688]{1,0:T(8,128)(2,1)S(1)}, u32[]{:S(2)}, u32[]{:S(2)}) collective-permute-start(bf16[8,2688]{1,0:T(8,128)(2,1)S(1)} %get-tuple-element.22), channel_id=1, source_target_pairs={{0,8},{8,16},{16,24},{24,0},{1,9},{9,17},{17,25},{25,1},{2,10},{10... | collective-permute-start | bytes 129032 | tf_op jit(solution)/shard_map/ppermute | solution.py:238
  39.4 4.6 %collective-permute-start.1 = (bf16[8,2688]{1,0:T(8,128)(2,1)S(1)}, bf16[8,2688]{1,0:T(8,128)(2,1)S(1)}, u32[]{:S(2)}, u32[]{:S(2)}) collective-permute-start(bf16[8,2688]{1,0:T(8,128)(2,1)S(1)} %get-tuple-element.24), channel_id=1, source_target_pairs={{0,16},{8,24},{16,0},{24,8},{1,17},{9,25},{17,1},{25,9},{2,18},{10... | collective-permute-start | bytes 129032 | tf_op jit(solution)/shard_map/ppermute | solution.py:238
  44.0 3.3 %collective-permute-start.2 = (bf16[8,2688]{1,0:T(8,128)(2,1)S(1)}, bf16[8,2688]{1,0:T(8,128)(2,1)S(1)}, u32[]{:S(2)}, u32[]{:S(2)}) collective-permute-start(bf16[8,2688]{1,0:T(8,128)(2,1)S(1)} %get-tuple-element.21), channel_id=1, source_target_pairs={{0,24},{8,0},{16,8},{24,16},{1,25},{9,1},{17,9},{25,17},{2,26},{10... | collective-permute-start | bytes 129032 | tf_op jit(solution)/shard_map/ppermute | solution.py:238
  47.4 0.0 collective-permute-done
  47.4 0.0 collective-permute-done.1
  47.4 2.6 %collective-permute-done.2 = bf16[8,2688]{1,0:T(8,128)(2,1)S(1)} collective-permute-done((bf16[8,2688]{1,0:T(8,128)(2,1)S(1)}, bf16[8,2688]{1,0:T(8,128)(2,1)S(1)}, u32[]{:S(2)}, u32[]{:S(2)}) %collective-permute-start.2) | collective-permute-done | bytes 43040 | tf_op jit(solution)/shard_map/ppermute | solution.py:238
  49.9 0.0 all-to-all-done.1.got_ref
  50.0 0.7 pad_maximum_fusion
  50.7 0.0 all-gather.9.cloned.1.call-update
  50.7 0.0 copy-done.2
  50.7 0.4 shard_map.66
  51.2 27.0 %all-gather.10 = f16[5504,256]{1,0:T(8,128)(2,1)S(1)} all-gather(f16[344,256]{1,0:T(8,128)(2,1)S(1)} %convert_element_type.18), channel_id=2, replica_groups=mesh['y'=8,'core'=2,'x'=4,'z'=8] {'y','core'}, dimensions={0}, use_global_device_ids=true | all-gather | bytes 2994176 | tf_op jit(solution)/shard_map/all_gather | solution.py:241
  78.1 0.2 fusion.3
  78.3 1.0 multiply_convert_fusion.w_ref
  79.4 0.0 all-gather.7.cloned.1.call-done.x_ref
  79.4 0.0 copy-start
  79.4 1.9 %copy-done = bf16[384,4096]{1,0:T(8,128)(2,1)S(1)} copy-done((bf16[384,4096]{1,0:T(8,128)(2,1)S(1)}, bf16[384,4096]{1,0:T(8,128)(2,1)}, u32[]{:S(2)}) %copy-start) | copy-done | bytes 3145752
  81.3 2.9 %shard_map.67 = bf16[384,384]{1,0:T(8,128)(2,1)S(1)} custom-call(bf16[384,4096]{1,0:T(8,128)(2,1)S(1)} %copy-done, bf16[16,336,256]{2,1,0:T(8,128)(2,1)S(1)} %multiply_convert_fusion.w_ref), custom_call_target="tpu_custom_call" | custom-call | flops 1056964608 | bytes 5898240 | tf_op jit(solution)/shard_map/pallas_call | solution.py:139
  84.2 0.1 convert_element_type.22
  84.3 31.4 %all-gather.11 = f16[3072,384]{1,0:T(8,128)(2,1)S(1)} all-gather(f16[384,384]{1,0:T(8,128)(2,1)S(1)} %convert_element_type.22), channel_id=1, replica_groups=mesh['y'=8,'core'=2,'x'=4,'z'=8] {'z'}, dimensions={0}, use_global_device_ids=true | all-gather | bytes 2654208 | tf_op jit(solution)/shard_map/all_gather | solution.py:248
  115.7 0.4 convert_element_type.23
  116.2 1.0 all-gather.9.cloned.1.call-done
  117.2 0.0 copy-start.1
  117.2 1.8 %copy-done.1 = bf16[512,2688]{1,0:T(8,128)(2,1)S(1)} copy-done((bf16[512,2688]{1,0:T(8,128)(2,1)S(1)}, bf16[512,2688]{1,0:T(8,128)(2,1)}, u32[]{:S(2)}) %copy-start.1) | copy-done | bytes 2752536
  119.0 0.0 copy-start.6
  119.0 0.0 copy-start.7
  119.0 1.7 %shard_map.68 = bf16[32,12,512]{2,1,0:T(8,128)(2,1)S(1)} custom-call(bf16[8,384,384]{2,1,0:T(8,128)(2,1)S(1)} %bitcast.15, bf16[16,32,2688]{2,1,0:T(8,128)(2,1)S(1)} %bitcast.16), custom_call_target="tpu_custom_call" | custom-call | flops 1056964608 | bytes 5111808 | tf_op jit(solution)/shard_map/pallas_call | solution.py:173
  120.7 28.2 %all_to_all.16.r_2_ = bf16[32,12,512]{2,1,0:T(8,128)(2,1)S(1)} all-to-all(bf16[32,12,512]{2,1,0:T(8,128)(2,1)S(1)} %shard_map.68), channel_id=1, replica_groups=mesh['y'=8,'core'=2,'x'=4,'z'=8] {'x','z'}, dimensions={0} | all-to-all | bytes 786432 | tf_op jit(solution)/shard_map/all_to_all | solution.py:250
  148.9 0.0 copy-done.6
  148.9 0.0 copy-done.7
  148.9 3.6 %shard_map.69 = bf16[132,4096]{1,0:T(8,128)(2,1)} custom-call(s32[2,132]{1,0:T(2,128)S(1)} %bitcast.19, f32[2,132]{1,0:T(2,128)S(1)} %bitcast.20, bf16[32,12,512]{2,1,0:T(8,128)(2,1)S(1)} %all_to_all.16.r_2_), custom_call_target="tpu_custom_call" | custom-call | tf_op jit(solution)/shard_map/pallas_call | solution.py:214
  (2 shorter events, 0.1 us)
Async XLA Ops:
  6.5 72.8 %all-gather.7.cloned.1.call-start = ((), (), s32[]{:S(2)}) async-start(), calls=%async_computation.3 | async-start | bytes 3538944 | tf_op jit(solution)/shard_map/all_gather | solution.py:231
  6.5 1.2 copy-start.3
  7.8 0.7 copy-start.5
  8.5 15.1 %copy-start.4 = (bf16[4,8,2688]{2,1,0:T(8,128)(2,1)S(1)}, bf16[4,8,2688]{2,1,0:T(8,128)(2,1)}, u32[]{:S(2)}) copy-start(bf16[4,8,2688]{2,1,0:T(8,128)(2,1)} %up_ref.1) | copy-start | bytes 516100
  8.5 42.2 %copy-start.2 = (bf16[4096,336]{0,1:T(8,128)(2,1)S(1)}, bf16[4096,336]{0,1:T(8,128)(2,1)}, u32[]{:S(2)}) copy-start(bf16[4096,336]{0,1:T(8,128)(2,1)} %param.11) | copy-start | bytes 8257540
  24.4 25.6 %all-to-all-start.1 = ((bf16[32,8,336]{2,1,0:T(8,128)(2,1)}), bf16[32,8,336]{2,1,0:T(8,128)(2,1)S(1)}, u32[]{:S(2)}, u32[]{:S(2)}) async-start(bf16[32,8,336]{2,1,0:T(8,128)(2,1)} %shard_map.65), calls=%async_computation.1 | async-start | bytes 393216 | tf_op jit(solution)/shard_map/all_to_all | solution.py:234
  35.1 82.1 %all-gather.9.cloned.1.call-start = ((), (), s32[]{:S(2)}) async-start(), calls=%async_computation.4 | async-start | bytes 2924544 | tf_op jit(solution)/shard_map/all_gather | solution.py:245
  36.0 11.4 %collective-permute-start = (bf16[8,2688]{1,0:T(8,128)(2,1)S(1)}, bf16[8,2688]{1,0:T(8,128)(2,1)S(1)}, u32[]{:S(2)}, u32[]{:S(2)}) collective-permute-start(bf16[8,2688]{1,0:T(8,128)(2,1)S(1)} %get-tuple-element.22), channel_id=1, source_target_pairs={{0,8},{8,16},{16,24},{24,0},{1,9},{9,17},{17,25},{25,1},{2,10},{10... | collective-permute-start | bytes 129032 | tf_op jit(solution)/shard_map/ppermute | solution.py:238
  39.4 8.0 %collective-permute-start.1 = (bf16[8,2688]{1,0:T(8,128)(2,1)S(1)}, bf16[8,2688]{1,0:T(8,128)(2,1)S(1)}, u32[]{:S(2)}, u32[]{:S(2)}) collective-permute-start(bf16[8,2688]{1,0:T(8,128)(2,1)S(1)} %get-tuple-element.24), channel_id=1, source_target_pairs={{0,16},{8,24},{16,0},{24,8},{1,17},{9,25},{17,1},{25,9},{2,18},{10... | collective-permute-start | bytes 129032 | tf_op jit(solution)/shard_map/ppermute | solution.py:238
  44.0 5.9 %collective-permute-start.2 = (bf16[8,2688]{1,0:T(8,128)(2,1)S(1)}, bf16[8,2688]{1,0:T(8,128)(2,1)S(1)}, u32[]{:S(2)}, u32[]{:S(2)}) collective-permute-start(bf16[8,2688]{1,0:T(8,128)(2,1)S(1)} %get-tuple-element.21), channel_id=1, source_target_pairs={{0,24},{8,0},{16,8},{24,16},{1,25},{9,1},{17,9},{25,17},{2,26},{10... | collective-permute-start | bytes 129032 | tf_op jit(solution)/shard_map/ppermute | solution.py:238
  79.4 1.9 %copy-start = (bf16[384,4096]{1,0:T(8,128)(2,1)S(1)}, bf16[384,4096]{1,0:T(8,128)(2,1)}, u32[]{:S(2)}) copy-start(bf16[384,4096]{1,0:T(8,128)(2,1)} %all-gather.7.cloned.1.call-done.x_ref) | copy-start | bytes 9437188
  117.2 1.8 %copy-start.1 = (bf16[512,2688]{1,0:T(8,128)(2,1)S(1)}, bf16[512,2688]{1,0:T(8,128)(2,1)}, u32[]{:S(2)}) copy-start(bf16[512,2688]{1,0:T(8,128)(2,1)} %all-gather.9.cloned.1.call-done) | copy-start | bytes 8257540
  119.0 29.9 %copy-start.6 = (s32[132,2]{0,1:T(2,128)S(1)}, s32[132,2]{0,1:T(2,128)}, u32[]{:S(2)}) copy-start(s32[132,2]{0,1:T(2,128)} %param.7) | copy-start | bytes 3172
  119.0 29.9 %copy-start.7 = (f32[132,2]{0,1:T(2,128)S(1)}, f32[132,2]{0,1:T(2,128)}, u32[]{:S(2)}) copy-start(f32[132,2]{0,1:T(2,128)} %param.8) | copy-start | bytes 3172
Sparse Core Ops, SparseCore 0:
  23.6 49.7 all-gather.6
  75.5 41.6 all-gather.8

commit v5 on v4

--- a/solution.py
+++ b/solution.py
@@ -6,8 +6,9 @@
 
 F32, BF16 = jnp.float32, jnp.bfloat16
 PITCH, FLIGHT = 12, 4
-HID_LANES, UP_ROWS = 384, 344
+LANES, HID_LANES, UP_ROWS, DOWN_AT = 128, 384, 344, 16
 VMEM_LIMIT = 48 * 1024 * 1024
+VMEM_MOST = 62 * 1024 * 1024
 
 
 def place(routes):
@@ -41,19 +42,45 @@
     return factor, power
 
 
-def dispatch_kernel(routes_ref, tokens_ref, out_ref):
+def dispatch_kernel(routes_ref, tokens_ref, down_ref, out_ref):
     taken, _, _ = place(routes_ref[...])
-    picked = jnp.dot(taken.astype(F32).astype(BF16), tokens_ref[...], preferred_element_type=F32).astype(BF16)
+    picked = jnp.dot(taken.astype(F32).astype(BF16), tokens_ref[...], preferred_element_type=F32)
+    width = picked.shape[1]
+    rows, total = down_ref.shape[1:]
+    gap = jnp.zeros((DOWN_AT - PITCH, width), F32)
     for e in range(FLIGHT):
-        out_ref[e] = picked[e * PITCH : (e + 1) * PITCH]
-
-
-def dispatch(routes_t, tokens):
+        mine = picked[e * PITCH : (e + 1) * PITCH]
+        out_ref[e, :DOWN_AT] = jnp.concatenate([mine, gap], axis=0).astype(BF16)
+        out_ref[e, DOWN_AT:, :total] = down_ref[e]
+        out_ref[e, DOWN_AT:, total:] = jnp.zeros((rows, width - total), BF16)
+
+
+def dispatch(routes_t, tokens, down):
     return pl.pallas_call(
         dispatch_kernel,
-        out_shape=jax.ShapeDtypeStruct((FLIGHT, PITCH, tokens.shape[1]), BF16),
-        compiler_params=pltpu.CompilerParams(vmem_limit_bytes=VMEM_LIMIT),
-    )(routes_t, tokens)
+        out_shape=jax.ShapeDtypeStruct((FLIGHT, DOWN_AT + down.shape[1], tokens.shape[1]), BF16),
+        compiler_params=pltpu.CompilerParams(vmem_limit_bytes=VMEM_LIMIT),
+    )(routes_t, tokens, down)
+
+
+def unpack_kernel(near_ref, rows_ref, down_ref):
+    rows, total = near_ref.shape[1] - DOWN_AT, down_ref.shape[1]
+    picked = [near_ref[e, :DOWN_AT].astype(F32)[:PITCH] for e in range(FLIGHT)]
+    rows_ref[...] = jnp.concatenate(picked, axis=0).astype(BF16)
+    down = [near_ref[e, DOWN_AT:, :total].astype(F32) for e in range(FLIGHT)]
+    down_ref[...] = jnp.concatenate(down, axis=0).astype(BF16)
+
+
+def unpack(near, total):
+    flight, height, width = near.shape
+    return pl.pallas_call(
+        unpack_kernel,
+        out_shape=(
+            jax.ShapeDtypeStruct((flight * PITCH, width), BF16),
+            jax.ShapeDtypeStruct((flight * (height - DOWN_AT), total), BF16),
+        ),
+        compiler_params=pltpu.CompilerParams(vmem_limit_bytes=VMEM_LIMIT),
+    )(near)
 
 
 def split_kernel(up_ref, out_ref):
@@ -107,73 +134,90 @@
     )(mine, got, noise_t)
 
 
-def up_kernel(x_ref, w_ref, out_ref, acc_ref):
-    step = pl.program_id(0)
-    group, units, span = w_ref.shape
+def up_kernel(x_hbm, w_hbm, out_ref, x_ref, w_ref, sems):
+    chunks, group, units, span = w_ref.shape
+    cols = group * span
+    copies = []
+    for c in range(chunks):
+        copies.append(
+            (
+                pltpu.make_async_copy(x_hbm.at[:, c * cols : (c + 1) * cols], x_ref.at[c], sems.at[0, c]),
+                pltpu.make_async_copy(w_hbm.at[c * group : (c + 1) * group], w_ref.at[c], sems.at[1, c]),
+            )
+        )
+    for pair in copies:
+        for copy in pair:
+            copy.start()
     total = None
-    for g in range(group):
-        x = x_ref[:, g * span : (g + 1) * span]
-        term = lax.dot_general(x, w_ref[g], (((1,), (1,)), ((), ())), preferred_element_type=F32)
-        total = term if total is None else total + term
-
-    @pl.when(step == 0)
-    def _():
-        acc_ref[...] = total
-
-    @pl.when(step > 0)
-    def _():
-        acc_ref[...] += total
-
-    @pl.when(step == pl.num_programs(0) - 1)
-    def _():
-        hidden = jnp.square(jnp.maximum(acc_ref[...], 0.0))
-        factor, power = rescale(jnp.max(hidden, axis=1, keepdims=True))
-        hidden = hidden.astype(BF16).astype(F32) * factor
-        power = jnp.broadcast_to(power, (power.shape[0], out_ref.shape[1] - units))
-        out_ref[...] = jnp.concatenate([hidden, power], axis=1).astype(BF16)
-
-
-def up_project(x, w, group=8):
+    for c, pair in enumerate(copies):
+        for copy in pair:
+            copy.wait()
+        for g in range(group):
+            x = x_ref[c, :, g * span : (g + 1) * span]
+            term = lax.dot_general(x, w_ref[c, g], (((1,), (1,)), ((), ())), preferred_element_type=F32)
+            total = term if total is None else total + term
+    hidden = jnp.square(jnp.maximum(total, 0.0))
+    factor, power = rescale(jnp.max(hidden, axis=1, keepdims=True))
+    hidden = hidden.astype(BF16).astype(F32) * factor
+    power = jnp.broadcast_to(power, (power.shape[0], out_ref.shape[1] - units))
+    out_ref[...] = jnp.concatenate([hidden, power], axis=1).astype(BF16)
+
+
+def up_project(x, w, chunks=4):
     rows, width = x.shape
     members, units, span = w.shape
     return pl.pallas_call(
         up_kernel,
-        grid=(members // group,),
-        in_specs=[
-            pl.BlockSpec((rows, group * span), lambda i: (0, i)),
-            pl.BlockSpec((group, units, span), lambda i: (i, 0, 0)),
+        in_specs=[pl.BlockSpec(memory_space=pltpu.HBM)] * 2,
+        out_shape=jax.ShapeDtypeStruct((rows, HID_LANES), BF16),
+        scratch_shapes=[
+            pltpu.VMEM((chunks, rows, width // chunks), BF16),
+            pltpu.VMEM((chunks, members // chunks, units, span), BF16),
+            pltpu.SemaphoreType.DMA((2, chunks)),
         ],
-        out_specs=pl.BlockSpec((rows, HID_LANES), lambda i: (0, 0)),
-        out_shape=jax.ShapeDtypeStruct((rows, HID_LANES), BF16),
-        scratch_shapes=[pltpu.VMEM((rows, units), F32)],
-        compiler_params=pltpu.CompilerParams(vmem_limit_bytes=VMEM_LIMIT),
+        compiler_params=pltpu.CompilerParams(vmem_limit_bytes=VMEM_MOST),
         cost_estimate=pl.CostEstimate(flops=2 * rows * width * units, bytes_accessed=2 * width * (rows + units), transcendentals=0),
     )(x, w)
 
 
-def down_kernel(units, hid_ref, w_ref, out_ref):
+def down_kernel(units, hid_hbm, w_hbm, out_ref, hid_ref, w_ref, sems):
     blocks = hid_ref.shape[0]
+    chunks, cols, total = w_ref.shape
+    first = [pltpu.make_async_copy(hid_hbm.at[b], hid_ref.at[b], sems.at[chunks + b]) for b in range(blocks)]
+    copies = [pltpu.make_async_copy(w_hbm.at[c * cols : (c + 1) * cols], w_ref.at[c], sems.at[c]) for c in range(chunks)]
+    for copy in first + copies:
+        copy.start()
     hidden = []
     for b in range(blocks):
+        first[b].wait()
         h = hid_ref[b].astype(F32)
         hidden.append(h[:, :units] * jnp.exp2(-h[:, units : units + 1]))
     hidden = jnp.concatenate(hidden, axis=1).astype(BF16)
-    w = w_ref[...].reshape(-1, w_ref.shape[2])
-    out = lax.dot_general(hidden, w, (((1,), (1,)), ((), ())), preferred_element_type=F32).astype(BF16)
-    for z in range(blocks):
-        for x in range(FLIGHT):
-            first = (z * FLIGHT + x) * PITCH
-            out_ref[x * blocks + z] = out[first : first + PITCH]
-
-
-def down_project(hid, w, units):
+    for c, copy in enumerate(copies):
+        copy.wait()
+        out = lax.dot_general(hidden, w_ref[c], (((1,), (1,)), ((), ())), preferred_element_type=F32)
+        for z in range(blocks):
+            for x in range(FLIGHT):
+                top = (z * FLIGHT + x) * PITCH
+                rows = out[top : top + PITCH]
+                tiles = [rows[:, t : t + LANES] for t in range(0, cols, LANES)]
+                at = c * PITCH * len(tiles)
+                out_ref[x * blocks + z, at : at + PITCH * len(tiles)] = jnp.concatenate(tiles, axis=0).astype(BF16)
+
+
+def down_project(hid, w, units, chunks=1):
     blocks, rows, lanes = hid.shape
-    members, count, total = w.shape
-    cols = members * count
+    cols, total = w.shape
     return pl.pallas_call(
         lambda *r: down_kernel(units, *r),
-        out_shape=jax.ShapeDtypeStruct((rows // PITCH, PITCH, cols), BF16),
-        compiler_params=pltpu.CompilerParams(vmem_limit_bytes=VMEM_LIMIT),
+        in_specs=[pl.BlockSpec(memory_space=pltpu.HBM)] * 2,
+        out_shape=jax.ShapeDtypeStruct((rows // PITCH, PITCH * cols // LANES, LANES), BF16),
+        scratch_shapes=[
+            pltpu.VMEM((blocks, rows, lanes), BF16),
+            pltpu.VMEM((chunks, cols // chunks, total), BF16),
+            pltpu.SemaphoreType.DMA((chunks + blocks,)),
+        ],
+        compiler_params=pltpu.CompilerParams(vmem_limit_bytes=VMEM_MOST),
         cost_estimate=pl.CostEstimate(flops=2 * rows * cols * total, bytes_accessed=2 * cols * total + 2 * blocks * rows * lanes, transcendentals=0),
     )(hid, w)
 
@@ -187,16 +231,22 @@
     rest = weight - high.astype(F32)
     middle = rest.astype(BF16)
     low = (rest - middle.astype(F32)).astype(BF16)
-    owners, _, cols = home_ref.shape
+    owners, height, _ = home_ref.shape
     blocks = owners // FLIGHT
+    tiles = height // PITCH
+    cols = tiles * LANES
+    piece = cols // blocks
     home = []
     for b in range(blocks):
-        home.append(jnp.concatenate([home_ref[e * blocks + b].astype(F32) for e in range(FLIGHT)], axis=0))
-    piece = cols // blocks
+        each = []
+        for e in range(FLIGHT):
+            tall = home_ref[e * blocks + b].astype(F32)
+            each.append(jnp.concatenate([tall[t * PITCH : (t + 1) * PITCH] for t in range(tiles)], axis=1))
+        home.append(jnp.concatenate(each, axis=0))
     src = lax.broadcasted_iota(jnp.int32, (cols, cols), 0)
     dst = lax.broadcasted_iota(jnp.int32, (cols, cols), 1)
-    block, rem = src // piece, src % piece
-    order = (dst == rem // rows * (blocks * rows) + block * rows + rem % rows).astype(F32).astype(BF16)
+    block, group, row = src >> (piece.bit_length() - 1), (src & (piece - 1)) >> (rows.bit_length() - 1), src & (rows - 1)
+    order = (dst == group * (blocks * rows) + block * rows + row).astype(F32).astype(BF16)
     turn = (((0,), (0,)), ((), ()))
     for q in range(blocks):
         chunk = jnp.concatenate([h[:, q * piece : (q + 1) * piece] for h in home], axis=1).astype(BF16)
@@ -210,10 +260,11 @@
 
 def mix(routes_t, gates_t, home, rows):
     toks = routes_t.shape[1]
-    owners, _, cols = home.shape
+    owners, height, _ = home.shape
+    width = owners // FLIGHT * height // PITCH * LANES
     return pl.pallas_call(
         lambda *r: mix_kernel(rows, *r),
-        out_shape=jax.ShapeDtypeStruct((toks, owners // FLIGHT * cols), BF16),
+        out_shape=jax.ShapeDtypeStruct((toks, width), BF16),
         compiler_params=pltpu.CompilerParams(vmem_limit_bytes=VMEM_LIMIT),
     )(routes_t, gates_t, home)
 
@@ -222,27 +273,19 @@
     flight, rows, total = dense_up.shape
     units = up_noise.shape[1]
     blocks = total // units
-    width = tokens.shape[1]
-    here = lax.axis_index("x")
     mine = lax.axis_index("y") * lax.axis_size("core") + lax.axis_index("core")
 
-    outgoing = dispatch(routes.T, tokens)
-    routed = lax.all_to_all(outgoing, "x", 0, 0, tiled=True).reshape(flight * PITCH, width)
+    near = lax.all_to_all(dispatch(routes.T, tokens, dense_down), "x", 0, 0, tiled=True)
+    routed, down = unpack(near, total)
     everyone = lax.all_gather(routed, "z", axis=0, tiled=True)
+    down = lax.all_gather(down, ("y", "core"), axis=0, tiled=True)
 
     pieces, _ = lax.optimization_barrier((split(dense_up, units), routed))
     got = lax.all_to_all(pieces, ("x", "z"), 0, 0, tiled=True)
-    near = []
-    for s in range(flight):
-        block = lax.dynamic_index_in_dim(dense_down, (here + s) % flight, 0, keepdims=False)
-        near.append(lax.ppermute(block, "x", [(i, (i + s) % flight) for i in range(flight)]) if s else block)
-    got, near = lax.optimization_barrier((got, near))
     shard = prepare(mine.reshape(1), got, up_noise.T).astype(jnp.float16)
     up = lax.all_gather(shard, ("y", "core"))
     power = up[:, units : units + 1, :1].astype(F32)
     up = (up[:, :units].astype(F32) * jnp.exp2(-power)).astype(BF16)
-    down = [lax.select_n(here, *[near[(x - k) % flight] for x in range(flight)]) for k in range(flight)]
-    down = lax.all_gather(jnp.concatenate(down, axis=0), ("y", "core"))
 
     hidden = up_project(everyone, up).astype(jnp.float16)
     hidden = lax.all_gather(hidden, "z", axis=0, tiled=True).astype(BF16)

time: 160 us -> 162 us (1.012)
  starting transfers between devices: 22.1 us -> 10.8 us
  waiting for transfers between devices: 3.65 us -> 14.3 us
  Pallas kernels: 9.91 us -> 15.5 us
  local copies, waits for them, and re-layouts: 7.31 us -> 2.86 us
  other arithmetic: 2.47 us -> 5.75 us
    ppermute x3 -> x0, starting transfers between devices: 11.3 us -> none  [on_device(): lax.ppermute(block, 'x', [(i, (i + s) % flight) for i in range(flight)])]
    all_to_all x1, waiting for transfers between devices: 0.01 us -> 10.4 us  [on_device(): got = lax.all_to_all(pieces, ('x', 'z'), 0, 0, tiled=True)]
    pallas_call x3 -> x4, Pallas kernels: 5.08 us -> 10.7 us  [the longest x1 4.71 us: down_project(): pl.pallas_call(lambda *r: down_kernel(units, *r), in_specs=[pl.BlockSpec(...]
    all_to_all x1, blocking collectives: 13.7 us -> 16.5 us  [on_device(): lax.all_to_all(dispatch(routes.T, tokens, dense_down), 'x', 0, 0, tiled=T...]
    unnamed x16 -> x14, local copies, waits for them, and re-layouts: 5.6 us -> 2.86 us
    ppermute x3 -> x0, waiting for transfers between devices: 2.56 us -> none  [on_device(): lax.ppermute(block, 'x', [(i, (i + s) % flight) for i in range(flight)])]
    all_to_all x1, blocking collectives: 28.2 us -> 25.9 us  [on_device(): home = lax.all_to_all(out, ('x', 'z'), 0, 0, tiled=True)]
    all_gather x1, waiting for transfers between devices: 1.03 us -> 3.19 us  [on_device(): down = lax.all_gather(down, ('y', 'core'), axis=0, tiled=True)]
  transfers between devices with their start and end apart: 6 -> 3, of which waited for: 2 -> 2; matrix products, arithmetic and copies ran while one was open for 2% -> 4% of each run, Pallas kernels for 3% -> 4%
where the time goes in v5:
time: 162 us
  blocking collectives  99.4 us (61%)
  Pallas kernels  15.5 us (10%)
  waiting for transfers between devices  14.3 us (9%)
  between operations  13.5 us (8%)
  starting transfers between devices  10.8 us (7%)
  other arithmetic  5.75 us (4%)
  local copies, waits for them, and re-layouts  2.86 us (2%)
    all_gather x1, blocking collectives, on_device(): hidden = lax.all_gather(hidden, 'z', axis=0, tiled=True).astype(BF16)  30 us
    all_gather x1, blocking collectives, on_device(): up = lax.all_gather(shard, ('y', 'core'))  27 us
    all_to_all x1, blocking collectives, on_device(): home = lax.all_to_all(out, ('x', 'z'), 0, 0, tiled=True)  25.9 us
    all_to_all x1, blocking collectives, on_device(): lax.all_to_all(dispatch(routes.T, tokens, dense_down), 'x', 0, 0, tiled=T...  16.5 us
    all_to_all x1, starting transfers between devices, on_device(): got = lax.all_to_all(pieces, ('x', 'z'), 0, 0, tiled=True)  10.7 us
    all_to_all x1, waiting for transfers between devices, on_device(): got = lax.all_to_all(pieces, ('x', 'z'), 0, 0, tiled=True)  10.4 us
    pallas_call x1, Pallas kernels, down_project(): pl.pallas_call(lambda *r: down_kernel(units, *r), in_specs=[pl.BlockSpec(...  4.71 us
    pallas_call x1, Pallas kernels, up_project(): pl.pallas_call(up_kernel, in_specs=[pl.BlockSpec(memory_space=pltpu.HBM)]...  4.7 us
  transfers between devices with their start and end apart: 3, of which 2 were waited for; matrix products, arithmetic and copies ran while one was open for 4% of the time, Pallas kernels for 4%

profile of v5, /device:TPU:64, one launch (start us, length us, event | category | flops | bytes accessed | tf_op | source)
XLA Modules:
  0.0 162.0 jit_solution(709071842053863641)
XLA Ops:
  6.5 0.0 all-gather.6.cloned.1.call-start
  6.5 0.0 copy-start.1
  6.5 1.2 copy-done.1
  7.8 0.0 copy-start.3
  7.8 0.9 copy-done.3
  8.7 0.0 copy-start.4
  8.7 0.7 copy-done.4
  9.4 0.0 copy-start.2
  9.4 0.0 copy-start
  9.4 0.4 shard_map.64
  9.8 16.5 %all_to_all.15.near_ref = bf16[4,24,4096]{2,1,0:T(8,128)(2,1)S(1)} all-to-all(bf16[4,24,4096]{2,1,0:T(8,128)(2,1)S(1)} %shard_map.64), channel_id=1, replica_groups=mesh['y'=8,'core'=2,'x'=4,'z'=8] {'x'}, dimensions={0} | all-to-all | bytes 1572864 | tf_op jit(solution)/shard_map/all_to_all | solution.py:278
  26.3 0.8 shard_map.65
  27.2 0.0 all-gather.6.cloned.1.call-update
  27.2 0.0 all-gather.8.cloned.1.call-start
  27.3 0.7 all-gather.8.cloned.1.call-update
  28.0 0.0 copy-done.2
  28.0 0.8 shard_map.66
  28.8 10.7 %all-to-all-start.1 = ((bf16[32,8,336]{2,1,0:T(8,128)(2,1)}), bf16[32,8,336]{2,1,0:T(8,128)(2,1)S(1)}, u32[]{:S(2)}, u32[]{:S(2)}) async-start(bf16[32,8,336]{2,1,0:T(8,128)(2,1)} %shard_map.66), calls=%async_computation.1 | async-start | bytes 393216 | tf_op jit(solution)/shard_map/all_to_all | solution.py:284
  39.5 10.4 %all-to-all-done.1.got_ref = bf16[32,8,336]{2,1,0:T(8,128)(2,1)S(1)} async-done(((bf16[32,8,336]{2,1,0:T(8,128)(2,1)}), bf16[32,8,336]{2,1,0:T(8,128)(2,1)S(1)}, u32[]{:S(2)}, u32[]{:S(2)}) %all-to-all-start.1) | async-done | bytes 172064 | tf_op jit(solution)/shard_map/all_to_all | solution.py:284
  49.9 0.0 copy-done
  49.9 0.4 shard_map.67
  50.3 27.0 %all-gather.9 = f16[5504,256]{1,0:T(8,128)(2,1)S(1)} all-gather(f16[344,256]{1,0:T(8,128)(2,1)S(1)} %convert_element_type.18), channel_id=2, replica_groups=mesh['y'=8,'core'=2,'x'=4,'z'=8] {'y','core'}, dimensions={0}, use_global_device_ids=true | all-gather | bytes 2994176 | tf_op jit(solution)/shard_map/all_gather | solution.py:286
  77.4 0.2 fusion.3
  77.6 2.6 %multiply_convert_fusion.w_hbm = bf16[16,336,256]{2,1,0:T(8,128)(2,1)} fusion(f16[16,344,256]{2,1,0:T(8,128)(2,1)S(1)} %bitcast.11, f32[16]{0:T(128)S(1)} %fusion.3), kind=kLoop, calls=%fused_computation | loop fusion | flops 4128768 | bytes 5505088 | tf_op jit(solution)/shard_map/convert_element_type | solution.py:288
  80.2 0.0 all-gather.6.cloned.1.call-done.x_hbm
  80.2 4.7 %shard_map.68 = bf16[384,384]{1,0:T(8,128)(2,1)} custom-call(bf16[384,4096]{1,0:T(8,128)(2,1)} %all-gather.6.cloned.1.call-done.x_hbm, bf16[16,336,256]{2,1,0:T(8,128)(2,1)} %multiply_convert_fusion.w_hbm), custom_call_target="tpu_custom_call" | custom-call | flops 1056964608 | bytes 5898240 | tf_op jit(solution)/shard_map/pallas_call | solution.py:169
  84.9 1.0 convert_element_type.22
  85.9 30.0 %all-gather.10 = f16[3072,384]{1,0:T(8,128)(2,1)S(1)} all-gather(f16[384,384]{1,0:T(8,128)(2,1)S(1)} %convert_element_type.22), channel_id=1, replica_groups=mesh['y'=8,'core'=2,'x'=4,'z'=8] {'z'}, dimensions={0}, use_global_device_ids=true | all-gather | bytes 2654208 | tf_op jit(solution)/shard_map/all_gather | solution.py:291
  115.9 1.9 %convert_element_type.23 = bf16[3072,384]{1,0:T(8,128)(2,1)} convert(f16[3072,384]{1,0:T(8,128)(2,1)S(1)} %all-gather.10) | non-fusion elementwise | flops 1179648 | bytes 4718592 | tf_op jit(solution)/shard_map/convert_element_type | solution.py:291
  117.8 3.2 %all-gather.8.cloned.1.call-done.r_1_ = bf16[512,2688]{1,0:T(8,128)(2,1)} async-done(((bf16[32,2688]{1,0:T(8,128)(2,1)}), bf16[512,2688]{1,0:T(8,128)(2,1)}) %all-gather.8.cloned.1.call-update) | async-done | bytes 2752528 | tf_op jit(solution)/shard_map/all_gather | solution.py:281
  120.9 0.0 copy-start.5
  120.9 0.0 copy-start.6
  121.0 4.7 %shard_map.69 = bf16[32,48,128]{2,1,0:T(8,128)(2,1)} custom-call(bf16[8,384,384]{2,1,0:T(8,128)(2,1)} %bitcast.12, bf16[512,2688]{1,0:T(8,128)(2,1)} %all-gather.8.cloned.1.call-done.r_1_), custom_call_target="tpu_custom_call" | custom-call | flops 1056964608 | bytes 5111808 | tf_op jit(solution)/shard_map/pallas_call | solution.py:211
  125.7 25.9 %all_to_all.16.r_2_ = bf16[32,48,128]{2,1,0:T(8,128)(2,1)S(1)} all-to-all(bf16[32,48,128]{2,1,0:T(8,128)(2,1)} %shard_map.69), channel_id=1, replica_groups=mesh['y'=8,'core'=2,'x'=4,'z'=8] {'x','z'}, dimensions={0} | all-to-all | bytes 786432 | tf_op jit(solution)/shard_map/all_to_all | solution.py:293
  151.6 0.0 copy-done.5
  151.6 0.0 copy-done.6
  151.6 3.6 %shard_map.70 = bf16[132,4096]{1,0:T(8,128)(2,1)} custom-call(s32[2,132]{1,0:T(2,128)S(1)} %bitcast.8, f32[2,132]{1,0:T(2,128)S(1)} %bitcast.9, bf16[32,48,128]{2,1,0:T(8,128)(2,1)S(1)} %all_to_all.16.r_2_), custom_call_target="tpu_custom_call" | custom-call | tf_op jit(solution)/shard_map/pallas_call | solution.py:265
  (1 shorter events, 0.0 us)
Async XLA Ops:
  6.5 73.6 %all-gather.6.cloned.1.call-start = ((), (), s32[]{:S(2)}) async-start(), calls=%async_computation.3 | async-start | bytes 3538944 | tf_op jit(solution)/shard_map/all_gather | solution.py:280
  6.5 1.2 copy-start.1
  7.8 0.9 copy-start.3
  8.7 0.7 copy-start.4
  9.4 18.6 %copy-start.2 = (bf16[4,8,2688]{2,1,0:T(8,128)(2,1)S(1)}, bf16[4,8,2688]{2,1,0:T(8,128)(2,1)}, u32[]{:S(2)}) copy-start(bf16[4,8,2688]{2,1,0:T(8,128)(2,1)} %up_ref.1) | copy-start | bytes 516100
  9.4 40.5 %copy-start = (bf16[4096,336]{0,1:T(8,128)(2,1)S(1)}, bf16[4096,336]{0,1:T(8,128)(2,1)}, u32[]{:S(2)}) copy-start(bf16[4096,336]{0,1:T(8,128)(2,1)} %param.11) | copy-start | bytes 8257540
  27.2 93.7 %all-gather.8.cloned.1.call-start = ((), (), s32[]{:S(2)}) async-start(), calls=%async_computation.4 | async-start | bytes 2924544 | tf_op jit(solution)/shard_map/all_gather | solution.py:281
  28.8 21.1 %all-to-all-start.1 = ((bf16[32,8,336]{2,1,0:T(8,128)(2,1)}), bf16[32,8,336]{2,1,0:T(8,128)(2,1)S(1)}, u32[]{:S(2)}, u32[]{:S(2)}) async-start(bf16[32,8,336]{2,1,0:T(8,128)(2,1)} %shard_map.66), calls=%async_computation.1 | async-start | bytes 393216 | tf_op jit(solution)/shard_map/all_to_all | solution.py:284
  120.9 30.6 %copy-start.5 = (s32[132,2]{0,1:T(2,128)S(1)}, s32[132,2]{0,1:T(2,128)}, u32[]{:S(2)}) copy-start(s32[132,2]{0,1:T(2,128)} %param.7) | copy-start | bytes 3172
  120.9 30.6 %copy-start.6 = (f32[132,2]{0,1:T(2,128)S(1)}, f32[132,2]{0,1:T(2,128)}, u32[]{:S(2)}) copy-start(f32[132,2]{0,1:T(2,128)} %param.8) | copy-start | bytes 3172
Sparse Core Ops, SparseCore 0:
  27.3 49.7 all-gather.5
  79.3 41.6 all-gather.7

commit v6 on v5

--- a/solution.py
+++ b/solution.py
@@ -6,7 +6,7 @@
 
 F32, BF16 = jnp.float32, jnp.bfloat16
 PITCH, FLIGHT = 12, 4
-LANES, HID_LANES, UP_ROWS, DOWN_AT = 128, 384, 344, 16
+LANES, HID_LANES, UP_ROWS, SENT_ROWS = 128, 384, 344, 16
 VMEM_LIMIT = 48 * 1024 * 1024
 VMEM_MOST = 62 * 1024 * 1024
 
@@ -42,72 +42,84 @@
     return factor, power
 
 
-def dispatch_kernel(routes_ref, tokens_ref, down_ref, out_ref):
+def dispatch_kernel(routes_ref, tokens_ref, out_ref):
     taken, _, _ = place(routes_ref[...])
     picked = jnp.dot(taken.astype(F32).astype(BF16), tokens_ref[...], preferred_element_type=F32)
-    width = picked.shape[1]
-    rows, total = down_ref.shape[1:]
-    gap = jnp.zeros((DOWN_AT - PITCH, width), F32)
+    width = out_ref.shape[2]
+    rest = picked.shape[1] - width
+    fold = width // rest
     for e in range(FLIGHT):
         mine = picked[e * PITCH : (e + 1) * PITCH]
-        out_ref[e, :DOWN_AT] = jnp.concatenate([mine, gap], axis=0).astype(BF16)
-        out_ref[e, DOWN_AT:, :total] = down_ref[e]
-        out_ref[e, DOWN_AT:, total:] = jnp.zeros((rows, width - total), BF16)
-
-
-def dispatch(routes_t, tokens, down):
+        rows = [mine[:, :width]]
+        for i in range(0, PITCH, fold):
+            rows.append(jnp.concatenate([mine[i + k : i + k + 1, width:] for k in range(fold)], axis=1))
+        out_ref[e] = jnp.concatenate(rows, axis=0).astype(BF16)
+
+
+def dispatch(routes_t, tokens):
     return pl.pallas_call(
         dispatch_kernel,
-        out_shape=jax.ShapeDtypeStruct((FLIGHT, DOWN_AT + down.shape[1], tokens.shape[1]), BF16),
-        compiler_params=pltpu.CompilerParams(vmem_limit_bytes=VMEM_LIMIT),
-    )(routes_t, tokens, down)
-
-
-def unpack_kernel(near_ref, rows_ref, down_ref):
-    rows, total = near_ref.shape[1] - DOWN_AT, down_ref.shape[1]
-    picked = [near_ref[e, :DOWN_AT].astype(F32)[:PITCH] for e in range(FLIGHT)]
-    rows_ref[...] = jnp.concatenate(picked, axis=0).astype(BF16)
-    down = [near_ref[e, DOWN_AT:, :total].astype(F32) for e in range(FLIGHT)]
-    down_ref[...] = jnp.concatenate(down, axis=0).astype(BF16)
-
-
-def unpack(near, total):
-    flight, height, width = near.shape
+        out_shape=jax.ShapeDtypeStruct((FLIGHT, SENT_ROWS, tokens.shape[1] * PITCH // SENT_ROWS), BF16),
+        compiler_params=pltpu.CompilerParams(vmem_limit_bytes=VMEM_LIMIT),
+    )(routes_t, tokens)
+
+
+def unpack_kernel(near_ref, rows_ref):
+    short = near_ref.shape[2]
+    rest = rows_ref.shape[1] - short
+    fold = short // rest
+    rows = []
+    for e in range(FLIGHT):
+        sent = near_ref[e].astype(F32)
+        tails = []
+        for i in range(PITCH):
+            at = PITCH + i // fold
+            tails.append(sent[at : at + 1, i % fold * rest : (i % fold + 1) * rest])
+        rows.append(jnp.concatenate([sent[:PITCH], jnp.concatenate(tails, axis=0)], axis=1))
+    rows_ref[...] = jnp.concatenate(rows, axis=0).astype(BF16)
+
+
+def unpack(near):
+    flight, height, short = near.shape
     return pl.pallas_call(
         unpack_kernel,
-        out_shape=(
-            jax.ShapeDtypeStruct((flight * PITCH, width), BF16),
-            jax.ShapeDtypeStruct((flight * (height - DOWN_AT), total), BF16),
-        ),
+        out_shape=jax.ShapeDtypeStruct((flight * PITCH, short * height // PITCH), BF16),
         compiler_params=pltpu.CompilerParams(vmem_limit_bytes=VMEM_LIMIT),
     )(near)
 
 
-def split_kernel(up_ref, out_ref):
+def split_kernel(up_ref, down_ref, out_ref):
     flight = up_ref.shape[0]
     units = out_ref.shape[2]
     blocks = out_ref.shape[0] // flight
+    cuts = [slice(b * units, (b + 1) * units) for b in range(blocks)]
     for e in range(flight):
+        down = down_ref[e].astype(F32)
         for b in range(blocks):
-            out_ref[e * blocks + b] = up_ref[e, :, b * units : (b + 1) * units]
-
-
-def split(up, units):
+            row = jnp.concatenate([down[b : b + 1, cut] for cut in cuts], axis=0)
+            out_ref[e * blocks + b] = jnp.concatenate([up_ref[e, :, cuts[b]].astype(F32), row], axis=0).astype(BF16)
+
+
+def split(up, down, units):
     flight, rows, total = up.shape
     return pl.pallas_call(
         split_kernel,
-        out_shape=jax.ShapeDtypeStruct((flight * total // units, rows, units), BF16),
-        compiler_params=pltpu.CompilerParams(vmem_limit_bytes=VMEM_LIMIT),
-    )(up)
-
-
-def prepare_kernel(mine_ref, got_ref, noise_ref, out_ref):
-    owners, rows, units = got_ref.shape
+        out_shape=jax.ShapeDtypeStruct((flight * total // units, 2 * rows, units), BF16),
+        compiler_params=pltpu.CompilerParams(vmem_limit_bytes=VMEM_LIMIT),
+    )(up, down)
+
+
+def prepare_kernel(mine_ref, got_ref, noise_ref, out_ref, down_ref):
+    owners, both, units = got_ref.shape
+    rows = both // 2
     span = owners * rows
-    got = got_ref[...].astype(F32).reshape(span, units).astype(BF16)
+    got = got_ref[...].astype(F32)
+    for b in range(rows):
+        down_ref[:, b * units : (b + 1) * units] = got[:, rows + b, :].astype(BF16)
+    flat = got[:, :rows].reshape(span, units).astype(BF16)
     same = lax.broadcasted_iota(jnp.int32, (span, span), 0) == lax.broadcasted_iota(jnp.int32, (span, span), 1)
     same = same.astype(F32).astype(BF16)
-    up = lax.dot_general(got, same, (((0,), (0,)), ((), ())), preferred_element_type=F32)
+    up = lax.dot_general(flat, same, (((0,), (0,)), ((), ())), preferred_element_type=F32)
     up = (up + noise_ref[...].astype(F32)).astype(BF16).astype(F32)
     top = jnp.max(jnp.max(jnp.abs(up), axis=1, keepdims=True), axis=0, keepdims=True)
     factor, power = rescale(top)
@@ -116,7 +128,8 @@
 
 
 def prepare(mine, got, noise_t):
-    owners, rows, units = got.shape
+    owners, both, units = got.shape
+    rows = both // 2
     span = owners * rows
     return pl.pallas_call(
         prepare_kernel,
@@ -124,12 +137,15 @@
             num_scalar_prefetch=1,
             grid=(1,),
             in_specs=[
-                pl.BlockSpec((owners, rows, units), lambda i, m: (0, 0, 0)),
+                pl.BlockSpec((owners, both, units), lambda i, m: (0, 0, 0)),
                 pl.BlockSpec((units, span), lambda i, m: (0, m[0])),
             ],
-            out_specs=pl.BlockSpec((UP_ROWS, span), lambda i, m: (0, 0)),
+            out_specs=(
+                pl.BlockSpec((UP_ROWS, span), lambda i, m: (0, 0)),
+                pl.BlockSpec((owners, rows * units), lambda i, m: (0, 0)),
+            ),
         ),
-        out_shape=jax.ShapeDtypeStruct((UP_ROWS, span), BF16),
+        out_shape=(jax.ShapeDtypeStruct((UP_ROWS, span), BF16), jax.ShapeDtypeStruct((owners, rows * units), BF16)),
         compiler_params=pltpu.CompilerParams(vmem_limit_bytes=VMEM_LIMIT),
     )(mine, got, noise_t)
 
@@ -193,16 +209,16 @@
         h = hid_ref[b].astype(F32)
         hidden.append(h[:, :units] * jnp.exp2(-h[:, units : units + 1]))
     hidden = jnp.concatenate(hidden, axis=1).astype(BF16)
+    out = []
     for c, copy in enumerate(copies):
         copy.wait()
-        out = lax.dot_general(hidden, w_ref[c], (((1,), (1,)), ((), ())), preferred_element_type=F32)
-        for z in range(blocks):
-            for x in range(FLIGHT):
-                top = (z * FLIGHT + x) * PITCH
-                rows = out[top : top + PITCH]
-                tiles = [rows[:, t : t + LANES] for t in range(0, cols, LANES)]
-                at = c * PITCH * len(tiles)
-                out_ref[x * blocks + z, at : at + PITCH * len(tiles)] = jnp.concatenate(tiles, axis=0).astype(BF16)
+        out.append(lax.dot_general(hidden, w_ref[c], (((1,), (1,)), ((), ())), preferred_element_type=F32))
+    out = jnp.concatenate(out, axis=1)
+    for z in range(blocks):
+        for x in range(FLIGHT):
+            top = (z * FLIGHT + x) * PITCH
+            tiles = [out[top : top + PITCH, t : t + LANES] for t in range(0, out.shape[1], LANES)]
+            out_ref[x * blocks + z] = jnp.concatenate(tiles, axis=0).astype(BF16)
 
 
 def down_project(hid, w, units, chunks=1):
@@ -222,7 +238,7 @@
     )(hid, w)
 
 
-def mix_kernel(rows, routes_ref, gates_ref, home_ref, out_ref):
+def mix_kernel(routes_ref, gates_ref, home_ref, out_ref):
     taken, first, second = place(routes_ref[...])
     gates = gates_ref[...]
     weight = jnp.where(first, gates[0:1], 0.0) + jnp.where(second, gates[1:2], 0.0)
@@ -245,8 +261,8 @@
         home.append(jnp.concatenate(each, axis=0))
     src = lax.broadcasted_iota(jnp.int32, (cols, cols), 0)
     dst = lax.broadcasted_iota(jnp.int32, (cols, cols), 1)
-    block, group, row = src >> (piece.bit_length() - 1), (src & (piece - 1)) >> (rows.bit_length() - 1), src & (rows - 1)
-    order = (dst == group * (blocks * rows) + block * rows + row).astype(F32).astype(BF16)
+    order = dst == (src & (piece - 1)) * blocks + (src >> (piece.bit_length() - 1))
+    order = order.astype(F32).astype(BF16)
     turn = (((0,), (0,)), ((), ()))
     for q in range(blocks):
         chunk = jnp.concatenate([h[:, q * piece : (q + 1) * piece] for h in home], axis=1).astype(BF16)
@@ -258,12 +274,12 @@
         out_ref[:, q * cols : (q + 1) * cols] = total.astype(BF16)
 
 
-def mix(routes_t, gates_t, home, rows):
+def mix(routes_t, gates_t, home):
     toks = routes_t.shape[1]
     owners, height, _ = home.shape
     width = owners // FLIGHT * height // PITCH * LANES
     return pl.pallas_call(
-        lambda *r: mix_kernel(rows, *r),
+        mix_kernel,
         out_shape=jax.ShapeDtypeStruct((toks, width), BF16),
         compiler_params=pltpu.CompilerParams(vmem_limit_bytes=VMEM_LIMIT),
     )(routes_t, gates_t, home)
@@ -275,15 +291,16 @@
     blocks = total // units
     mine = lax.axis_index("y") * lax.axis_size("core") + lax.axis_index("core")
 
-    near = lax.all_to_all(dispatch(routes.T, tokens, dense_down), "x", 0, 0, tiled=True)
-    routed, down = unpack(near, total)
+    near = lax.all_to_all(dispatch(routes.T, tokens), "x", 0, 0, tiled=True)
+    near, pieces = lax.optimization_barrier((near, split(dense_up, dense_down, units)))
+    routed = unpack(near)
     everyone = lax.all_gather(routed, "z", axis=0, tiled=True)
+
+    pieces, _ = lax.optimization_barrier((pieces, routed))
+    got = lax.all_to_all(pieces, ("x", "z"), 0, 0, tiled=True)
+    shard, down = prepare(mine.reshape(1), got, up_noise.T)
     down = lax.all_gather(down, ("y", "core"), axis=0, tiled=True)
-
-    pieces, _ = lax.optimization_barrier((split(dense_up, units), routed))
-    got = lax.all_to_all(pieces, ("x", "z"), 0, 0, tiled=True)
-    shard = prepare(mine.reshape(1), got, up_noise.T).astype(jnp.float16)
-    up = lax.all_gather(shard, ("y", "core"))
+    up = lax.all_gather(shard.astype(jnp.float16), ("y", "core"))
     power = up[:, units : units + 1, :1].astype(F32)
     up = (up[:, :units].astype(F32) * jnp.exp2(-power)).astype(BF16)
 
@@ -291,7 +308,7 @@
     hidden = lax.all_gather(hidden, "z", axis=0, tiled=True).astype(BF16)
     out = down_project(hidden.reshape(blocks, -1, HID_LANES), down, units)
     home = lax.all_to_all(out, ("x", "z"), 0, 0, tiled=True)
-    return mix(routes.T, gate_values.T, home, rows)
+    return mix(routes.T, gate_values.T, home)
 
 
 def solution(mesh):

time: 162 us -> 161 us (level)
  blocking collectives: 99.4 us -> 82.4 us
  Pallas kernels: 15.5 us -> 20.6 us
  starting transfers between devices: 10.8 us -> 15.6 us
  waiting for transfers between devices: 14.3 us -> 18.5 us
    all_to_all x1 -> x0, blocking collectives: 16.5 us -> none  [on_device(): lax.all_to_all(dispatch(routes.T, tokens, dense_down), 'x', 0, 0, tiled=T...]
    all_to_all x1, waiting for transfers between devices: 10.4 us -> 15.5 us  [on_device(): got = lax.all_to_all(pieces, ('x', 'z'), 0, 0, tiled=True)]
    all_to_all x0 -> x1, starting transfers between devices: none -> 4.29 us  [on_device(): near = lax.all_to_all(dispatch(routes.T, tokens), 'x', 0, 0, tiled=True)]
    pallas_call x1, Pallas kernels: 0.8 us -> 4.4 us  [split(): pl.pallas_call(split_kernel, out_shape=jax.ShapeDtypeStruct((flight * tot...]
    all_gather x1, waiting for transfers between devices: 3.19 us -> 1.08 us  [on_device(): down = lax.all_gather(down, ('y', 'core'), axis=0, tiled=True)]
    all_to_all x0 -> x1, waiting for transfers between devices: none -> 1.83 us  [on_device(): near = lax.all_to_all(dispatch(routes.T, tokens), 'x', 0, 0, tiled=True)]
  transfers between devices with their start and end apart: 3 -> 4, of which waited for: 2 -> 3; matrix products, arithmetic and copies ran while one was open for 4% -> 4% of each run, Pallas kernels for 4% -> 6%
where the time goes in v6:
time: 161 us; the launch traced here: 160 us
  blocking collectives  82.4 us (51%)
  Pallas kernels  20.6 us (13%)
  waiting for transfers between devices  18.5 us (11%)
  starting transfers between devices  15.6 us (10%)
  between operations  13.5 us (8%)
  other arithmetic  5.75 us (4%)
  local copies, waits for them, and re-layouts  3.92 us (2%)
    all_gather x1, blocking collectives, on_device(): hidden = lax.all_gather(hidden, 'z', axis=0, tiled=True).astype(BF16)  29.6 us
    all_gather x1, blocking collectives, on_device(): up = lax.all_gather(shard.astype(jnp.float16), ('y', 'core'))  27 us
    all_to_all x1, blocking collectives, on_device(): home = lax.all_to_all(out, ('x', 'z'), 0, 0, tiled=True)  25.8 us
    all_to_all x1, waiting for transfers between devices, on_device(): got = lax.all_to_all(pieces, ('x', 'z'), 0, 0, tiled=True)  15.5 us
    all_to_all x1, starting transfers between devices, on_device(): got = lax.all_to_all(pieces, ('x', 'z'), 0, 0, tiled=True)  11.3 us
    pallas_call x1, Pallas kernels, down_project(): pl.pallas_call(lambda *r: down_kernel(units, *r), in_specs=[pl.BlockSpec(...  4.71 us
    pallas_call x1, Pallas kernels, up_project(): pl.pallas_call(up_kernel, in_specs=[pl.BlockSpec(memory_space=pltpu.HBM)]...  4.7 us
    pallas_call x1, Pallas kernels, split(): pl.pallas_call(split_kernel, out_shape=jax.ShapeDtypeStruct((flight * tot...  4.4 us
  transfers between devices with their start and end apart: 4, of which 3 were waited for; matrix products, arithmetic and copies ran while one was open for 4% of the time, Pallas kernels for 6%

profile of v6, /device:TPU:64, one launch (start us, length us, event | category | flops | bytes accessed | tf_op | source)
XLA Modules:
  0.0 160.3 jit_solution(6797538099707114629)
XLA Ops:
  6.5 0.0 copy-start
  6.5 0.0 copy-start.1
  6.5 1.4 copy-done.1
  7.9 0.0 copy-start.4
  7.9 0.7 copy-done.4
  8.6 1.3 shard_map.64
  9.9 4.3 %all-to-all-start = ((bf16[4,16,3072]{2,1,0:T(8,128)(2,1)}), bf16[4,16,3072]{2,1,0:T(8,128)(2,1)S(1)}, u32[]{:S(2)}, u32[]{:S(2)}) async-start(bf16[4,16,3072]{2,1,0:T(8,128)(2,1)} %shard_map.64), calls=%async_computation | async-start | bytes 786432 | tf_op jit(solution)/shard_map/all_to_all | solution.py:294
  14.2 0.0 all-gather.6.cloned.1.call-start
  14.2 0.0 copy-start.2
  14.2 0.9 copy-done.2
  15.1 0.0 copy-start.3
  15.1 0.9 copy-done.3
  16.0 4.4 %shard_map.65 = bf16[32,16,336]{2,1,0:T(8,128)(2,1)} custom-call(bf16[4,8,2688]{2,1,0:T(8,128)(2,1)S(1)} %copy-done.2, bf16[4,8,2688]{2,1,0:T(8,128)(2,1)S(1)} %copy-done.3), custom_call_target="tpu_custom_call" | custom-call | tf_op jit(solution)/shard_map/pallas_call | solution.py:105
  20.4 1.8 %all-to-all-done.near_ref = bf16[4,16,3072]{2,1,0:T(8,128)(2,1)S(1)} async-done(((bf16[4,16,3072]{2,1,0:T(8,128)(2,1)}), bf16[4,16,3072]{2,1,0:T(8,128)(2,1)S(1)}, u32[]{:S(2)}, u32[]{:S(2)}) %all-to-all-start) | async-done | bytes 393248 | tf_op jit(solution)/shard_map/all_to_all | solution.py:294
  22.2 0.9 shard_map.66
  23.1 0.0 all-gather.6.cloned.1.call-update
  23.2 11.3 %all-to-all-start.1 = ((bf16[32,16,336]{2,1,0:T(8,128)(2,1)}), bf16[32,16,336]{2,1,0:T(8,128)(2,1)S(1)}, u32[]{:S(2)}, u32[]{:S(2)}) async-start(bf16[32,16,336]{2,1,0:T(8,128)(2,1)} %shard_map.65), calls=%async_computation.1 | async-start | bytes 786432 | tf_op jit(solution)/shard_map/all_to_all | solution.py:300
  34.4 0.0 all-gather.8.cloned.1.call-start
  34.5 15.5 %all-to-all-done.1.got_ref = bf16[32,16,336]{2,1,0:T(8,128)(2,1)S(1)} async-done(((bf16[32,16,336]{2,1,0:T(8,128)(2,1)}), bf16[32,16,336]{2,1,0:T(8,128)(2,1)S(1)}, u32[]{:S(2)}, u32[]{:S(2)}) %all-to-all-start.1) | async-done | bytes 344096 | tf_op jit(solution)/shard_map/all_to_all | solution.py:300
  50.0 0.0 copy-done
  50.0 1.1 shard_map.67
  51.2 0.0 all-gather.8.cloned.1.call-update
  51.2 27.0 %all-gather.9 = f16[5504,256]{1,0:T(8,128)(2,1)S(1)} all-gather(f16[344,256]{1,0:T(8,128)(2,1)S(1)} %convert_element_type.18), channel_id=2, replica_groups=mesh['y'=8,'core'=2,'x'=4,'z'=8] {'y','core'}, dimensions={0}, use_global_device_ids=true | all-gather | bytes 2994176 | tf_op jit(solution)/shard_map/all_gather | solution.py:303
  78.2 0.2 fusion.3
  78.4 2.6 %multiply_convert_fusion.w_hbm = bf16[16,336,256]{2,1,0:T(8,128)(2,1)} fusion(f16[16,344,256]{2,1,0:T(8,128)(2,1)S(1)} %bitcast.11, f32[16]{0:T(128)S(1)} %fusion.3), kind=kLoop, calls=%fused_computation | loop fusion | flops 4128768 | bytes 5505088 | tf_op jit(solution)/shard_map/convert_element_type | solution.py:305
  81.0 0.0 all-gather.6.cloned.1.call-done.x_hbm
  81.0 4.7 %shard_map.68 = bf16[384,384]{1,0:T(8,128)(2,1)} custom-call(bf16[384,4096]{1,0:T(8,128)(2,1)} %all-gather.6.cloned.1.call-done.x_hbm, bf16[16,336,256]{2,1,0:T(8,128)(2,1)} %multiply_convert_fusion.w_hbm), custom_call_target="tpu_custom_call" | custom-call | flops 1056964608 | bytes 5898240 | tf_op jit(solution)/shard_map/pallas_call | solution.py:185
  85.7 1.0 convert_element_type.22
  86.7 29.6 %all-gather.10 = f16[3072,384]{1,0:T(8,128)(2,1)S(1)} all-gather(f16[384,384]{1,0:T(8,128)(2,1)S(1)} %convert_element_type.22), channel_id=1, replica_groups=mesh['y'=8,'core'=2,'x'=4,'z'=8] {'z'}, dimensions={0}, use_global_device_ids=true | all-gather | bytes 2654208 | tf_op jit(solution)/shard_map/all_gather | solution.py:308
  116.4 1.9 %convert_element_type.23 = bf16[3072,384]{1,0:T(8,128)(2,1)} convert(f16[3072,384]{1,0:T(8,128)(2,1)S(1)} %all-gather.10) | non-fusion elementwise | flops 1179648 | bytes 4718592 | tf_op jit(solution)/shard_map/convert_element_type | solution.py:308
  118.3 1.1 all-gather.8.cloned.1.call-done.r_1_
  119.3 0.0 copy-start.5
  119.3 0.0 copy-start.6
  119.3 4.7 %shard_map.69 = bf16[32,48,128]{2,1,0:T(8,128)(2,1)} custom-call(bf16[8,384,384]{2,1,0:T(8,128)(2,1)} %bitcast.12, bf16[512,2688]{1,0:T(8,128)(2,1)} %all-gather.8.cloned.1.call-done.r_1_), custom_call_target="tpu_custom_call" | custom-call | flops 1056964608 | bytes 5111808 | tf_op jit(solution)/shard_map/pallas_call | solution.py:227
  124.1 25.8 %all_to_all.15.home_ref = bf16[32,48,128]{2,1,0:T(8,128)(2,1)S(1)} all-to-all(bf16[32,48,128]{2,1,0:T(8,128)(2,1)} %shard_map.69), channel_id=1, replica_groups=mesh['y'=8,'core'=2,'x'=4,'z'=8] {'x','z'}, dimensions={0} | all-to-all | bytes 786432 | tf_op jit(solution)/shard_map/all_to_all | solution.py:310
  149.9 0.0 copy-done.5
  149.9 0.0 copy-done.6
  149.9 3.6 %shard_map.70 = bf16[132,4096]{1,0:T(8,128)(2,1)} custom-call(s32[2,132]{1,0:T(2,128)S(1)} %bitcast.8, f32[2,132]{1,0:T(2,128)S(1)} %bitcast.9, bf16[32,48,128]{2,1,0:T(8,128)(2,1)S(1)} %all_to_all.15.home_ref), custom_call_target="tpu_custom_call" | custom-call | tf_op jit(solution)/shard_map/pallas_call | solution.py:281
  (1 shorter events, 0.0 us)
Async XLA Ops:
  6.5 43.5 %copy-start = (bf16[4096,336]{0,1:T(8,128)(2,1)S(1)}, bf16[4096,336]{0,1:T(8,128)(2,1)}, u32[]{:S(2)}) copy-start(bf16[4096,336]{0,1:T(8,128)(2,1)} %param.11) | copy-start | bytes 8257540
  6.5 1.4 copy-start.1
  7.9 0.7 copy-start.4
  9.9 12.4 %all-to-all-start = ((bf16[4,16,3072]{2,1,0:T(8,128)(2,1)}), bf16[4,16,3072]{2,1,0:T(8,128)(2,1)S(1)}, u32[]{:S(2)}, u32[]{:S(2)}) async-start(bf16[4,16,3072]{2,1,0:T(8,128)(2,1)} %shard_map.64), calls=%async_computation | async-start | bytes 786432 | tf_op jit(solution)/shard_map/all_to_all | solution.py:294
  14.2 66.9 %all-gather.6.cloned.1.call-start = ((), (), s32[]{:S(2)}) async-start(), calls=%async_computation.3 | async-start | bytes 3538944 | tf_op jit(solution)/shard_map/all_gather | solution.py:297
  14.2 0.9 copy-start.2
  15.1 0.9 copy-start.3
  23.2 26.9 %all-to-all-start.1 = ((bf16[32,16,336]{2,1,0:T(8,128)(2,1)}), bf16[32,16,336]{2,1,0:T(8,128)(2,1)S(1)}, u32[]{:S(2)}, u32[]{:S(2)}) async-start(bf16[32,16,336]{2,1,0:T(8,128)(2,1)} %shard_map.65), calls=%async_computation.1 | async-start | bytes 786432 | tf_op jit(solution)/shard_map/all_to_all | solution.py:300
  34.4 84.9 %all-gather.8.cloned.1.call-start = ((), (), s32[]{:S(2)}) async-start(), calls=%async_computation.4 | async-start | bytes 2924544 | tf_op jit(solution)/shard_map/all_gather | solution.py:302
  119.3 30.6 %copy-start.5 = (s32[132,2]{0,1:T(2,128)S(1)}, s32[132,2]{0,1:T(2,128)}, u32[]{:S(2)}) copy-start(s32[132,2]{0,1:T(2,128)} %param.7) | copy-start | bytes 3172
  119.3 30.6 %copy-start.6 = (f32[132,2]{0,1:T(2,128)S(1)}, f32[132,2]{0,1:T(2,128)}, u32[]{:S(2)}) copy-start(f32[132,2]{0,1:T(2,128)} %param.8) | copy-start | bytes 3172
Sparse Core Ops, SparseCore 0:
  23.3 51.4 all-gather.5
  76.9 42.3 all-gather.7

commit v7 on v6

--- a/solution.py
+++ b/solution.py
@@ -42,25 +42,40 @@
     return factor, power
 
 
-def dispatch_kernel(routes_ref, tokens_ref, out_ref):
+def dispatch_kernel(routes_ref, tokens_hbm, out_ref, tokens_ref, sems):
+    chunks, _, piece = tokens_ref.shape
+    copies = [
+        pltpu.make_async_copy(tokens_hbm.at[:, c * piece : (c + 1) * piece], tokens_ref.at[c], sems.at[c]) for c in range(chunks)
+    ]
+    for copy in copies[-1:] + copies[:-1]:
+        copy.start()
     taken, _, _ = place(routes_ref[...])
-    picked = jnp.dot(taken.astype(F32).astype(BF16), tokens_ref[...], preferred_element_type=F32)
-    width = out_ref.shape[2]
-    rest = picked.shape[1] - width
-    fold = width // rest
-    for e in range(FLIGHT):
-        mine = picked[e * PITCH : (e + 1) * PITCH]
-        rows = [mine[:, :width]]
-        for i in range(0, PITCH, fold):
-            rows.append(jnp.concatenate([mine[i + k : i + k + 1, width:] for k in range(fold)], axis=1))
-        out_ref[e] = jnp.concatenate(rows, axis=0).astype(BF16)
+    taken = taken.astype(F32).astype(BF16)
+
+    def pick(c):
+        copies[c].wait()
+        return jnp.dot(taken, tokens_ref[c], preferred_element_type=F32)
+
+    rest = pick(chunks - 1)
+    for c in range(chunks - 1):
+        picked = pick(c)
+        for e in range(FLIGHT):
+            at = e * PITCH
+            tails = [rest[at + i : at + i + 1] for i in range(c, PITCH, chunks - 1)]
+            rows = jnp.concatenate([picked[at : at + PITCH]] + tails, axis=0)
+            out_ref[e, :, c * piece : (c + 1) * piece] = rows.astype(BF16)
 
 
 def dispatch(routes_t, tokens):
+    toks, width = tokens.shape
+    chunks = SENT_ROWS // (SENT_ROWS - PITCH)
+    piece = width // chunks
     return pl.pallas_call(
         dispatch_kernel,
-        out_shape=jax.ShapeDtypeStruct((FLIGHT, SENT_ROWS, tokens.shape[1] * PITCH // SENT_ROWS), BF16),
-        compiler_params=pltpu.CompilerParams(vmem_limit_bytes=VMEM_LIMIT),
+        in_specs=[pl.BlockSpec(memory_space=pltpu.VMEM), pl.BlockSpec(memory_space=pltpu.HBM)],
+        out_shape=jax.ShapeDtypeStruct((FLIGHT, SENT_ROWS, width - piece), BF16),
+        scratch_shapes=[pltpu.VMEM((chunks, toks, piece), BF16), pltpu.SemaphoreType.DMA((chunks,))],
+        compiler_params=pltpu.CompilerParams(vmem_limit_bytes=VMEM_MOST),
     )(routes_t, tokens)
 
 
@@ -150,70 +165,70 @@
     )(mine, got, noise_t)
 
 
-def up_kernel(x_hbm, w_hbm, out_ref, x_ref, w_ref, sems):
-    chunks, group, units, span = w_ref.shape
-    cols = group * span
-    copies = []
-    for c in range(chunks):
-        copies.append(
-            (
-                pltpu.make_async_copy(x_hbm.at[:, c * cols : (c + 1) * cols], x_ref.at[c], sems.at[0, c]),
-                pltpu.make_async_copy(w_hbm.at[c * group : (c + 1) * group], w_ref.at[c], sems.at[1, c]),
-            )
-        )
-    for pair in copies:
-        for copy in pair:
-            copy.start()
+def up_kernel(x_ref, w_ref, out_ref, acc_ref):
+    step = pl.program_id(0)
+    group, units, span = w_ref.shape
     total = None
-    for c, pair in enumerate(copies):
-        for copy in pair:
-            copy.wait()
-        for g in range(group):
-            x = x_ref[c, :, g * span : (g + 1) * span]
-            term = lax.dot_general(x, w_ref[c, g], (((1,), (1,)), ((), ())), preferred_element_type=F32)
-            total = term if total is None else total + term
-    hidden = jnp.square(jnp.maximum(total, 0.0))
-    factor, power = rescale(jnp.max(hidden, axis=1, keepdims=True))
-    hidden = hidden.astype(BF16).astype(F32) * factor
-    power = jnp.broadcast_to(power, (power.shape[0], out_ref.shape[1] - units))
-    out_ref[...] = jnp.concatenate([hidden, power], axis=1).astype(BF16)
-
-
-def up_project(x, w, chunks=4):
+    for g in range(group):
+        x = x_ref[:, g * span : (g + 1) * span]
+        term = lax.dot_general(x, w_ref[g], (((1,), (1,)), ((), ())), preferred_element_type=F32)
+        total = term if total is None else total + term
+
+    @pl.when(step == 0)
+    def _():
+        acc_ref[...] = total
+
+    @pl.when(step > 0)
+    def _():
+        acc_ref[...] += total
+
+    @pl.when(step == pl.num_programs(0) - 1)
+    def _():
+        hidden = jnp.square(jnp.maximum(acc_ref[...], 0.0))
+        factor, power = rescale(jnp.max(hidden, axis=1, keepdims=True))
+        hidden = hidden.astype(BF16).astype(F32) * factor
+        power = jnp.broadcast_to(power, (power.shape[0], out_ref.shape[1] - units))
+        out_ref[...] = jnp.concatenate([hidden, power], axis=1).astype(BF16)
+
+
+def up_project(x, w, group=8):
     rows, width = x.shape
     members, units, span = w.shape
     return pl.pallas_call(
         up_kernel,
-        in_specs=[pl.BlockSpec(memory_space=pltpu.HBM)] * 2,
+        grid=(members // group,),
+        in_specs=[
+            pl.BlockSpec((rows, group * span), lambda i: (0, i)),
+            pl.BlockSpec((group, units, span), lambda i: (i, 0, 0)),
+        ],
+        out_specs=pl.BlockSpec((rows, HID_LANES), lambda i: (0, 0)),
         out_shape=jax.ShapeDtypeStruct((rows, HID_LANES), BF16),
-        scratch_shapes=[
-            pltpu.VMEM((chunks, rows, width // chunks), BF16),
-            pltpu.VMEM((chunks, members // chunks, units, span), BF16),
-            pltpu.SemaphoreType.DMA((2, chunks)),
-        ],
-        compiler_params=pltpu.CompilerParams(vmem_limit_bytes=VMEM_MOST),
+        scratch_shapes=[pltpu.VMEM((rows, units), F32)],
+        compiler_params=pltpu.CompilerParams(vmem_limit_bytes=VMEM_LIMIT),
         cost_estimate=pl.CostEstimate(flops=2 * rows * width * units, bytes_accessed=2 * width * (rows + units), transcendentals=0),
     )(x, w)
 
 
-def down_kernel(units, hid_hbm, w_hbm, out_ref, hid_ref, w_ref, sems):
-    blocks = hid_ref.shape[0]
-    chunks, cols, total = w_ref.shape
-    first = [pltpu.make_async_copy(hid_hbm.at[b], hid_ref.at[b], sems.at[chunks + b]) for b in range(blocks)]
-    copies = [pltpu.make_async_copy(w_hbm.at[c * cols : (c + 1) * cols], w_ref.at[c], sems.at[c]) for c in range(chunks)]
-    for copy in first + copies:
-        copy.start()
+def join_kernel(units, hid_ref, out_ref):
     hidden = []
-    for b in range(blocks):
-        first[b].wait()
+    for b in range(hid_ref.shape[0]):
         h = hid_ref[b].astype(F32)
         hidden.append(h[:, :units] * jnp.exp2(-h[:, units : units + 1]))
-    hidden = jnp.concatenate(hidden, axis=1).astype(BF16)
-    out = []
-    for c, copy in enumerate(copies):
-        copy.wait()
-        out.append(lax.dot_general(hidden, w_ref[c], (((1,), (1,)), ((), ())), preferred_element_type=F32))
-    out = jnp.concatenate(out, axis=1)
+    out_ref[...] = jnp.concatenate(hidden, axis=1).astype(BF16)
+
+
+def join(hid, units):
+    blocks, rows, _ = hid.shape
+    return pl.pallas_call(
+        lambda *r: join_kernel(units, *r),
+        out_shape=jax.ShapeDtypeStruct((rows, blocks * units), BF16),
+        compiler_params=pltpu.CompilerParams(vmem_limit_bytes=VMEM_LIMIT),
+    )(hid)
+
+
+def down_kernel(hid_ref, w_ref, out_ref):
+    out = lax.dot_general(hid_ref[...], w_ref[...], (((1,), (1,)), ((), ())), preferred_element_type=F32)
+    blocks = out_ref.shape[0] // FLIGHT
     for z in range(blocks):
         for x in range(FLIGHT):
             top = (z * FLIGHT + x) * PITCH
@@ -221,20 +236,14 @@
             out_ref[x * blocks + z] = jnp.concatenate(tiles, axis=0).astype(BF16)
 
 
-def down_project(hid, w, units, chunks=1):
-    blocks, rows, lanes = hid.shape
-    cols, total = w.shape
-    return pl.pallas_call(
-        lambda *r: down_kernel(units, *r),
-        in_specs=[pl.BlockSpec(memory_space=pltpu.HBM)] * 2,
+def down_project(hid, w):
+    rows, total = hid.shape
+    cols = w.shape[0]
+    return pl.pallas_call(
+        down_kernel,
         out_shape=jax.ShapeDtypeStruct((rows // PITCH, PITCH * cols // LANES, LANES), BF16),
-        scratch_shapes=[
-            pltpu.VMEM((blocks, rows, lanes), BF16),
-            pltpu.VMEM((chunks, cols // chunks, total), BF16),
-            pltpu.SemaphoreType.DMA((chunks + blocks,)),
-        ],
-        compiler_params=pltpu.CompilerParams(vmem_limit_bytes=VMEM_MOST),
-        cost_estimate=pl.CostEstimate(flops=2 * rows * cols * total, bytes_accessed=2 * cols * total + 2 * blocks * rows * lanes, transcendentals=0),
+        compiler_params=pltpu.CompilerParams(vmem_limit_bytes=VMEM_LIMIT),
+        cost_estimate=pl.CostEstimate(flops=2 * rows * cols * total, bytes_accessed=2 * total * (cols + rows), transcendentals=0),
     )(hid, w)
 
 
@@ -246,7 +255,8 @@
     high = weight.astype(BF16)
     rest = weight - high.astype(F32)
     middle = rest.astype(BF16)
-    low = (rest - middle.astype(F32)).astype(BF16)
+    low = rest - middle.astype(F32)
+    weight = jnp.concatenate([low, middle.astype(F32), high.astype(F32)], axis=0).astype(BF16)
     owners, height, _ = home_ref.shape
     blocks = owners // FLIGHT
     tiles = height // PITCH
@@ -263,14 +273,14 @@
     dst = lax.broadcasted_iota(jnp.int32, (cols, cols), 1)
     order = dst == (src & (piece - 1)) * blocks + (src >> (piece.bit_length() - 1))
     order = order.astype(F32).astype(BF16)
-    turn = (((0,), (0,)), ((), ()))
+    chunks = [jnp.concatenate([h[:, q * piece : (q + 1) * piece] for h in home], axis=1) for q in range(blocks)]
+    count = chunks[0].shape[0]
+    chunks = jnp.dot(jnp.concatenate(chunks, axis=0).astype(BF16), order, preferred_element_type=F32).astype(BF16)
     for q in range(blocks):
-        chunk = jnp.concatenate([h[:, q * piece : (q + 1) * piece] for h in home], axis=1).astype(BF16)
-        chunk = jnp.dot(chunk, order, preferred_element_type=F32).astype(BF16)
-        total = None
-        for part in (low, middle, high):
-            term = lax.dot_general(part, chunk, turn, preferred_element_type=F32)
-            total = term if total is None else total + term
+        chunk = chunks[q * count : (q + 1) * count]
+        total = lax.dot_general(
+            weight, jnp.concatenate([chunk] * 3, axis=0), (((0,), (0,)), ((), ())), preferred_element_type=F32
+        )
         out_ref[:, q * cols : (q + 1) * cols] = total.astype(BF16)
 
 
@@ -306,7 +316,8 @@
 
     hidden = up_project(everyone, up).astype(jnp.float16)
     hidden = lax.all_gather(hidden, "z", axis=0, tiled=True).astype(BF16)
-    out = down_project(hidden.reshape(blocks, -1, HID_LANES), down, units)
+    hidden = join(hidden.reshape(blocks, -1, HID_LANES), units)
+    out = down_project(hidden, down)
     home = lax.all_to_all(out, ("x", "z"), 0, 0, tiled=True)
     return mix(routes.T, gate_values.T, home)
 

time: 161 us -> 157 us (0.975)
  other arithmetic: 5.75 us -> 1.77 us
  Pallas kernels: 20.6 us -> 17 us
  waiting for transfers between devices: 18.5 us -> 20.7 us
    all_gather x1, waiting for transfers between devices: 1.08 us -> 3.27 us  [on_device(): down = lax.all_gather(down, ('y', 'core'), axis=0, tiled=True)]
    pallas_call x3 -> x4, Pallas kernels: 10.7 us -> 8.72 us  [the longest x1 3.17 us: dispatch(): pl.pallas_call(dispatch_kernel, in_specs=[pl.BlockSpec(memory_space=pltpu...]
    pallas_call x1, Pallas kernels: 3.57 us -> 1.91 us  [mix(): pl.pallas_call(mix_kernel, out_shape=jax.ShapeDtypeStruct((toks, width),...]
  transfers between devices with their start and end apart: 4 -> 4, of which waited for: 3 -> 3; matrix products, arithmetic and copies ran while one was open for 4% -> 1% of each run, Pallas kernels for 6% -> 6%
where the time goes in v7:
time: 157 us
  blocking collectives  82.5 us (53%)
  waiting for transfers between devices  20.7 us (13%)
  Pallas kernels  17 us (11%)
  starting transfers between devices  15.9 us (10%)
  between operations  13.5 us (9%)
  local copies, waits for them, and re-layouts  5.51 us (4%)
  other arithmetic  1.77 us (1%)
    all_gather x1, blocking collectives, on_device(): hidden = lax.all_gather(hidden, 'z', axis=0, tiled=True).astype(BF16)  29.9 us
    all_gather x1, blocking collectives, on_device(): up = lax.all_gather(shard.astype(jnp.float16), ('y', 'core'))  27.1 us
    all_to_all x1, blocking collectives, on_device(): home = lax.all_to_all(out, ('x', 'z'), 0, 0, tiled=True)  25.5 us
    all_to_all x1, waiting for transfers between devices, on_device(): got = lax.all_to_all(pieces, ('x', 'z'), 0, 0, tiled=True)  15.5 us
    all_to_all x1, starting transfers between devices, on_device(): got = lax.all_to_all(pieces, ('x', 'z'), 0, 0, tiled=True)  11.3 us
    unnamed x14, local copies, waits for them, and re-layouts  5.51 us
    all_to_all x1, starting transfers between devices, on_device(): near = lax.all_to_all(dispatch(routes.T, tokens), 'x', 0, 0, tiled=True)  4.57 us
    pallas_call x1, Pallas kernels, split(): pl.pallas_call(split_kernel, out_shape=jax.ShapeDtypeStruct((flight * tot...  4.4 us
  transfers between devices with their start and end apart: 4, of which 3 were waited for; matrix products, arithmetic and copies ran while one was open for 1% of the time, Pallas kernels for 6%

profile of v7, /device:TPU:64, one launch (start us, length us, event | category | flops | bytes accessed | tf_op | source)
XLA Modules:
  0.0 156.9 jit_solution(12751335724684743743)
XLA Ops:
  6.5 3.2 %shard_map.64 = bf16[4,16,3072]{2,1,0:T(8,128)(2,1)} custom-call(s32[2,132]{1,0:T(2,128)} %bitcast.8, bf16[132,4096]{1,0:T(8,128)(2,1)} %tokens_hbm.1), custom_call_target="tpu_custom_call" | custom-call | tf_op jit(solution)/shard_map/pallas_call | solution.py:73
  9.7 0.0 copy-start.2
  9.7 4.6 %all-to-all-start = ((bf16[4,16,3072]{2,1,0:T(8,128)(2,1)}), bf16[4,16,3072]{2,1,0:T(8,128)(2,1)S(1)}, u32[]{:S(2)}, u32[]{:S(2)}) async-start(bf16[4,16,3072]{2,1,0:T(8,128)(2,1)} %shard_map.64), calls=%async_computation | async-start | bytes 786432 | tf_op jit(solution)/shard_map/all_to_all | solution.py:304
  14.3 0.0 all-gather.6.cloned.1.call-start
  14.3 0.0 copy-start.3
  14.3 0.9 copy-done.3
  15.2 0.0 copy-start.4
  15.2 0.9 copy-done.4
  16.1 4.4 %shard_map.65 = bf16[32,16,336]{2,1,0:T(8,128)(2,1)} custom-call(bf16[4,8,2688]{2,1,0:T(8,128)(2,1)S(1)} %copy-done.3, bf16[4,8,2688]{2,1,0:T(8,128)(2,1)S(1)} %copy-done.4), custom_call_target="tpu_custom_call" | custom-call | tf_op jit(solution)/shard_map/pallas_call | solution.py:120
  20.5 1.8 %all-to-all-done.near_ref = bf16[4,16,3072]{2,1,0:T(8,128)(2,1)S(1)} async-done(((bf16[4,16,3072]{2,1,0:T(8,128)(2,1)}), bf16[4,16,3072]{2,1,0:T(8,128)(2,1)S(1)}, u32[]{:S(2)}, u32[]{:S(2)}) %all-to-all-start) | async-done | bytes 393248 | tf_op jit(solution)/shard_map/all_to_all | solution.py:304
  22.4 0.9 shard_map.66
  23.3 0.0 all-gather.6.cloned.1.call-update
  23.3 11.3 %all-to-all-start.1 = ((bf16[32,16,336]{2,1,0:T(8,128)(2,1)}), bf16[32,16,336]{2,1,0:T(8,128)(2,1)S(1)}, u32[]{:S(2)}, u32[]{:S(2)}) async-start(bf16[32,16,336]{2,1,0:T(8,128)(2,1)} %shard_map.65), calls=%async_computation.1 | async-start | bytes 786432 | tf_op jit(solution)/shard_map/all_to_all | solution.py:310
  34.6 0.0 all-gather.8.cloned.1.call-start
  34.6 15.5 %all-to-all-done.1.got_ref = bf16[32,16,336]{2,1,0:T(8,128)(2,1)S(1)} async-done(((bf16[32,16,336]{2,1,0:T(8,128)(2,1)}), bf16[32,16,336]{2,1,0:T(8,128)(2,1)S(1)}, u32[]{:S(2)}, u32[]{:S(2)}) %all-to-all-start.1) | async-done | bytes 344096 | tf_op jit(solution)/shard_map/all_to_all | solution.py:310
  50.2 0.0 copy-done.2
  50.2 1.1 shard_map.67
  51.3 0.0 all-gather.8.cloned.1.call-update
  51.3 27.1 %all-gather.9 = f16[5504,256]{1,0:T(8,128)(2,1)S(1)} all-gather(f16[344,256]{1,0:T(8,128)(2,1)S(1)} %convert_element_type.18), channel_id=2, replica_groups=mesh['y'=8,'core'=2,'x'=4,'z'=8] {'y','core'}, dimensions={0}, use_global_device_ids=true | all-gather | bytes 2994176 | tf_op jit(solution)/shard_map/all_gather | solution.py:313
  78.4 0.2 fusion.3
  78.6 1.0 multiply_convert_fusion.w_ref
  79.6 0.0 all-gather.6.cloned.1.call-done.x_ref
  79.7 0.0 copy-start
  79.7 1.9 %copy-done = bf16[384,4096]{1,0:T(8,128)(2,1)S(1)} copy-done((bf16[384,4096]{1,0:T(8,128)(2,1)S(1)}, bf16[384,4096]{1,0:T(8,128)(2,1)}, u32[]{:S(2)}) %copy-start) | copy-done | bytes 3145752
  81.6 2.9 %shard_map.68 = bf16[384,384]{1,0:T(8,128)(2,1)S(1)} custom-call(bf16[384,4096]{1,0:T(8,128)(2,1)S(1)} %copy-done, bf16[16,336,256]{2,1,0:T(8,128)(2,1)S(1)} %multiply_convert_fusion.w_ref), custom_call_target="tpu_custom_call" | custom-call | flops 1056964608 | bytes 5898240 | tf_op jit(solution)/shard_map/pallas_call | solution.py:197
  84.5 0.1 convert_element_type.22
  84.6 29.9 %all-gather.10 = f16[3072,384]{1,0:T(8,128)(2,1)S(1)} all-gather(f16[384,384]{1,0:T(8,128)(2,1)S(1)} %convert_element_type.22), channel_id=1, replica_groups=mesh['y'=8,'core'=2,'x'=4,'z'=8] {'z'}, dimensions={0}, use_global_device_ids=true | all-gather | bytes 2654208 | tf_op jit(solution)/shard_map/all_gather | solution.py:318
  114.5 0.4 convert_element_type.23
  114.9 1.3 shard_map.69.hid_ref
  116.2 3.3 %all-gather.8.cloned.1.call-done.w_ref = bf16[512,2688]{1,0:T(8,128)(2,1)} async-done(((bf16[32,2688]{1,0:T(8,128)(2,1)}), bf16[512,2688]{1,0:T(8,128)(2,1)}) %all-gather.8.cloned.1.call-update) | async-done | bytes 2752528 | tf_op jit(solution)/shard_map/all_gather | solution.py:312
  119.5 0.0 copy-start.1
  119.5 1.8 %copy-done.1 = bf16[512,2688]{1,0:T(8,128)(2,1)S(1)} copy-done((bf16[512,2688]{1,0:T(8,128)(2,1)S(1)}, bf16[512,2688]{1,0:T(8,128)(2,1)}, u32[]{:S(2)}) %copy-start.1) | copy-done | bytes 2752536
  121.2 0.0 copy-start.5
  121.3 0.0 copy-start.6
  121.3 1.3 shard_map.70
  122.6 25.5 %all_to_all.15.home_ref = bf16[32,48,128]{2,1,0:T(8,128)(2,1)S(1)} all-to-all(bf16[32,48,128]{2,1,0:T(8,128)(2,1)S(1)} %shard_map.70), channel_id=1, replica_groups=mesh['y'=8,'core'=2,'x'=4,'z'=8] {'x','z'}, dimensions={0} | all-to-all | bytes 786432 | tf_op jit(solution)/shard_map/all_to_all | solution.py:321
  148.1 0.0 copy-done.5
  148.1 0.0 copy-done.6
  148.1 1.9 %shard_map.71 = bf16[132,4096]{1,0:T(8,128)(2,1)} custom-call(s32[2,132]{1,0:T(2,128)S(1)} %bitcast.9, f32[2,132]{1,0:T(2,128)S(1)} %bitcast.10, bf16[32,48,128]{2,1,0:T(8,128)(2,1)S(1)} %all_to_all.15.home_ref), custom_call_target="tpu_custom_call" | custom-call | tf_op jit(solution)/shard_map/pallas_call | solution.py:291
  (1 shorter events, 0.0 us)
Async XLA Ops:
  9.7 40.5 %copy-start.2 = (bf16[4096,336]{0,1:T(8,128)(2,1)S(1)}, bf16[4096,336]{0,1:T(8,128)(2,1)}, u32[]{:S(2)}) copy-start(bf16[4096,336]{0,1:T(8,128)(2,1)} %param.11) | copy-start | bytes 8257540
  9.7 12.6 %all-to-all-start = ((bf16[4,16,3072]{2,1,0:T(8,128)(2,1)}), bf16[4,16,3072]{2,1,0:T(8,128)(2,1)S(1)}, u32[]{:S(2)}, u32[]{:S(2)}) async-start(bf16[4,16,3072]{2,1,0:T(8,128)(2,1)} %shard_map.64), calls=%async_computation | async-start | bytes 786432 | tf_op jit(solution)/shard_map/all_to_all | solution.py:304
  14.3 65.4 %all-gather.6.cloned.1.call-start = ((), (), s32[]{:S(2)}) async-start(), calls=%async_computation.3 | async-start | bytes 3538944 | tf_op jit(solution)/shard_map/all_gather | solution.py:307
  14.3 0.9 copy-start.3
  15.2 0.9 copy-start.4
  23.3 26.9 %all-to-all-start.1 = ((bf16[32,16,336]{2,1,0:T(8,128)(2,1)}), bf16[32,16,336]{2,1,0:T(8,128)(2,1)S(1)}, u32[]{:S(2)}, u32[]{:S(2)}) async-start(bf16[32,16,336]{2,1,0:T(8,128)(2,1)} %shard_map.65), calls=%async_computation.1 | async-start | bytes 786432 | tf_op jit(solution)/shard_map/all_to_all | solution.py:310
  34.6 84.9 %all-gather.8.cloned.1.call-start = ((), (), s32[]{:S(2)}) async-start(), calls=%async_computation.4 | async-start | bytes 2924544 | tf_op jit(solution)/shard_map/all_gather | solution.py:312
  79.7 1.9 %copy-start = (bf16[384,4096]{1,0:T(8,128)(2,1)S(1)}, bf16[384,4096]{1,0:T(8,128)(2,1)}, u32[]{:S(2)}) copy-start(bf16[384,4096]{1,0:T(8,128)(2,1)} %all-gather.6.cloned.1.call-done.x_ref) | copy-start | bytes 9437188
  119.5 1.8 %copy-start.1 = (bf16[512,2688]{1,0:T(8,128)(2,1)S(1)}, bf16[512,2688]{1,0:T(8,128)(2,1)}, u32[]{:S(2)}) copy-start(bf16[512,2688]{1,0:T(8,128)(2,1)} %all-gather.8.cloned.1.call-done.w_ref) | copy-start | bytes 8257540
  121.2 26.9 %copy-start.5 = (s32[132,2]{0,1:T(2,128)S(1)}, s32[132,2]{0,1:T(2,128)}, u32[]{:S(2)}) copy-start(s32[132,2]{0,1:T(2,128)} %param.7) | copy-start | bytes 3172
  121.3 26.9 %copy-start.6 = (f32[132,2]{0,1:T(2,128)S(1)}, f32[132,2]{0,1:T(2,128)}, u32[]{:S(2)}) copy-start(f32[132,2]{0,1:T(2,128)} %param.8) | copy-start | bytes 3172
Sparse Core Ops, SparseCore 0:
  23.4 51.4 all-gather.5
  77.0 42.3 all-gather.7

commit v8 on v7

v8 whole, which is shorter than its diff:
```python
import jax, jax.numpy as jnp
from jax import lax
from jax.experimental import pallas as pl
from jax.experimental.pallas import tpu as pltpu
from jax.sharding import Mesh, PartitionSpec as P

F32, BF16 = jnp.float32, jnp.bfloat16
PITCH, FLIGHT = 12, 4
LANES, HID_LANES, SENT_ROWS = 128, 384, 16
VMEM_LIMIT = 48 * 1024 * 1024
VMEM_SOME = 52_500_000


def place(routes):
    toks = routes.shape[1]
    rows = FLIGHT * PITCH
    slot = lax.broadcasted_iota(jnp.int32, (rows, toks), 0)
    expert = sum((slot >= PITCH * e).astype(jnp.int32) for e in range(1, FLIGHT))
    slot = slot - PITCH * expert
    first, second = routes[0:1] == expert, routes[1:2] == expert
    present = jnp.logical_or(first, second)
    earlier = lax.broadcasted_iota(jnp.int32, (toks, toks), 0) < lax.broadcasted_iota(jnp.int32, (toks, toks), 1)
    before = jnp.dot(
        present.astype(F32).astype(BF16), earlier.astype(F32).astype(BF16), preferred_element_type=F32
    )
    taken = jnp.logical_and(present, before == slot.astype(F32))
    return taken, first, second


def rescale(top):
    factor, power = jnp.ones_like(top), jnp.zeros_like(top)
    for bits in (32, 16, 8, 4, 2, 1):
        high = top * (2.0**-bits) >= 8192.0
        scale = jnp.where(high, 2.0**-bits, 1.0)
        top, factor = top * scale, factor * scale
        power = power - jnp.where(high, float(bits), 0.0)
    for bits in (32, 16, 8, 4, 2, 1):
        low = top * (2.0**bits) < 16384.0
        scale = jnp.where(low, 2.0**bits, 1.0)
        top, factor = top * scale, factor * scale
        power = power + jnp.where(low, float(bits), 0.0)
    return factor, power


def dispatch_kernel(routes_ref, tokens_hbm, out_ref, shrink_ref, tokens_ref, sems):
    chunks, _, piece = tokens_ref.shape
    copies = [
        pltpu.make_async_copy(tokens_hbm.at[:, c * piece : (c + 1) * piece], tokens_ref.at[c], sems.at[c]) for c in range(chunks)
    ]
    for copy in copies:
        copy.start()
    taken, _, _ = place(routes_ref[...])
    taken = taken.astype(F32).astype(BF16)
    picked, top = [], None
    for c in range(chunks):
        copies[c].wait()
        picked.append(jnp.dot(taken, tokens_ref[c], preferred_element_type=F32))
        most = jnp.max(jnp.abs(picked[c]), axis=1, keepdims=True)
        top = most if top is None else jnp.maximum(top, most)
    grow, _ = rescale(top)
    shrink_ref[...] = 1.0 / grow
    rest = picked[-1] * grow
    for c in range(chunks - 1):
        rows = picked[c] * grow
        for e in range(FLIGHT):
            at = e * PITCH
            tails = [rest[at + i : at + i + 1] for i in range(c, PITCH, chunks - 1)]
            out_ref[e, :, c * piece : (c + 1) * piece] = jnp.concatenate([rows[at : at + PITCH]] + tails, axis=0).astype(BF16)


def dispatch(routes_t, tokens):
    toks, width = tokens.shape
    chunks = SENT_ROWS // (SENT_ROWS - PITCH)
    piece = width // chunks
    return pl.pallas_call(
        dispatch_kernel,
        in_specs=[pl.BlockSpec(memory_space=pltpu.VMEM), pl.BlockSpec(memory_space=pltpu.HBM)],
        out_shape=(
            jax.ShapeDtypeStruct((FLIGHT, SENT_ROWS, width - piece), BF16),
            jax.ShapeDtypeStruct((FLIGHT * PITCH, 1), F32),
        ),
        scratch_shapes=[pltpu.VMEM((chunks, toks, piece), BF16), pltpu.SemaphoreType.DMA((chunks,))],
        compiler_params=pltpu.CompilerParams(vmem_limit_bytes=VMEM_LIMIT),
    )(routes_t, tokens)


def unpack_kernel(here_ref, *refs):
    near, rows_ref = refs[:-1], refs[-1]
    here = here_ref[0]
    short = near[0].shape[1]
    rest = rows_ref.shape[1] - short
    fold = short // rest
    blocks = [ref[...].astype(F32) for ref in near]
    rows = []
    for k in range(FLIGHT):
        sent = blocks[(FLIGHT - 1 - k) % FLIGHT]
        for x in range(FLIGHT - 1):
            sent = jnp.where(here == x, blocks[(x - k) % FLIGHT], sent)
        tails = []
        for i in range(PITCH):
            at = PITCH + i // fold
            tails.append(sent[at : at + 1, i % fold * rest : (i % fold + 1) * rest])
        rows.append(jnp.concatenate([sent[:PITCH], jnp.concatenate(tails, axis=0)], axis=1))
    rows_ref[...] = jnp.concatenate(rows, axis=0).astype(BF16)


def unpack(here, near):
    height, short = near[0].shape
    width = short * height // PITCH
    whole = pl.BlockSpec((height, short), lambda i, m: (0, 0))
    return pl.pallas_call(
        unpack_kernel,
        grid_spec=pltpu.PrefetchScalarGridSpec(
            num_scalar_prefetch=1,
            grid=(1,),
            in_specs=[whole] * len(near),
            out_specs=pl.BlockSpec((len(near) * PITCH, width), lambda i, m: (0, 0)),
        ),
        out_shape=jax.ShapeDtypeStruct((len(near) * PITCH, width), BF16),
        compiler_params=pltpu.CompilerParams(vmem_limit_bytes=VMEM_LIMIT),
    )(here, *near)


def split_kernel(up_ref, down_ref, out_ref):
    flight, rows, total = up_ref.shape
    wide = out_ref.shape[2]
    blocks = out_ref.shape[0] // flight
    units = total // blocks
    rim = jnp.zeros((rows, wide - units), F32)
    fill = jnp.zeros((rows - total // wide, wide), F32)
    for e in range(flight):
        up, down = up_ref[e].astype(F32), down_ref[e].astype(F32)
        for b in range(blocks):
            top = jnp.concatenate([up[:, b * units : (b + 1) * units], rim], axis=1)
            row = [down[b : b + 1, at : at + wide] for at in range(0, total, wide)]
            out_ref[e * blocks + b] = jnp.concatenate([top] + row + [fill], axis=0).astype(BF16)


def split(up, down, blocks):
    flight, rows, _ = up.shape
    return pl.pallas_call(
        split_kernel,
        out_shape=jax.ShapeDtypeStruct((flight * blocks, 2 * rows, HID_LANES), BF16),
        compiler_params=pltpu.CompilerParams(vmem_limit_bytes=VMEM_LIMIT),
    )(up, down)


def prepare_kernel(mine_ref, got_ref, noise_ref, out_ref):
    owners, both, wide = got_ref.shape
    rows = both // 2
    units, span = noise_ref.shape
    got = got_ref[...].astype(F32)
    flat = got[:, :rows, :units].reshape(span, units).astype(BF16)
    same = lax.broadcasted_iota(jnp.int32, (span, span), 0) == lax.broadcasted_iota(jnp.int32, (span, span), 1)
    same = same.astype(F32).astype(BF16)
    up = lax.dot_general(flat, same, (((0,), (0,)), ((), ())), preferred_element_type=F32)
    up = (up + noise_ref[...].astype(F32)).astype(BF16)
    for half in range(span // LANES):
        out_ref[half * units : (half + 1) * units] = up[:, half * LANES : (half + 1) * LANES]
    start = span // LANES * units
    per = wide // LANES
    for q in range((out_ref.shape[0] - start) // owners):
        row = got[:, rows + q // per, q % per * LANES : (q % per + 1) * LANES]
        out_ref[start + q * owners : start + (q + 1) * owners] = row.astype(BF16)


def prepare(mine, got, noise_t, total):
    owners, both, wide = got.shape
    units = noise_t.shape[0]
    span = owners * both // 2
    height = (span * units + owners * total) // LANES
    return pl.pallas_call(
        prepare_kernel,
        grid_spec=pltpu.PrefetchScalarGridSpec(
            num_scalar_prefetch=1,
            grid=(1,),
            in_specs=[
                pl.BlockSpec((owners, both, wide), lambda i, m: (0, 0, 0)),
                pl.BlockSpec((units, span), lambda i, m: (0, m[0])),
            ],
            out_specs=pl.BlockSpec((height, LANES), lambda i, m: (0, 0)),
        ),
        out_shape=jax.ShapeDtypeStruct((height, LANES), BF16),
        compiler_params=pltpu.CompilerParams(vmem_limit_bytes=VMEM_LIMIT),
    )(mine, got, noise_t)


def up_kernel(x_ref, w_ref, out_ref, acc_ref):
    step = pl.program_id(0)
    group, height, _ = w_ref.shape
    units = acc_ref.shape[1]
    parts = height // units
    span = parts * LANES
    total = None
    for g in range(group):
        w = jnp.concatenate([w_ref[g, h * units : (h + 1) * units] for h in range(parts)], axis=1)
        x = x_ref[:, g * span : (g + 1) * span]
        term = lax.dot_general(x, w, (((1,), (1,)), ((), ())), preferred_element_type=F32)
        total = term if total is None else total + term

    @pl.when(step == 0)
    def _():
        acc_ref[...] = total

    @pl.when(step > 0)
    def _():
        acc_ref[...] += total

    @pl.when(step == pl.num_programs(0) - 1)
    def _():
        hidden = jnp.square(jnp.maximum(acc_ref[...], 0.0))
        factor, power = rescale(jnp.max(hidden, axis=1, keepdims=True))
        hidden = hidden.astype(BF16).astype(F32) * factor
        power = jnp.broadcast_to(power, (power.shape[0], out_ref.shape[1] - units))
        out_ref[...] = jnp.concatenate([hidden, power], axis=1).astype(BF16)


def up_project(x, w, units, group=8):
    rows, width = x.shape
    members = w.shape[0]
    span = width // members
    height = span // LANES * units
    return pl.pallas_call(
        up_kernel,
        grid=(members // group,),
        in_specs=[
            pl.BlockSpec((rows, group * span), lambda i: (0, i)),
            pl.BlockSpec((group, height, LANES), lambda i: (i, 0, 0)),
        ],
        out_specs=pl.BlockSpec((rows, HID_LANES), lambda i: (0, 0)),
        out_shape=jax.ShapeDtypeStruct((rows, HID_LANES), BF16),
        scratch_shapes=[pltpu.VMEM((rows, units), F32)],
        compiler_params=pltpu.CompilerParams(vmem_limit_bytes=VMEM_SOME),
        cost_estimate=pl.CostEstimate(flops=2 * rows * width * units, bytes_accessed=2 * width * (rows + units), transcendentals=0),
    )(x, w)


def join_kernel(units, hid_ref, out_ref):
    hidden = []
    for b in range(hid_ref.shape[0]):
        h = hid_ref[b].astype(F32)
        hidden.append(h[:, :units] * jnp.exp2(-h[:, units : units + 1]))
    out_ref[...] = jnp.concatenate(hidden, axis=1).astype(BF16)


def join(hid, units):
    blocks, rows, _ = hid.shape
    return pl.pallas_call(
        lambda *r: join_kernel(units, *r),
        out_shape=jax.ShapeDtypeStruct((rows, blocks * units), BF16),
        compiler_params=pltpu.CompilerParams(vmem_limit_bytes=VMEM_LIMIT),
    )(hid)


def down_kernel(hid_ref, w_ref, out_ref):
    members, height, _ = w_ref.shape
    tiles = hid_ref.shape[1] // LANES
    count = height // tiles
    w = [w_ref[:, q * count : (q + 1) * count].reshape(members * count, LANES) for q in range(tiles)]
    w = jnp.concatenate(w, axis=1)
    out = lax.dot_general(hid_ref[...], w, (((1,), (1,)), ((), ())), preferred_element_type=F32)
    blocks = out_ref.shape[0] // FLIGHT
    for z in range(blocks):
        for x in range(FLIGHT):
            top = (z * FLIGHT + x) * PITCH
            tiles = [out[top : top + PITCH, t : t + LANES] for t in range(0, out.shape[1], LANES)]
            out_ref[x * blocks + z] = jnp.concatenate(tiles, axis=0).astype(BF16)


def down_project(hid, w):
    rows, total = hid.shape
    members, height, _ = w.shape
    cols = members * height // 2 * LANES // total
    return pl.pallas_call(
        down_kernel,
        grid=(1,),
        in_specs=[
            pl.BlockSpec((rows, total), lambda i: (0, 0)),
            pl.BlockSpec((members, height // 2, LANES), lambda i: (0, 1, 0)),
        ],
        out_specs=pl.BlockSpec((rows // PITCH, PITCH * cols // LANES, LANES), lambda i: (0, 0, 0)),
        out_shape=jax.ShapeDtypeStruct((rows // PITCH, PITCH * cols // LANES, LANES), BF16),
        compiler_params=pltpu.CompilerParams(vmem_limit_bytes=VMEM_SOME),
        cost_estimate=pl.CostEstimate(flops=2 * rows * cols * total, bytes_accessed=2 * total * (cols + rows), transcendentals=0),
    )(hid, w)


def mix_kernel(routes_ref, gates_ref, shrink_ref, home_ref, out_ref):
    taken, first, second = place(routes_ref[...])
    gates = gates_ref[...]
    weight = jnp.where(first, gates[0:1], 0.0) + jnp.where(second, gates[1:2], 0.0)
    weight = jnp.where(taken, weight, 0.0) * shrink_ref[...]
    high = weight.astype(BF16)
    rest = weight - high.astype(F32)
    middle = rest.astype(BF16)
    low = rest - middle.astype(F32)
    weight = jnp.concatenate([low, middle.astype(F32), high.astype(F32)], axis=0).astype(BF16)
    owners, height, _ = home_ref.shape
    blocks = owners // FLIGHT
    tiles = height // PITCH
    cols = tiles * LANES
    piece = cols // blocks
    home = []
    for b in range(blocks):
        each = []
        for e in range(FLIGHT):
            tall = home_ref[e * blocks + b].astype(F32)
            each.append(jnp.concatenate([tall[t * PITCH : (t + 1) * PITCH] for t in range(tiles)], axis=1))
        home.append(jnp.concatenate(each, axis=0) * shrink_ref[...])
    src = lax.broadcasted_iota(jnp.int32, (cols, cols), 0)
    dst = lax.broadcasted_iota(jnp.int32, (cols, cols), 1)
    order = dst == (src & (piece - 1)) * blocks + (src >> (piece.bit_length() - 1))
    order = order.astype(F32).astype(BF16)
    chunks = [jnp.concatenate([h[:, q * piece : (q + 1) * piece] for h in home], axis=1) for q in range(blocks)]
    count = chunks[0].shape[0]
    chunks = jnp.dot(jnp.concatenate(chunks, axis=0).astype(BF16), order, preferred_element_type=F32).astype(BF16)
    for q in range(blocks):
        chunk = chunks[q * count : (q + 1) * count]
        total = lax.dot_general(
            weight, jnp.concatenate([chunk] * 3, axis=0), (((0,), (0,)), ((), ())), preferred_element_type=F32
        )
        out_ref[:, q * cols : (q + 1) * cols] = total.astype(BF16)


def mix(routes_t, gates_t, shrink, home):
    toks = routes_t.shape[1]
    owners, height, _ = home.shape
    width = owners // FLIGHT * height // PITCH * LANES
    return pl.pallas_call(
        mix_kernel,
        out_shape=jax.ShapeDtypeStruct((toks, width), BF16),
        compiler_params=pltpu.CompilerParams(vmem_limit_bytes=VMEM_LIMIT),
    )(routes_t, gates_t, shrink, home)


def on_device(tokens, routes, gate_values, dense_up, dense_down, up_noise):
    flight, _, total = dense_up.shape
    units = up_noise.shape[1]
    blocks = total // units
    here = lax.axis_index("x")
    mine = lax.axis_index("y") * lax.axis_size("core") + lax.axis_index("core")

    got = lax.all_to_all(split(dense_up, dense_down, blocks), ("x", "z"), 0, 0, tiled=True)

    outgoing, shrink = dispatch(routes.T, tokens)
    near = []
    for s in range(flight):
        block = lax.dynamic_index_in_dim(outgoing, (here + s) % flight, 0, keepdims=False)
        near.append(lax.ppermute(block, "x", [(i, (i + s) % flight) for i in range(flight)]) if s else block)
    got, near[1], near[2] = lax.optimization_barrier((got, near[1], near[2]))
    shard = prepare(mine.reshape(1), got, up_noise.T, total)
    weights = lax.all_gather(shard, ("y", "core"))
    routed = unpack(here.reshape(1), near).astype(jnp.float16)
    routed, _ = lax.optimization_barrier((routed, shard))
    everyone = lax.all_gather(routed, "z", axis=0, tiled=True).astype(BF16)

    hidden = up_project(everyone, weights, units).astype(jnp.float16)
    hidden = lax.all_gather(hidden, "z", axis=0, tiled=True).astype(BF16)
    hidden = join(hidden.reshape(blocks, -1, HID_LANES), units)
    out = down_project(hidden, weights)
    home = lax.all_to_all(out, ("x", "z"), 0, 0, tiled=True)
    return mix(routes.T, gate_values.T, shrink, home)


def solution(mesh):
    split = Mesh(mesh.devices.reshape(8, 2, 4, 8), ("y", "core", "x", "z"))
    every = ("y", "core", "x", "z")
    return jax.shard_map(
        on_device,
        mesh=split,
        in_specs=(
            P(every, None),
            P(every, None),
            P(every, None),
            P(None, every, None),
            P(None, every, None),
            P(None, ("x", "z")),
        ),
        out_specs=P(every, None),
        check_vma=False,
    )
```

time: 157 us -> 159 us (1.013)
  starting transfers between devices: 15.9 us -> 24.4 us
  waiting for transfers between devices: 20.7 us -> 12.5 us
  blocking collectives: 82.5 us -> 87.7 us
  Pallas kernels: 17 us -> 14.4 us
    all_to_all x2 -> x1, waiting for transfers between devices: 17.4 us -> 0.01 us  [on_device(): lax.all_to_all(split(dense_up, dense_down, blocks), ('x', 'z'), 0, 0, til...]
    ppermute x0 -> x3, starting transfers between devices: none -> 11.8 us  [on_device(): lax.ppermute(block, 'x', [(i, (i + s) % flight) for i in range(flight)])]
    all_gather x1, blocking collectives: 27.1 us -> 34.4 us  [on_device(): everyone = lax.all_gather(routed, 'z', axis=0, tiled=True).astype(BF16)]
    ppermute x0 -> x3, waiting for transfers between devices: none -> 6.4 us  [on_device(): lax.ppermute(block, 'x', [(i, (i + s) % flight) for i in range(flight)])]
    all_to_all x1, blocking collectives: 25.5 us -> 21.1 us  [on_device(): home = lax.all_to_all(out, ('x', 'z'), 0, 0, tiled=True)]
    all_to_all x2 -> x1, starting transfers between devices: 15.8 us -> 12.6 us  [on_device(): lax.all_to_all(split(dense_up, dense_down, blocks), ('x', 'z'), 0, 0, til...]
    all_gather x2 -> x1, waiting for transfers between devices: 3.29 us -> 6.1 us  [on_device(): weights = lax.all_gather(shard, ('y', 'core'))]
    all_gather x1, blocking collectives: 29.9 us -> 32.2 us  [on_device(): hidden = lax.all_gather(hidden, 'z', axis=0, tiled=True).astype(BF16)]
  transfers between devices with their start and end apart: 4 -> 5, of which waited for: 3 -> 3; matrix products, arithmetic and copies ran while one was open for 1% -> 1% of each run, Pallas kernels for 6% -> 1%
where the time goes in v8:
time: 159 us
  blocking collectives  87.7 us (55%)
  starting transfers between devices  24.4 us (15%)
  Pallas kernels  14.4 us (9%)
  between operations  13.6 us (9%)
  waiting for transfers between devices  12.5 us (8%)
  local copies, waits for them, and re-layouts  5.29 us (3%)
    all_gather x1, blocking collectives, on_device(): everyone = lax.all_gather(routed, 'z', axis=0, tiled=True).astype(BF16)  34.4 us
    all_gather x1, blocking collectives, on_device(): hidden = lax.all_gather(hidden, 'z', axis=0, tiled=True).astype(BF16)  32.2 us
    all_to_all x1, blocking collectives, on_device(): home = lax.all_to_all(out, ('x', 'z'), 0, 0, tiled=True)  21.1 us
    all_to_all x1, starting transfers between devices, on_device(): lax.all_to_all(split(dense_up, dense_down, blocks), ('x', 'z'), 0, 0, til...  12.6 us
    ppermute x3, starting transfers between devices, on_device(): lax.ppermute(block, 'x', [(i, (i + s) % flight) for i in range(flight)])  11.8 us
    ppermute x3, waiting for transfers between devices, on_device(): lax.ppermute(block, 'x', [(i, (i + s) % flight) for i in range(flight)])  6.4 us
    all_gather x1, waiting for transfers between devices, on_device(): weights = lax.all_gather(shard, ('y', 'core'))  6.1 us
    unnamed x22, local copies, waits for them, and re-layouts  4.54 us
  transfers between devices with their start and end apart: 5, of which 3 were waited for; matrix products, arithmetic and copies ran while one was open for 1% of the time, Pallas kernels for 1%

profile of v8, /device:TPU:64, one launch (start us, length us, event | category | flops | bytes accessed | tf_op | source)
XLA Modules:
  0.0 158.9 jit_solution(7779821896609920905)
XLA Ops:
  6.5 0.0 copy-start
  6.5 0.0 copy-start.3
  6.5 1.1 copy-done.3
  7.6 0.0 copy-start.4
  7.6 0.9 copy-done.4
  8.5 1.0 shard_map.65
  9.5 12.6 %all-to-all-start = ((bf16[32,16,384]{2,1,0:T(8,128)(2,1)}), bf16[32,16,384]{2,1,0:T(8,128)(2,1)S(1)}, u32[]{:S(2)}, u32[]{:S(2)}) async-start(bf16[32,16,384]{2,1,0:T(8,128)(2,1)} %shard_map.65), calls=%async_computation | async-start | bytes 786432 | tf_op jit(solution)/shard_map/all_to_all | solution.py:343
  22.1 0.0 all-gather.5.cloned.1.call-start
  22.2 0.0 copy-start.1
  22.2 1.2 copy-done.1
  23.5 0.0 copy-start.7
  23.5 0.7 copy-done.7
  24.2 1.5 shard_map.64
  25.7 0.0 copy-start.5
  25.7 0.6 copy-done.5
  26.3 0.8 dynamic-slice_bitcast_fusion
  27.0 0.0 copy-start.10
  27.0 3.5 %collective-permute-start = (bf16[16,3072]{1,0:T(8,128)(2,1)}, bf16[16,3072]{1,0:T(8,128)(2,1)S(1)}, u32[]{:S(2)}, u32[]{:S(2)}) collective-permute-start(bf16[16,3072]{1,0:T(8,128)(2,1)} %get-tuple-element.19), channel_id=1, source_target_pairs={{0,8},{8,16},{16,24},{24,0},{1,9},{9,17},{17,25},{25,1},{2,10},{10... | collective-permute-start | bytes 294920 | tf_op jit(solution)/shard_map/ppermute | solution.py:349
  30.5 4.6 %collective-permute-start.1 = (bf16[16,3072]{1,0:T(8,128)(2,1)}, bf16[16,3072]{1,0:T(8,128)(2,1)S(1)}, u32[]{:S(2)}, u32[]{:S(2)}) collective-permute-start(bf16[16,3072]{1,0:T(8,128)(2,1)} %get-tuple-element.18), channel_id=1, source_target_pairs={{0,16},{8,24},{16,0},{24,8},{1,17},{9,25},{17,1},{25,9},{2,18},{10... | collective-permute-start | bytes 294920 | tf_op jit(solution)/shard_map/ppermute | solution.py:349
  35.2 0.0 collective-permute-done.refs_1_
  35.2 3.5 %collective-permute-done.1.refs_2_ = bf16[16,3072]{1,0:T(8,128)(2,1)S(1)} collective-permute-done((bf16[16,3072]{1,0:T(8,128)(2,1)}, bf16[16,3072]{1,0:T(8,128)(2,1)S(1)}, u32[]{:S(2)}, u32[]{:S(2)}) %collective-permute-start.1) | collective-permute-done | bytes 98336 | tf_op jit(solution)/shard_map/ppermute | solution.py:349
  38.8 0.0 all-to-all-done.got_ref
  38.8 0.0 copy-done
  38.8 1.1 shard_map.67
  39.9 0.0 all-gather.5.cloned.1.call-update
  39.9 0.0 copy-done.10
  39.9 3.7 %collective-permute-start.2 = (bf16[16,3072]{1,0:T(8,128)(2,1)S(1)}, bf16[16,3072]{1,0:T(8,128)(2,1)S(1)}, u32[]{:S(2)}, u32[]{:S(2)}) collective-permute-start(bf16[16,3072]{1,0:T(8,128)(2,1)S(1)} %copy-done.10), channel_id=1, source_target_pairs={{0,24},{8,0},{16,8},{24,16},{1,25},{9,1},{17,9},{25,17},{2,26},{10... | collective-permute-start | bytes 294920 | tf_op jit(solution)/shard_map/ppermute | solution.py:349
  43.6 2.8 %collective-permute-done.2.refs_3_ = bf16[16,3072]{1,0:T(8,128)(2,1)S(1)} collective-permute-done((bf16[16,3072]{1,0:T(8,128)(2,1)S(1)}, bf16[16,3072]{1,0:T(8,128)(2,1)S(1)}, u32[]{:S(2)}, u32[]{:S(2)}) %collective-permute-start.2) | collective-permute-done | bytes 98336 | tf_op jit(solution)/shard_map/ppermute | solution.py:349
  46.4 0.0 copy-done.2
  46.4 0.3 shard_map.66
  46.7 0.1 convert_element_type.12
  46.8 34.4 %all-gather.6 = f16[384,4096]{1,0:T(8,128)(2,1)S(1)} all-gather(f16[48,4096]{1,0:T(8,128)(2,1)S(1)} %convert_element_type.12), channel_id=1, replica_groups=mesh['y'=8,'core'=2,'x'=4,'z'=8] {'z'}, dimensions={0}, use_global_device_ids=true | all-gather | bytes 3538944 | tf_op jit(solution)/shard_map/all_gather | solution.py:355
  81.1 0.4 convert_element_type.13.x_ref
  81.6 6.1 %all-gather.5.cloned.1.call-done = bf16[21504,128]{1,0:T(8,128)(2,1)} async-done(((bf16[1344,128]{1,0:T(8,128)(2,1)}), bf16[21504,128]{1,0:T(8,128)(2,1)}) %all-gather.5.cloned.1.call-update) | async-done | bytes 5505040 | tf_op jit(solution)/shard_map/all_gather | solution.py:352
  87.7 4.2 %shard_map.68 = bf16[384,384]{1,0:T(8,128)(2,1)S(1)} custom-call(bf16[384,4096]{1,0:T(8,128)(2,1)S(1)} %convert_element_type.13.x_ref, bf16[16,1344,128]{2,1,0:T(8,128)(2,1)} %bitcast.20), custom_call_target="tpu_custom_call" | custom-call | flops 1056964608 | bytes 5898240 | tf_op jit(solution)/shard_map/pallas_call | solution.py:223
  91.9 0.1 convert_element_type.14
  91.9 32.2 %all-gather.7 = f16[3072,384]{1,0:T(8,128)(2,1)S(1)} all-gather(f16[384,384]{1,0:T(8,128)(2,1)S(1)} %convert_element_type.14), channel_id=1, replica_groups=mesh['y'=8,'core'=2,'x'=4,'z'=8] {'z'}, dimensions={0}, use_global_device_ids=true | all-gather | bytes 2654208 | tf_op jit(solution)/shard_map/all_gather | solution.py:358
  124.1 0.4 convert_element_type.15
  124.5 1.3 shard_map.69.hid_ref
  125.8 0.0 copy-start.6
  125.9 0.0 copy-start.8
  125.9 0.0 copy-start.9
  125.9 3.1 %shard_map.70 = bf16[32,48,128]{2,1,0:T(8,128)(2,1)S(1)} custom-call(bf16[384,2688]{1,0:T(8,128)(2,1)S(1)} %shard_map.69.hid_ref, bf16[16,1344,128]{2,1,0:T(8,128)(2,1)} %bitcast.21), custom_call_target="tpu_custom_call" | custom-call | flops 1056964608 | bytes 4816896 | tf_op jit(solution)/shard_map/pallas_call | solution.py:274
  129.0 21.1 %all_to_all.10.home_ref = bf16[32,48,128]{2,1,0:T(8,128)(2,1)S(1)} all-to-all(bf16[32,48,128]{2,1,0:T(8,128)(2,1)S(1)} %shard_map.70), channel_id=1, replica_groups=mesh['y'=8,'core'=2,'x'=4,'z'=8] {'x','z'}, dimensions={0} | all-to-all | bytes 786432 | tf_op jit(solution)/shard_map/all_to_all | solution.py:361
  150.1 0.0 copy-done.6
  150.1 0.0 copy-done.8
  150.1 0.0 copy-done.9
  150.1 1.9 %shard_map.71 = bf16[132,4096]{1,0:T(8,128)(2,1)} custom-call(s32[2,132]{1,0:T(2,128)S(1)} %bitcast.18, f32[2,132]{1,0:T(2,128)S(1)} %bitcast.19, f32[48,1]{1,0:T(8,128)S(1)} %copy-done.6, bf16[32,48,128]{2,1,0:T(8,128)(2,1)S(1)} %all_to_all.10.home_ref), custom_call_target="tpu_custom_call" | custom-call | tf_op jit(solution)/shard_map/pallas_call | solution.py:329
  (1 shorter events, 0.0 us)
Async XLA Ops:
  6.5 32.2 %copy-start = (bf16[4096,336]{0,1:T(8,128)(2,1)S(1)}, bf16[4096,336]{0,1:T(8,128)(2,1)}, u32[]{:S(2)}) copy-start(bf16[4096,336]{0,1:T(8,128)(2,1)} %param.11) | copy-start | bytes 8257540
  6.5 1.1 copy-start.3
  7.6 0.9 copy-start.4
  9.5 29.2 %all-to-all-start = ((bf16[32,16,384]{2,1,0:T(8,128)(2,1)}), bf16[32,16,384]{2,1,0:T(8,128)(2,1)S(1)}, u32[]{:S(2)}, u32[]{:S(2)}) async-start(bf16[32,16,384]{2,1,0:T(8,128)(2,1)} %shard_map.65), calls=%async_computation | async-start | bytes 786432 | tf_op jit(solution)/shard_map/all_to_all | solution.py:343
  22.1 65.5 %all-gather.5.cloned.1.call-start = ((), (), s32[]{:S(2)}) async-start(), calls=%async_computation.2 | async-start | bytes 5849088 | tf_op jit(solution)/shard_map/all_gather | solution.py:352
  22.2 1.3 copy-start.1
  23.5 0.7 copy-start.7
  25.7 0.6 copy-start.5
  27.0 12.9 %copy-start.10 = (bf16[16,3072]{1,0:T(8,128)(2,1)S(1)}, bf16[16,3072]{1,0:T(8,128)(2,1)}, u32[]{:S(2)}) copy-start(bf16[16,3072]{1,0:T(8,128)(2,1)} %get-tuple-element.17) | copy-start | bytes 294916
  27.0 19.4 %copy-start.2 = (bf16[16,3072]{1,0:T(8,128)(2,1)S(1)}, bf16[16,3072]{1,0:T(8,128)(2,1)}, u32[]{:S(2)}) copy-start(bf16[16,3072]{1,0:T(8,128)(2,1)} %get-tuple-element.20.refs_0_) | copy-start | bytes 294916
  27.0 8.2 %collective-permute-start = (bf16[16,3072]{1,0:T(8,128)(2,1)}, bf16[16,3072]{1,0:T(8,128)(2,1)S(1)}, u32[]{:S(2)}, u32[]{:S(2)}) collective-permute-start(bf16[16,3072]{1,0:T(8,128)(2,1)} %get-tuple-element.19), channel_id=1, source_target_pairs={{0,8},{8,16},{16,24},{24,0},{1,9},{9,17},{17,25},{25,1},{2,10},{10... | collective-permute-start | bytes 294920 | tf_op jit(solution)/shard_map/ppermute | solution.py:349
  30.5 8.2 %collective-permute-start.1 = (bf16[16,3072]{1,0:T(8,128)(2,1)}, bf16[16,3072]{1,0:T(8,128)(2,1)S(1)}, u32[]{:S(2)}, u32[]{:S(2)}) collective-permute-start(bf16[16,3072]{1,0:T(8,128)(2,1)} %get-tuple-element.18), channel_id=1, source_target_pairs={{0,16},{8,24},{16,0},{24,8},{1,17},{9,25},{17,1},{25,9},{2,18},{10... | collective-permute-start | bytes 294920 | tf_op jit(solution)/shard_map/ppermute | solution.py:349
  39.9 6.5 %collective-permute-start.2 = (bf16[16,3072]{1,0:T(8,128)(2,1)S(1)}, bf16[16,3072]{1,0:T(8,128)(2,1)S(1)}, u32[]{:S(2)}, u32[]{:S(2)}) collective-permute-start(bf16[16,3072]{1,0:T(8,128)(2,1)S(1)} %copy-done.10), channel_id=1, source_target_pairs={{0,24},{8,0},{16,8},{24,16},{1,25},{9,1},{17,9},{25,17},{2,26},{10... | collective-permute-start | bytes 294920 | tf_op jit(solution)/shard_map/ppermute | solution.py:349
  125.8 24.2 %copy-start.6 = (f32[48,1]{1,0:T(8,128)S(1)}, f32[48,1]{1,0:T(8,128)}, u32[]{:S(2)}) copy-start(f32[48,1]{1,0:T(8,128)} %copy-done.5) | copy-start | bytes 580
  125.9 24.2 %copy-start.8 = (s32[132,2]{0,1:T(2,128)S(1)}, s32[132,2]{0,1:T(2,128)}, u32[]{:S(2)}) copy-start(s32[132,2]{0,1:T(2,128)} %param.7) | copy-start | bytes 3172
  125.9 24.2 %copy-start.9 = (f32[132,2]{0,1:T(2,128)S(1)}, f32[132,2]{0,1:T(2,128)}, u32[]{:S(2)}) copy-start(f32[132,2]{0,1:T(2,128)} %param.8) | copy-start | bytes 3172
Sparse Core Ops, SparseCore 0:
  40.0 47.5 all-gather.4

commit v9 on v8

--- a/solution.py
+++ b/solution.py
@@ -8,7 +8,7 @@
 PITCH, FLIGHT = 12, 4
 LANES, HID_LANES, SENT_ROWS = 128, 384, 16
 VMEM_LIMIT = 48 * 1024 * 1024
-VMEM_SOME = 52_500_000
+VMEM_SOME = 48_500_000
 
 
 def place(routes):
@@ -185,51 +185,49 @@
     )(mine, got, noise_t)
 
 
-def up_kernel(x_ref, w_ref, out_ref, acc_ref):
-    step = pl.program_id(0)
-    group, height, _ = w_ref.shape
-    units = acc_ref.shape[1]
+def up_kernel(x_ref, w_hbm, out_ref, down_ref, w_ref, sems):
+    members, height, _ = w_ref.shape
+    chunks = sems.shape[0] - 1
+    group = members // chunks
+    units = height * LANES * members // x_ref.shape[1]
     parts = height // units
     span = parts * LANES
+    copies = []
+    for c in range(chunks):
+        some = slice(c * group, (c + 1) * group)
+        copies.append(pltpu.make_async_copy(w_hbm.at[some, :height], w_ref.at[some], sems.at[c]))
+    later = pltpu.make_async_copy(w_hbm.at[:, height:], down_ref, sems.at[chunks])
+    for copy in copies + [later]:
+        copy.start()
     total = None
-    for g in range(group):
+    for g in range(members):
+        if g % group == 0:
+            copies[g // group].wait()
         w = jnp.concatenate([w_ref[g, h * units : (h + 1) * units] for h in range(parts)], axis=1)
         x = x_ref[:, g * span : (g + 1) * span]
         term = lax.dot_general(x, w, (((1,), (1,)), ((), ())), preferred_element_type=F32)
         total = term if total is None else total + term
-
-    @pl.when(step == 0)
-    def _():
-        acc_ref[...] = total
-
-    @pl.when(step > 0)
-    def _():
-        acc_ref[...] += total
-
-    @pl.when(step == pl.num_programs(0) - 1)
-    def _():
-        hidden = jnp.square(jnp.maximum(acc_ref[...], 0.0))
-        factor, power = rescale(jnp.max(hidden, axis=1, keepdims=True))
-        hidden = hidden.astype(BF16).astype(F32) * factor
-        power = jnp.broadcast_to(power, (power.shape[0], out_ref.shape[1] - units))
-        out_ref[...] = jnp.concatenate([hidden, power], axis=1).astype(BF16)
-
-
-def up_project(x, w, units, group=8):
+    hidden = jnp.square(jnp.maximum(total, 0.0))
+    factor, power = rescale(jnp.max(hidden, axis=1, keepdims=True))
+    hidden = hidden.astype(BF16).astype(F32) * factor
+    power = jnp.broadcast_to(power, (power.shape[0], out_ref.shape[1] - units))
+    out_ref[...] = jnp.concatenate([hidden, power], axis=1).astype(BF16)
+    later.wait()
+
+
+def up_project(x, w, units, chunks=4):
     rows, width = x.shape
-    members = w.shape[0]
-    span = width // members
-    height = span // LANES * units
+    members, both, _ = w.shape
+    height = width // members // LANES * units
     return pl.pallas_call(
         up_kernel,
-        grid=(members // group,),
-        in_specs=[
-            pl.BlockSpec((rows, group * span), lambda i: (0, i)),
-            pl.BlockSpec((group, height, LANES), lambda i: (i, 0, 0)),
-        ],
-        out_specs=pl.BlockSpec((rows, HID_LANES), lambda i: (0, 0)),
-        out_shape=jax.ShapeDtypeStruct((rows, HID_LANES), BF16),
-        scratch_shapes=[pltpu.VMEM((rows, units), F32)],
+        in_specs=[pl.BlockSpec(memory_space=pltpu.VMEM), pl.BlockSpec(memory_space=pltpu.HBM)],
+        out_specs=(pl.BlockSpec(memory_space=pltpu.VMEM), pl.BlockSpec(memory_space=pltpu.VMEM)),
+        out_shape=(
+            jax.ShapeDtypeStruct((rows, HID_LANES), BF16),
+            jax.ShapeDtypeStruct((members, both - height, LANES), BF16),
+        ),
+        scratch_shapes=[pltpu.VMEM((members, height, LANES), BF16), pltpu.SemaphoreType.DMA((chunks + 1,))],
         compiler_params=pltpu.CompilerParams(vmem_limit_bytes=VMEM_SOME),
         cost_estimate=pl.CostEstimate(flops=2 * rows * width * units, bytes_accessed=2 * width * (rows + units), transcendentals=0),
     )(x, w)
@@ -270,17 +268,11 @@
 def down_project(hid, w):
     rows, total = hid.shape
     members, height, _ = w.shape
-    cols = members * height // 2 * LANES // total
+    cols = members * height * LANES // total
     return pl.pallas_call(
         down_kernel,
-        grid=(1,),
-        in_specs=[
-            pl.BlockSpec((rows, total), lambda i: (0, 0)),
-            pl.BlockSpec((members, height // 2, LANES), lambda i: (0, 1, 0)),
-        ],
-        out_specs=pl.BlockSpec((rows // PITCH, PITCH * cols // LANES, LANES), lambda i: (0, 0, 0)),
         out_shape=jax.ShapeDtypeStruct((rows // PITCH, PITCH * cols // LANES, LANES), BF16),
-        compiler_params=pltpu.CompilerParams(vmem_limit_bytes=VMEM_SOME),
+        compiler_params=pltpu.CompilerParams(vmem_limit_bytes=VMEM_LIMIT),
         cost_estimate=pl.CostEstimate(flops=2 * rows * cols * total, bytes_accessed=2 * total * (cols + rows), transcendentals=0),
     )(hid, w)
 
@@ -347,17 +339,17 @@
     for s in range(flight):
         block = lax.dynamic_index_in_dim(outgoing, (here + s) % flight, 0, keepdims=False)
         near.append(lax.ppermute(block, "x", [(i, (i + s) % flight) for i in range(flight)]) if s else block)
-    got, near[1], near[2] = lax.optimization_barrier((got, near[1], near[2]))
+    got, near[1] = lax.optimization_barrier((got, near[1]))
     shard = prepare(mine.reshape(1), got, up_noise.T, total)
     weights = lax.all_gather(shard, ("y", "core"))
     routed = unpack(here.reshape(1), near).astype(jnp.float16)
     routed, _ = lax.optimization_barrier((routed, shard))
     everyone = lax.all_gather(routed, "z", axis=0, tiled=True).astype(BF16)
 
-    hidden = up_project(everyone, weights, units).astype(jnp.float16)
-    hidden = lax.all_gather(hidden, "z", axis=0, tiled=True).astype(BF16)
+    hidden, down = up_project(everyone, weights, units)
+    hidden = lax.all_gather(hidden.astype(jnp.float16), "z", axis=0, tiled=True).astype(BF16)
     hidden = join(hidden.reshape(blocks, -1, HID_LANES), units)
-    out = down_project(hidden, weights)
+    out = down_project(hidden, down)
     home = lax.all_to_all(out, ("x", "z"), 0, 0, tiled=True)
     return mix(routes.T, gate_values.T, shrink, home)
 

time: 159 us -> 152 us (0.956)
  Pallas kernels: 14.4 us -> 12.1 us
  waiting for transfers between devices: 12.5 us -> 10.3 us
    all_gather x1, waiting for transfers between devices: 6.1 us -> 0.99 us  [on_device(): weights = lax.all_gather(shard, ('y', 'core'))]
    pallas_call x2, Pallas kernels: 7.28 us -> 5.02 us  [the longest x1 3.71 us: up_project(): pl.pallas_call(up_kernel, in_specs=[pl.BlockSpec(memory_space=pltpu.VMEM)...]
    all_to_all x1, waiting for transfers between devices: 0.01 us -> 1.78 us  [on_device(): lax.all_to_all(split(dense_up, dense_down, blocks), ('x', 'z'), 0, 0, til...]
    unnamed x22 -> x24, local copies, waits for them, and re-layouts: 4.54 us -> 4.54 us
  transfers between devices with their start and end apart: 5 -> 5, of which waited for: 3 -> 5; matrix products, arithmetic and copies ran while one was open for 1% -> 1% of each run, Pallas kernels for 1% -> 1%
where the time goes in v9:
time: 152 us
  blocking collectives  86.5 us (57%)
  starting transfers between devices  23.2 us (15%)
  between operations  13.6 us (9%)
  Pallas kernels  12.1 us (8%)
  waiting for transfers between devices  10.3 us (7%)
  local copies, waits for them, and re-layouts  5.31 us (3%)
    all_gather x1, blocking collectives, on_device(): everyone = lax.all_gather(routed, 'z', axis=0, tiled=True).astype(BF16)  33.2 us
    all_gather x1, blocking collectives, on_device(): lax.all_gather(hidden.astype(jnp.float16), 'z', axis=0, tiled=True)  32.2 us
    all_to_all x1, blocking collectives, on_device(): home = lax.all_to_all(out, ('x', 'z'), 0, 0, tiled=True)  21.1 us
    all_to_all x1, starting transfers between devices, on_device(): lax.all_to_all(split(dense_up, dense_down, blocks), ('x', 'z'), 0, 0, til...  12.6 us
    ppermute x3, starting transfers between devices, on_device(): lax.ppermute(block, 'x', [(i, (i + s) % flight) for i in range(flight)])  10.6 us
    ppermute x3, waiting for transfers between devices, on_device(): lax.ppermute(block, 'x', [(i, (i + s) % flight) for i in range(flight)])  7.47 us
    unnamed x24, local copies, waits for them, and re-layouts  4.54 us
    pallas_call x1, Pallas kernels, up_project(): pl.pallas_call(up_kernel, in_specs=[pl.BlockSpec(memory_space=pltpu.VMEM)...  3.71 us
  transfers between devices with their start and end apart: 5, of which 5 were waited for; matrix products, arithmetic and copies ran while one was open for 1% of the time, Pallas kernels for 1%

profile of v9, /device:TPU:64, one launch (start us, length us, event | category | flops | bytes accessed | tf_op | source)
XLA Modules:
  0.0 151.9 jit_solution(18278632514293671242)
XLA Ops:
  6.5 0.0 copy-start
  6.5 0.0 copy-start.3
  6.5 1.1 copy-done.3
  7.6 0.0 copy-start.4
  7.6 0.9 copy-done.4
  8.5 1.0 shard_map.65
  9.5 12.6 %all-to-all-start = ((bf16[32,16,384]{2,1,0:T(8,128)(2,1)}), bf16[32,16,384]{2,1,0:T(8,128)(2,1)S(1)}, u32[]{:S(2)}, u32[]{:S(2)}) async-start(bf16[32,16,384]{2,1,0:T(8,128)(2,1)} %shard_map.65), calls=%async_computation | async-start | bytes 786432 | tf_op jit(solution)/shard_map/all_to_all | solution.py:335
  22.1 0.0 all-gather.5.cloned.1.call-start
  22.2 0.0 copy-start.1
  22.2 1.2 copy-done.1
  23.5 0.0 copy-start.7
  23.5 0.7 copy-done.7
  24.2 1.5 shard_map.64
  25.7 0.0 copy-start.5
  25.7 0.6 copy-done.5
  26.3 0.8 dynamic-slice_bitcast_fusion
  27.0 3.5 %collective-permute-start = (bf16[16,3072]{1,0:T(8,128)(2,1)}, bf16[16,3072]{1,0:T(8,128)(2,1)S(1)}, u32[]{:S(2)}, u32[]{:S(2)}) collective-permute-start(bf16[16,3072]{1,0:T(8,128)(2,1)} %get-tuple-element.21), channel_id=1, source_target_pairs={{0,8},{8,16},{16,24},{24,0},{1,9},{9,17},{17,25},{25,1},{2,10},{10... | collective-permute-start | bytes 294920 | tf_op jit(solution)/shard_map/ppermute | solution.py:341
  30.6 4.7 %collective-permute-done.refs_1_ = bf16[16,3072]{1,0:T(8,128)(2,1)S(1)} collective-permute-done((bf16[16,3072]{1,0:T(8,128)(2,1)}, bf16[16,3072]{1,0:T(8,128)(2,1)S(1)}, u32[]{:S(2)}, u32[]{:S(2)}) %collective-permute-start) | collective-permute-done | bytes 98336 | tf_op jit(solution)/shard_map/ppermute | solution.py:341
  35.2 1.8 %all-to-all-done.got_ref = bf16[32,16,384]{2,1,0:T(8,128)(2,1)S(1)} async-done(((bf16[32,16,384]{2,1,0:T(8,128)(2,1)}), bf16[32,16,384]{2,1,0:T(8,128)(2,1)S(1)}, u32[]{:S(2)}, u32[]{:S(2)}) %all-to-all-start) | async-done | bytes 393248 | tf_op jit(solution)/shard_map/all_to_all | solution.py:335
  37.0 0.0 copy-done
  37.0 1.1 shard_map.67
  38.1 0.0 all-gather.5.cloned.1.call-update
  38.1 0.0 copy-done.11
  38.2 3.4 %collective-permute-start.1 = (bf16[16,3072]{1,0:T(8,128)(2,1)S(1)}, bf16[16,3072]{1,0:T(8,128)(2,1)S(1)}, u32[]{:S(2)}, u32[]{:S(2)}) collective-permute-start(bf16[16,3072]{1,0:T(8,128)(2,1)S(1)} %copy-done.11), channel_id=1, source_target_pairs={{0,16},{8,24},{16,0},{24,8},{1,17},{9,25},{17,1},{25,9},{2,18},{10... | collective-permute-start | bytes 294920 | tf_op jit(solution)/shard_map/ppermute | solution.py:341
  41.6 0.0 copy-done.10
  41.6 3.7 %collective-permute-start.2 = (bf16[16,3072]{1,0:T(8,128)(2,1)S(1)}, bf16[16,3072]{1,0:T(8,128)(2,1)S(1)}, u32[]{:S(2)}, u32[]{:S(2)}) collective-permute-start(bf16[16,3072]{1,0:T(8,128)(2,1)S(1)} %copy-done.10), channel_id=1, source_target_pairs={{0,24},{8,0},{16,8},{24,16},{1,25},{9,1},{17,9},{25,17},{2,26},{10... | collective-permute-start | bytes 294920 | tf_op jit(solution)/shard_map/ppermute | solution.py:341
  45.3 0.9 collective-permute-done.1.refs_2_
  46.2 1.9 %collective-permute-done.2.refs_3_ = bf16[16,3072]{1,0:T(8,128)(2,1)S(1)} collective-permute-done((bf16[16,3072]{1,0:T(8,128)(2,1)S(1)}, bf16[16,3072]{1,0:T(8,128)(2,1)S(1)}, u32[]{:S(2)}, u32[]{:S(2)}) %collective-permute-start.2) | collective-permute-done | bytes 98336 | tf_op jit(solution)/shard_map/ppermute | solution.py:341
  48.1 0.0 copy-done.2
  48.1 0.3 shard_map.66
  48.3 0.1 convert_element_type.12
  48.4 33.2 %all-gather.6 = f16[384,4096]{1,0:T(8,128)(2,1)S(1)} all-gather(f16[48,4096]{1,0:T(8,128)(2,1)S(1)} %convert_element_type.12), channel_id=1, replica_groups=mesh['y'=8,'core'=2,'x'=4,'z'=8] {'z'}, dimensions={0}, use_global_device_ids=true | all-gather | bytes 3538944 | tf_op jit(solution)/shard_map/all_gather | solution.py:347
  81.6 0.4 convert_element_type.13.x_ref
  82.0 1.0 all-gather.5.cloned.1.call-done
  83.0 3.7 %shard_map.68 = (bf16[384,384]{1,0:T(8,128)(2,1)S(1)}, bf16[16,672,128]{2,1,0:T(8,128)(2,1)S(1)}) custom-call(bf16[384,4096]{1,0:T(8,128)(2,1)S(1)} %convert_element_type.13.x_ref, bf16[16,1344,128]{2,1,0:T(8,128)(2,1)} %bitcast.20), custom_call_target="tpu_custom_call" | custom-call | flops 1056964608 | bytes 5898240 | tf_op jit(solution)/shard_map/pallas_call | solution.py:222
  86.8 0.1 convert_element_type.14
  86.8 32.2 %all-gather.7 = f16[3072,384]{1,0:T(8,128)(2,1)S(1)} all-gather(f16[384,384]{1,0:T(8,128)(2,1)S(1)} %convert_element_type.14), channel_id=1, replica_groups=mesh['y'=8,'core'=2,'x'=4,'z'=8] {'z'}, dimensions={0}, use_global_device_ids=true | all-gather | bytes 2654208 | tf_op jit(solution)/shard_map/all_gather | solution.py:350
  119.0 0.4 convert_element_type.15
  119.4 1.3 shard_map.69.hid_ref
  120.7 0.0 copy-start.6
  120.7 0.0 copy-start.8
  120.7 0.0 copy-start.9
  120.7 1.3 shard_map.70
  122.0 21.1 %all_to_all.10.home_ref = bf16[32,48,128]{2,1,0:T(8,128)(2,1)S(1)} all-to-all(bf16[32,48,128]{2,1,0:T(8,128)(2,1)S(1)} %shard_map.70), channel_id=1, replica_groups=mesh['y'=8,'core'=2,'x'=4,'z'=8] {'x','z'}, dimensions={0} | all-to-all | bytes 786432 | tf_op jit(solution)/shard_map/all_to_all | solution.py:353
  143.1 0.0 copy-done.6
  143.1 0.0 copy-done.8
  143.1 0.0 copy-done.9
  143.1 1.9 %shard_map.71 = bf16[132,4096]{1,0:T(8,128)(2,1)} custom-call(s32[2,132]{1,0:T(2,128)S(1)} %bitcast.18, f32[2,132]{1,0:T(2,128)S(1)} %bitcast.19, f32[48,1]{1,0:T(8,128)S(1)} %copy-done.6, bf16[32,48,128]{2,1,0:T(8,128)(2,1)S(1)} %all_to_all.10.home_ref), custom_call_target="tpu_custom_call" | custom-call | tf_op jit(solution)/shard_map/pallas_call | solution.py:321
  (3 shorter events, 0.0 us)
Async XLA Ops:
  6.5 30.5 %copy-start = (bf16[4096,336]{0,1:T(8,128)(2,1)S(1)}, bf16[4096,336]{0,1:T(8,128)(2,1)}, u32[]{:S(2)}) copy-start(bf16[4096,336]{0,1:T(8,128)(2,1)} %param.11) | copy-start | bytes 8257540
  6.5 1.1 copy-start.3
  7.6 0.9 copy-start.4
  9.5 27.5 %all-to-all-start = ((bf16[32,16,384]{2,1,0:T(8,128)(2,1)}), bf16[32,16,384]{2,1,0:T(8,128)(2,1)S(1)}, u32[]{:S(2)}, u32[]{:S(2)}) async-start(bf16[32,16,384]{2,1,0:T(8,128)(2,1)} %shard_map.65), calls=%async_computation | async-start | bytes 786432 | tf_op jit(solution)/shard_map/all_to_all | solution.py:335
  22.1 60.9 %all-gather.5.cloned.1.call-start = ((), (), s32[]{:S(2)}) async-start(), calls=%async_computation.2 | async-start | bytes 5849088 | tf_op jit(solution)/shard_map/all_gather | solution.py:344
  22.2 1.3 copy-start.1
  23.5 0.7 copy-start.7
  25.7 0.6 copy-start.5
  27.0 11.1 %copy-start.11 = (bf16[16,3072]{1,0:T(8,128)(2,1)S(1)}, bf16[16,3072]{1,0:T(8,128)(2,1)}, u32[]{:S(2)}) copy-start(bf16[16,3072]{1,0:T(8,128)(2,1)} %get-tuple-element.20) | copy-start | bytes 294916
  27.0 14.5 %copy-start.10 = (bf16[16,3072]{1,0:T(8,128)(2,1)S(1)}, bf16[16,3072]{1,0:T(8,128)(2,1)}, u32[]{:S(2)}) copy-start(bf16[16,3072]{1,0:T(8,128)(2,1)} %get-tuple-element.19) | copy-start | bytes 294916
  27.0 21.0 %copy-start.2 = (bf16[16,3072]{1,0:T(8,128)(2,1)S(1)}, bf16[16,3072]{1,0:T(8,128)(2,1)}, u32[]{:S(2)}) copy-start(bf16[16,3072]{1,0:T(8,128)(2,1)} %get-tuple-element.22.refs_0_) | copy-start | bytes 294916
  27.0 8.2 %collective-permute-start = (bf16[16,3072]{1,0:T(8,128)(2,1)}, bf16[16,3072]{1,0:T(8,128)(2,1)S(1)}, u32[]{:S(2)}, u32[]{:S(2)}) collective-permute-start(bf16[16,3072]{1,0:T(8,128)(2,1)} %get-tuple-element.21), channel_id=1, source_target_pairs={{0,8},{8,16},{16,24},{24,0},{1,9},{9,17},{17,25},{25,1},{2,10},{10... | collective-permute-start | bytes 294920 | tf_op jit(solution)/shard_map/ppermute | solution.py:341
  38.2 8.0 %collective-permute-start.1 = (bf16[16,3072]{1,0:T(8,128)(2,1)S(1)}, bf16[16,3072]{1,0:T(8,128)(2,1)S(1)}, u32[]{:S(2)}, u32[]{:S(2)}) collective-permute-start(bf16[16,3072]{1,0:T(8,128)(2,1)S(1)} %copy-done.11), channel_id=1, source_target_pairs={{0,16},{8,24},{16,0},{24,8},{1,17},{9,25},{17,1},{25,9},{2,18},{10... | collective-permute-start | bytes 294920 | tf_op jit(solution)/shard_map/ppermute | solution.py:341
  41.6 6.5 %collective-permute-start.2 = (bf16[16,3072]{1,0:T(8,128)(2,1)S(1)}, bf16[16,3072]{1,0:T(8,128)(2,1)S(1)}, u32[]{:S(2)}, u32[]{:S(2)}) collective-permute-start(bf16[16,3072]{1,0:T(8,128)(2,1)S(1)} %copy-done.10), channel_id=1, source_target_pairs={{0,24},{8,0},{16,8},{24,16},{1,25},{9,1},{17,9},{25,17},{2,26},{10... | collective-permute-start | bytes 294920 | tf_op jit(solution)/shard_map/ppermute | solution.py:341
  120.7 22.4 %copy-start.6 = (f32[48,1]{1,0:T(8,128)S(1)}, f32[48,1]{1,0:T(8,128)}, u32[]{:S(2)}) copy-start(f32[48,1]{1,0:T(8,128)} %copy-done.5) | copy-start | bytes 580
  120.7 22.4 %copy-start.8 = (s32[132,2]{0,1:T(2,128)S(1)}, s32[132,2]{0,1:T(2,128)}, u32[]{:S(2)}) copy-start(s32[132,2]{0,1:T(2,128)} %param.7) | copy-start | bytes 3172
  120.7 22.4 %copy-start.9 = (f32[132,2]{0,1:T(2,128)S(1)}, f32[132,2]{0,1:T(2,128)}, u32[]{:S(2)}) copy-start(f32[132,2]{0,1:T(2,128)} %param.8) | copy-start | bytes 3172
Sparse Core Ops, SparseCore 0:
  38.3 44.7 all-gather.4

commit v10 on v9

--- a/solution.py
+++ b/solution.py
@@ -9,14 +9,16 @@
 LANES, HID_LANES, SENT_ROWS = 128, 384, 16
 VMEM_LIMIT = 48 * 1024 * 1024
 VMEM_SOME = 48_500_000
-
-
-def place(routes):
+VMEM_MOST = 62 * 1024 * 1024
+
+
+def place(routes, here):
     toks = routes.shape[1]
     rows = FLIGHT * PITCH
     slot = lax.broadcasted_iota(jnp.int32, (rows, toks), 0)
     expert = sum((slot >= PITCH * e).astype(jnp.int32) for e in range(1, FLIGHT))
     slot = slot - PITCH * expert
+    expert = (expert + here) & (FLIGHT - 1)
     first, second = routes[0:1] == expert, routes[1:2] == expert
     present = jnp.logical_or(first, second)
     earlier = lax.broadcasted_iota(jnp.int32, (toks, toks), 0) < lax.broadcasted_iota(jnp.int32, (toks, toks), 1)
@@ -42,19 +44,16 @@
     return factor, power
 
 
-def dispatch_kernel(routes_ref, tokens_hbm, out_ref, shrink_ref, tokens_ref, sems):
-    chunks, _, piece = tokens_ref.shape
-    copies = [
-        pltpu.make_async_copy(tokens_hbm.at[:, c * piece : (c + 1) * piece], tokens_ref.at[c], sems.at[c]) for c in range(chunks)
-    ]
-    for copy in copies:
-        copy.start()
-    taken, _, _ = place(routes_ref[...])
+def dispatch_kernel(here_ref, routes_ref, tokens_ref, *refs):
+    out_refs, shrink_ref = refs[:FLIGHT], refs[FLIGHT]
+    piece = tokens_ref.shape[1] - out_refs[0].shape[1]
+    chunks = tokens_ref.shape[1] // piece
+    taken, _, _ = place(routes_ref[...], here_ref[0])
     taken = taken.astype(F32).astype(BF16)
     picked, top = [], None
     for c in range(chunks):
-        copies[c].wait()
-        picked.append(jnp.dot(taken, tokens_ref[c], preferred_element_type=F32))
+        columns = tokens_ref[:, c * piece : (c + 1) * piece]
+        picked.append(jnp.dot(taken, columns, preferred_element_type=F32))
         most = jnp.max(jnp.abs(picked[c]), axis=1, keepdims=True)
         top = most if top is None else jnp.maximum(top, most)
     grow, _ = rescale(top)
@@ -65,23 +64,26 @@
         for e in range(FLIGHT):
             at = e * PITCH
             tails = [rest[at + i : at + i + 1] for i in range(c, PITCH, chunks - 1)]
-            out_ref[e, :, c * piece : (c + 1) * piece] = jnp.concatenate([rows[at : at + PITCH]] + tails, axis=0).astype(BF16)
-
-
-def dispatch(routes_t, tokens):
-    toks, width = tokens.shape
+            out_refs[e][:, c * piece : (c + 1) * piece] = jnp.concatenate([rows[at : at + PITCH]] + tails, axis=0).astype(BF16)
+
+
+def dispatch(here, routes_t, tokens):
+    width = tokens.shape[1]
     chunks = SENT_ROWS // (SENT_ROWS - PITCH)
     piece = width // chunks
     return pl.pallas_call(
         dispatch_kernel,
-        in_specs=[pl.BlockSpec(memory_space=pltpu.VMEM), pl.BlockSpec(memory_space=pltpu.HBM)],
+        in_specs=[
+            pl.BlockSpec(memory_space=pltpu.SMEM),
+            pl.BlockSpec(memory_space=pltpu.VMEM),
+            pl.BlockSpec(memory_space=pltpu.VMEM),
+        ],
         out_shape=(
-            jax.ShapeDtypeStruct((FLIGHT, SENT_ROWS, width - piece), BF16),
+            *[jax.ShapeDtypeStruct((SENT_ROWS, width - piece), BF16)] * FLIGHT,
             jax.ShapeDtypeStruct((FLIGHT * PITCH, 1), F32),
         ),
-        scratch_shapes=[pltpu.VMEM((chunks, toks, piece), BF16), pltpu.SemaphoreType.DMA((chunks,))],
-        compiler_params=pltpu.CompilerParams(vmem_limit_bytes=VMEM_LIMIT),
-    )(routes_t, tokens)
+        compiler_params=pltpu.CompilerParams(vmem_limit_bytes=VMEM_LIMIT),
+    )(here, routes_t, tokens)
 
 
 def unpack_kernel(here_ref, *refs):
@@ -141,11 +143,11 @@
     return pl.pallas_call(
         split_kernel,
         out_shape=jax.ShapeDtypeStruct((flight * blocks, 2 * rows, HID_LANES), BF16),
-        compiler_params=pltpu.CompilerParams(vmem_limit_bytes=VMEM_LIMIT),
+        compiler_params=pltpu.CompilerParams(vmem_limit_bytes=VMEM_MOST),
     )(up, down)
 
 
-def prepare_kernel(mine_ref, got_ref, noise_ref, out_ref):
+def prepare_kernel(got_ref, noise_ref, out_ref):
     owners, both, wide = got_ref.shape
     rows = both // 2
     units, span = noise_ref.shape
@@ -164,25 +166,14 @@
         out_ref[start + q * owners : start + (q + 1) * owners] = row.astype(BF16)
 
 
-def prepare(mine, got, noise_t, total):
-    owners, both, wide = got.shape
-    units = noise_t.shape[0]
-    span = owners * both // 2
-    height = (span * units + owners * total) // LANES
+def prepare(got, noise_t, total):
+    units, span = noise_t.shape
+    height = (span * units + got.shape[0] * total) // LANES
     return pl.pallas_call(
         prepare_kernel,
-        grid_spec=pltpu.PrefetchScalarGridSpec(
-            num_scalar_prefetch=1,
-            grid=(1,),
-            in_specs=[
-                pl.BlockSpec((owners, both, wide), lambda i, m: (0, 0, 0)),
-                pl.BlockSpec((units, span), lambda i, m: (0, m[0])),
-            ],
-            out_specs=pl.BlockSpec((height, LANES), lambda i, m: (0, 0)),
-        ),
         out_shape=jax.ShapeDtypeStruct((height, LANES), BF16),
         compiler_params=pltpu.CompilerParams(vmem_limit_bytes=VMEM_LIMIT),
-    )(mine, got, noise_t)
+    )(got, noise_t)
 
 
 def up_kernel(x_ref, w_hbm, out_ref, down_ref, w_ref, sems):
@@ -277,8 +268,8 @@
     )(hid, w)
 
 
-def mix_kernel(routes_ref, gates_ref, shrink_ref, home_ref, out_ref):
-    taken, first, second = place(routes_ref[...])
+def mix_kernel(here_ref, routes_ref, gates_ref, shrink_ref, home_ref, out_ref):
+    taken, first, second = place(routes_ref[...], here_ref[0])
     gates = gates_ref[...]
     weight = jnp.where(first, gates[0:1], 0.0) + jnp.where(second, gates[1:2], 0.0)
     weight = jnp.where(taken, weight, 0.0) * shrink_ref[...]
@@ -296,7 +287,7 @@
     for b in range(blocks):
         each = []
         for e in range(FLIGHT):
-            tall = home_ref[e * blocks + b].astype(F32)
+            tall = home_ref[((here_ref[0] + e) & (FLIGHT - 1)) * blocks + b].astype(F32)
             each.append(jnp.concatenate([tall[t * PITCH : (t + 1) * PITCH] for t in range(tiles)], axis=1))
         home.append(jnp.concatenate(each, axis=0) * shrink_ref[...])
     src = lax.broadcasted_iota(jnp.int32, (cols, cols), 0)
@@ -314,35 +305,36 @@
         out_ref[:, q * cols : (q + 1) * cols] = total.astype(BF16)
 
 
-def mix(routes_t, gates_t, shrink, home):
+def mix(here, routes_t, gates_t, shrink, home):
     toks = routes_t.shape[1]
     owners, height, _ = home.shape
     width = owners // FLIGHT * height // PITCH * LANES
     return pl.pallas_call(
         mix_kernel,
+        in_specs=[pl.BlockSpec(memory_space=pltpu.SMEM)] + [pl.BlockSpec(memory_space=pltpu.VMEM)] * 4,
         out_shape=jax.ShapeDtypeStruct((toks, width), BF16),
         compiler_params=pltpu.CompilerParams(vmem_limit_bytes=VMEM_LIMIT),
-    )(routes_t, gates_t, shrink, home)
+    )(here, routes_t, gates_t, shrink, home)
 
 
 def on_device(tokens, routes, gate_values, dense_up, dense_down, up_noise):
     flight, _, total = dense_up.shape
     units = up_noise.shape[1]
     blocks = total // units
-    here = lax.axis_index("x")
+    here = lax.axis_index("x").reshape(1)
     mine = lax.axis_index("y") * lax.axis_size("core") + lax.axis_index("core")
 
     got = lax.all_to_all(split(dense_up, dense_down, blocks), ("x", "z"), 0, 0, tiled=True)
 
-    outgoing, shrink = dispatch(routes.T, tokens)
-    near = []
-    for s in range(flight):
-        block = lax.dynamic_index_in_dim(outgoing, (here + s) % flight, 0, keepdims=False)
-        near.append(lax.ppermute(block, "x", [(i, (i + s) % flight) for i in range(flight)]) if s else block)
-    got, near[1] = lax.optimization_barrier((got, near[1]))
-    shard = prepare(mine.reshape(1), got, up_noise.T, total)
+    *near, shrink = dispatch(here, routes.T, tokens)
+    for s in range(1, flight):
+        near[s] = lax.ppermute(near[s], "x", [(i, (i + s) % flight) for i in range(flight)])
+    span = up_noise.shape[0] // lax.axis_size(("y", "core"))
+    noise = lax.dynamic_slice_in_dim(up_noise.T, mine * span, span, axis=1)
+    got, near[1], noise = lax.optimization_barrier((got, near[1], noise))
+    shard = prepare(got, noise, total)
     weights = lax.all_gather(shard, ("y", "core"))
-    routed = unpack(here.reshape(1), near).astype(jnp.float16)
+    routed = unpack(here, near).astype(jnp.float16)
     routed, _ = lax.optimization_barrier((routed, shard))
     everyone = lax.all_gather(routed, "z", axis=0, tiled=True).astype(BF16)
 
@@ -351,7 +343,7 @@
     hidden = join(hidden.reshape(blocks, -1, HID_LANES), units)
     out = down_project(hidden, down)
     home = lax.all_to_all(out, ("x", "z"), 0, 0, tiled=True)
-    return mix(routes.T, gate_values.T, shrink, home)
+    return mix(here, routes.T, gate_values.T, shrink, home)
 
 
 def solution(mesh):

time: 152 us -> 150 us (0.987)
  local copies, waits for them, and re-layouts: 5.31 us -> 2.87 us
    unnamed x24 -> x8, local copies, waits for them, and re-layouts: 4.54 us -> 1.94 us
    all_to_all x1, waiting for transfers between devices: 1.78 us -> 3.74 us  [on_device(): lax.all_to_all(split(dense_up, dense_down, blocks), ('x', 'z'), 0, 0, til...]
  transfers between devices with their start and end apart: 5 -> 5, of which waited for: 5 -> 4; matrix products, arithmetic and copies ran while one was open for 1% -> 1% of each run, Pallas kernels for 1% -> 1%
where the time goes in v10:
time: 150 us; the launch traced here: 149 us
  blocking collectives  85.6 us (57%)
  starting transfers between devices  23.1 us (15%)
  between operations  13.5 us (9%)
  Pallas kernels  12.4 us (8%)
  waiting for transfers between devices  10.7 us (7%)
  local copies, waits for them, and re-layouts  2.87 us (2%)
    all_gather x1, blocking collectives, on_device(): everyone = lax.all_gather(routed, 'z', axis=0, tiled=True).astype(BF16)  32.8 us
    all_gather x1, blocking collectives, on_device(): lax.all_gather(hidden.astype(jnp.float16), 'z', axis=0, tiled=True)  31.9 us
    all_to_all x1, blocking collectives, on_device(): home = lax.all_to_all(out, ('x', 'z'), 0, 0, tiled=True)  20.9 us
    all_to_all x1, starting transfers between devices, on_device(): lax.all_to_all(split(dense_up, dense_down, blocks), ('x', 'z'), 0, 0, til...  12.6 us
    ppermute x3, starting transfers between devices, on_device(): lax.ppermute(near[s], 'x', [(i, (i + s) % flight) for i in range(flight)])  10.5 us
    ppermute x3, waiting for transfers between devices, on_device(): lax.ppermute(near[s], 'x', [(i, (i + s) % flight) for i in range(flight)])  6.88 us
    all_to_all x1, waiting for transfers between devices, on_device(): lax.all_to_all(split(dense_up, dense_down, blocks), ('x', 'z'), 0, 0, til...  3.74 us
    pallas_call x1, Pallas kernels, up_project(): pl.pallas_call(up_kernel, in_specs=[pl.BlockSpec(memory_space=pltpu.VMEM)...  3.73 us
  transfers between devices with their start and end apart: 5, of which 4 were waited for; matrix products, arithmetic and copies ran while one was open for 1% of the time, Pallas kernels for 1%

profile of v10, /device:TPU:64, one launch (start us, length us, event | category | flops | bytes accessed | tf_op | source)
XLA Modules:
  0.0 149.2 jit_solution(16280665040256883025)
XLA Ops:
  6.5 2.0 %shard_map.65 = bf16[32,16,384]{2,1,0:T(8,128)(2,1)} custom-call(bf16[4,8,2688]{2,1,0:T(8,128)(2,1)} %up_ref.1, bf16[4,8,2688]{2,1,0:T(8,128)(2,1)} %down_ref.1), custom_call_target="tpu_custom_call" | custom-call | tf_op jit(solution)/shard_map/pallas_call | solution.py:143
  8.6 12.6 %all-to-all-start = ((bf16[32,16,384]{2,1,0:T(8,128)(2,1)}), bf16[32,16,384]{2,1,0:T(8,128)(2,1)S(1)}, u32[]{:S(2)}, u32[]{:S(2)}) async-start(bf16[32,16,384]{2,1,0:T(8,128)(2,1)} %shard_map.65), calls=%async_computation | async-start | bytes 786432 | tf_op jit(solution)/shard_map/all_to_all | solution.py:327
  21.1 0.0 all-gather.5.cloned.1.call-start
  21.2 0.0 copy-start
  21.2 1.2 copy-done
  22.4 0.0 copy-start.1
  22.5 0.7 copy-done.1
  23.1 0.7 shard_map.64
  23.9 3.4 %collective-permute-start = (bf16[16,3072]{1,0:T(8,128)(2,1)S(1)}, bf16[16,3072]{1,0:T(8,128)(2,1)S(1)}, u32[]{:S(2)}, u32[]{:S(2)}) collective-permute-start(bf16[16,3072]{1,0:T(8,128)(2,1)S(1)} %get-tuple-element.18), channel_id=1, source_target_pairs={{0,8},{8,16},{16,24},{24,0},{1,9},{9,17},{17,25},{25,1},{2,10},{10... | collective-permute-start | bytes 294920 | tf_op jit(solution)/shard_map/ppermute | solution.py:331
  27.3 0.9 dynamic-slice_bitcast_fusion.noise_ref
  28.2 4.1 %collective-permute-done.refs_1_ = bf16[16,3072]{1,0:T(8,128)(2,1)S(1)} collective-permute-done((bf16[16,3072]{1,0:T(8,128)(2,1)S(1)}, bf16[16,3072]{1,0:T(8,128)(2,1)S(1)}, u32[]{:S(2)}, u32[]{:S(2)}) %collective-permute-start) | collective-permute-done | bytes 98336 | tf_op jit(solution)/shard_map/ppermute | solution.py:331
  32.3 3.7 %all-to-all-done.got_ref = bf16[32,16,384]{2,1,0:T(8,128)(2,1)S(1)} async-done(((bf16[32,16,384]{2,1,0:T(8,128)(2,1)}), bf16[32,16,384]{2,1,0:T(8,128)(2,1)S(1)}, u32[]{:S(2)}, u32[]{:S(2)}) %all-to-all-start) | async-done | bytes 393248 | tf_op jit(solution)/shard_map/all_to_all | solution.py:327
  36.0 1.1 shard_map.67
  37.1 0.0 all-gather.5.cloned.1.call-update
  37.2 3.4 %collective-permute-start.1 = (bf16[16,3072]{1,0:T(8,128)(2,1)S(1)}, bf16[16,3072]{1,0:T(8,128)(2,1)S(1)}, u32[]{:S(2)}, u32[]{:S(2)}) collective-permute-start(bf16[16,3072]{1,0:T(8,128)(2,1)S(1)} %get-tuple-element.20), channel_id=1, source_target_pairs={{0,16},{8,24},{16,0},{24,8},{1,17},{9,25},{17,1},{25,9},{2,18},{10... | collective-permute-start | bytes 294920 | tf_op jit(solution)/shard_map/ppermute | solution.py:331
  40.6 3.7 %collective-permute-start.2 = (bf16[16,3072]{1,0:T(8,128)(2,1)S(1)}, bf16[16,3072]{1,0:T(8,128)(2,1)S(1)}, u32[]{:S(2)}, u32[]{:S(2)}) collective-permute-start(bf16[16,3072]{1,0:T(8,128)(2,1)S(1)} %get-tuple-element.21), channel_id=1, source_target_pairs={{0,24},{8,0},{16,8},{24,16},{1,25},{9,1},{17,9},{25,17},{2,26},{10... | collective-permute-start | bytes 294920 | tf_op jit(solution)/shard_map/ppermute | solution.py:331
  44.3 0.9 collective-permute-done.1.refs_2_
  45.2 1.9 %collective-permute-done.2.refs_3_ = bf16[16,3072]{1,0:T(8,128)(2,1)S(1)} collective-permute-done((bf16[16,3072]{1,0:T(8,128)(2,1)S(1)}, bf16[16,3072]{1,0:T(8,128)(2,1)S(1)}, u32[]{:S(2)}, u32[]{:S(2)}) %collective-permute-start.2) | collective-permute-done | bytes 98336 | tf_op jit(solution)/shard_map/ppermute | solution.py:331
  47.1 0.3 shard_map.66
  47.3 0.1 convert_element_type.12
  47.4 32.8 %all-gather.6 = f16[384,4096]{1,0:T(8,128)(2,1)S(1)} all-gather(f16[48,4096]{1,0:T(8,128)(2,1)S(1)} %convert_element_type.12), channel_id=1, replica_groups=mesh['y'=8,'core'=2,'x'=4,'z'=8] {'z'}, dimensions={0}, use_global_device_ids=true | all-gather | bytes 3538944 | tf_op jit(solution)/shard_map/all_gather | solution.py:339
  80.2 0.4 convert_element_type.13.x_ref
  80.6 0.0 all-gather.5.cloned.1.call-done
  80.6 3.7 %shard_map.68 = (bf16[384,384]{1,0:T(8,128)(2,1)S(1)}, bf16[16,672,128]{2,1,0:T(8,128)(2,1)S(1)}) custom-call(bf16[384,4096]{1,0:T(8,128)(2,1)S(1)} %convert_element_type.13.x_ref, bf16[16,1344,128]{2,1,0:T(8,128)(2,1)} %bitcast.11), custom_call_target="tpu_custom_call" | custom-call | flops 1056964608 | bytes 5898240 | tf_op jit(solution)/shard_map/pallas_call | solution.py:213
  84.4 0.1 convert_element_type.14
  84.4 31.9 %all-gather.7 = f16[3072,384]{1,0:T(8,128)(2,1)S(1)} all-gather(f16[384,384]{1,0:T(8,128)(2,1)S(1)} %convert_element_type.14), channel_id=1, replica_groups=mesh['y'=8,'core'=2,'x'=4,'z'=8] {'z'}, dimensions={0}, use_global_device_ids=true | all-gather | bytes 2654208 | tf_op jit(solution)/shard_map/all_gather | solution.py:342
  116.3 0.4 convert_element_type.15
  116.8 1.3 shard_map.69.hid_ref
  118.1 0.0 copy-start.2
  118.1 0.0 copy-start.3
  118.2 1.3 shard_map.70
  119.5 20.9 %all_to_all.10.home_ref = bf16[32,48,128]{2,1,0:T(8,128)(2,1)S(1)} all-to-all(bf16[32,48,128]{2,1,0:T(8,128)(2,1)S(1)} %shard_map.70), channel_id=1, replica_groups=mesh['y'=8,'core'=2,'x'=4,'z'=8] {'x','z'}, dimensions={0} | all-to-all | bytes 786432 | tf_op jit(solution)/shard_map/all_to_all | solution.py:345
  140.4 0.0 copy-done.2
  140.4 0.0 copy-done.3
  140.4 1.9 %shard_map.71 = bf16[132,4096]{1,0:T(8,128)(2,1)} custom-call(s32[1]{0:T(128)} %bitcast.here_ref, s32[2,132]{1,0:T(2,128)S(1)} %bitcast.9, f32[2,132]{1,0:T(2,128)S(1)} %bitcast.10, f32[48,1]{1,0:T(8,128)S(1)} %get-tuple-element.16.shrink_ref, bf16[32,48,128]{2,1,0:T(8,128)(2,1)S(1)} %all_to_all.10.home_ref), custom_call_target="tpu_custom_call" | custom-call | tf_op jit(solution)/shard_map/pallas_call | solution.py:312
Async XLA Ops:
  8.6 27.5 %all-to-all-start = ((bf16[32,16,384]{2,1,0:T(8,128)(2,1)}), bf16[32,16,384]{2,1,0:T(8,128)(2,1)S(1)}, u32[]{:S(2)}, u32[]{:S(2)}) async-start(bf16[32,16,384]{2,1,0:T(8,128)(2,1)} %shard_map.65), calls=%async_computation | async-start | bytes 786432 | tf_op jit(solution)/shard_map/all_to_all | solution.py:327
  21.1 59.5 %all-gather.5.cloned.1.call-start = ((), (), s32[]{:S(2)}) async-start(), calls=%async_computation.2 | async-start | bytes 5849088 | tf_op jit(solution)/shard_map/all_gather | solution.py:336
  21.2 1.3 copy-start
  22.4 0.7 copy-start.1
  23.9 8.4 %collective-permute-start = (bf16[16,3072]{1,0:T(8,128)(2,1)S(1)}, bf16[16,3072]{1,0:T(8,128)(2,1)S(1)}, u32[]{:S(2)}, u32[]{:S(2)}) collective-permute-start(bf16[16,3072]{1,0:T(8,128)(2,1)S(1)} %get-tuple-element.18), channel_id=1, source_target_pairs={{0,8},{8,16},{16,24},{24,0},{1,9},{9,17},{17,25},{25,1},{2,10},{10... | collective-permute-start | bytes 294920 | tf_op jit(solution)/shard_map/ppermute | solution.py:331
  37.2 8.0 %collective-permute-start.1 = (bf16[16,3072]{1,0:T(8,128)(2,1)S(1)}, bf16[16,3072]{1,0:T(8,128)(2,1)S(1)}, u32[]{:S(2)}, u32[]{:S(2)}) collective-permute-start(bf16[16,3072]{1,0:T(8,128)(2,1)S(1)} %get-tuple-element.20), channel_id=1, source_target_pairs={{0,16},{8,24},{16,0},{24,8},{1,17},{9,25},{17,1},{25,9},{2,18},{10... | collective-permute-start | bytes 294920 | tf_op jit(solution)/shard_map/ppermute | solution.py:331
  40.6 6.5 %collective-permute-start.2 = (bf16[16,3072]{1,0:T(8,128)(2,1)S(1)}, bf16[16,3072]{1,0:T(8,128)(2,1)S(1)}, u32[]{:S(2)}, u32[]{:S(2)}) collective-permute-start(bf16[16,3072]{1,0:T(8,128)(2,1)S(1)} %get-tuple-element.21), channel_id=1, source_target_pairs={{0,24},{8,0},{16,8},{24,16},{1,25},{9,1},{17,9},{25,17},{2,26},{10... | collective-permute-start | bytes 294920 | tf_op jit(solution)/shard_map/ppermute | solution.py:331
  118.1 22.2 %copy-start.2 = (s32[132,2]{0,1:T(2,128)S(1)}, s32[132,2]{0,1:T(2,128)}, u32[]{:S(2)}) copy-start(s32[132,2]{0,1:T(2,128)} %param.7) | copy-start | bytes 3172
  118.1 22.2 %copy-start.3 = (f32[132,2]{0,1:T(2,128)S(1)}, f32[132,2]{0,1:T(2,128)}, u32[]{:S(2)}) copy-start(f32[132,2]{0,1:T(2,128)} %param.8) | copy-start | bytes 3172
Sparse Core Ops, SparseCore 0:
  37.3 42.8 all-gather.4

commit v11 on v10

--- a/solution.py
+++ b/solution.py
@@ -331,7 +331,7 @@
         near[s] = lax.ppermute(near[s], "x", [(i, (i + s) % flight) for i in range(flight)])
     span = up_noise.shape[0] // lax.axis_size(("y", "core"))
     noise = lax.dynamic_slice_in_dim(up_noise.T, mine * span, span, axis=1)
-    got, near[1], noise = lax.optimization_barrier((got, near[1], noise))
+    got, near[1], near[2], noise = lax.optimization_barrier((got, near[1], near[2], noise))
     shard = prepare(got, noise, total)
     weights = lax.all_gather(shard, ("y", "core"))
     routed = unpack(here, near).astype(jnp.float16)

time: 150 us -> 154 us (1.027)
  blocking collectives: 85.6 us -> 87.3 us
  waiting for transfers between devices: 10.7 us -> 12.3 us
    all_gather x1, waiting for transfers between devices: 0.02 us -> 5.74 us  [on_device(): weights = lax.all_gather(shard, ('y', 'core'))]
    all_to_all x1, waiting for transfers between devices: 3.74 us -> 0.36 us  [on_device(): lax.all_to_all(split(dense_up, dense_down, blocks), ('x', 'z'), 0, 0, til...]
where the time goes in v11:
time: 154 us; the launch traced here: 153 us
  blocking collectives  87.3 us (57%)
  starting transfers between devices  23.8 us (15%)
  between operations  13.5 us (9%)
  Pallas kernels  12.4 us (8%)
  waiting for transfers between devices  12.3 us (8%)
  local copies, waits for them, and re-layouts  2.87 us (2%)
    all_gather x1, blocking collectives, on_device(): everyone = lax.all_gather(routed, 'z', axis=0, tiled=True).astype(BF16)  34 us
    all_gather x1, blocking collectives, on_device(): lax.all_gather(hidden.astype(jnp.float16), 'z', axis=0, tiled=True)  32.2 us
    all_to_all x1, blocking collectives, on_device(): home = lax.all_to_all(out, ('x', 'z'), 0, 0, tiled=True)  21.1 us
    all_to_all x1, starting transfers between devices, on_device(): lax.all_to_all(split(dense_up, dense_down, blocks), ('x', 'z'), 0, 0, til...  12.6 us
    ppermute x3, starting transfers between devices, on_device(): lax.ppermute(near[s], 'x', [(i, (i + s) % flight) for i in range(flight)])  11.2 us
    ppermute x3, waiting for transfers between devices, on_device(): lax.ppermute(near[s], 'x', [(i, (i + s) % flight) for i in range(flight)])  6.15 us
    all_gather x1, waiting for transfers between devices, on_device(): weights = lax.all_gather(shard, ('y', 'core'))  5.74 us
    pallas_call x1, Pallas kernels, up_project(): pl.pallas_call(up_kernel, in_specs=[pl.BlockSpec(memory_space=pltpu.VMEM)...  3.72 us
  transfers between devices with their start and end apart: 5, of which 4 were waited for; matrix products, arithmetic and copies ran while one was open for 1% of the time, Pallas kernels for 1%

profile of v11, /device:TPU:64, one launch (start us, length us, event | category | flops | bytes accessed | tf_op | source)
XLA Modules:
  0.0 153.2 jit_solution(2090501851638358966)
XLA Ops:
  6.5 2.0 %shard_map.65 = bf16[32,16,384]{2,1,0:T(8,128)(2,1)} custom-call(bf16[4,8,2688]{2,1,0:T(8,128)(2,1)} %up_ref.1, bf16[4,8,2688]{2,1,0:T(8,128)(2,1)} %down_ref.1), custom_call_target="tpu_custom_call" | custom-call | tf_op jit(solution)/shard_map/pallas_call | solution.py:143
  8.6 12.6 %all-to-all-start = ((bf16[32,16,384]{2,1,0:T(8,128)(2,1)}), bf16[32,16,384]{2,1,0:T(8,128)(2,1)S(1)}, u32[]{:S(2)}, u32[]{:S(2)}) async-start(bf16[32,16,384]{2,1,0:T(8,128)(2,1)} %shard_map.65), calls=%async_computation | async-start | bytes 786432 | tf_op jit(solution)/shard_map/all_to_all | solution.py:327
  21.1 0.0 all-gather.5.cloned.1.call-start
  21.2 0.0 copy-start
  21.2 1.2 copy-done
  22.4 0.0 copy-start.1
  22.5 0.7 copy-done.1
  23.1 0.7 shard_map.64
  23.9 3.4 %collective-permute-start = (bf16[16,3072]{1,0:T(8,128)(2,1)S(1)}, bf16[16,3072]{1,0:T(8,128)(2,1)S(1)}, u32[]{:S(2)}, u32[]{:S(2)}) collective-permute-start(bf16[16,3072]{1,0:T(8,128)(2,1)S(1)} %get-tuple-element.19), channel_id=1, source_target_pairs={{0,8},{8,16},{16,24},{24,0},{1,9},{9,17},{17,25},{25,1},{2,10},{10... | collective-permute-start | bytes 294920 | tf_op jit(solution)/shard_map/ppermute | solution.py:331
  27.2 4.6 %collective-permute-start.1 = (bf16[16,3072]{1,0:T(8,128)(2,1)S(1)}, bf16[16,3072]{1,0:T(8,128)(2,1)S(1)}, u32[]{:S(2)}, u32[]{:S(2)}) collective-permute-start(bf16[16,3072]{1,0:T(8,128)(2,1)S(1)} %get-tuple-element.20), channel_id=1, source_target_pairs={{0,16},{8,24},{16,0},{24,8},{1,17},{9,25},{17,1},{25,9},{2,18},{10... | collective-permute-start | bytes 294920 | tf_op jit(solution)/shard_map/ppermute | solution.py:331
  31.9 0.9 dynamic-slice_bitcast_fusion.noise_ref
  32.8 0.0 collective-permute-done.refs_1_
  32.8 2.8 %collective-permute-done.1.refs_2_ = bf16[16,3072]{1,0:T(8,128)(2,1)S(1)} collective-permute-done((bf16[16,3072]{1,0:T(8,128)(2,1)S(1)}, bf16[16,3072]{1,0:T(8,128)(2,1)S(1)}, u32[]{:S(2)}, u32[]{:S(2)}) %collective-permute-start.1) | collective-permute-done | bytes 98336 | tf_op jit(solution)/shard_map/ppermute | solution.py:331
  35.7 0.4 all-to-all-done.got_ref
  36.0 1.1 shard_map.67
  37.1 0.0 all-gather.5.cloned.1.call-update
  37.2 3.2 %collective-permute-start.2 = (bf16[16,3072]{1,0:T(8,128)(2,1)S(1)}, bf16[16,3072]{1,0:T(8,128)(2,1)S(1)}, u32[]{:S(2)}, u32[]{:S(2)}) collective-permute-start(bf16[16,3072]{1,0:T(8,128)(2,1)S(1)} %get-tuple-element.23), channel_id=1, source_target_pairs={{0,24},{8,0},{16,8},{24,16},{1,25},{9,1},{17,9},{25,17},{2,26},{10... | collective-permute-start | bytes 294920 | tf_op jit(solution)/shard_map/ppermute | solution.py:331
  40.3 3.3 %collective-permute-done.2.refs_3_ = bf16[16,3072]{1,0:T(8,128)(2,1)S(1)} collective-permute-done((bf16[16,3072]{1,0:T(8,128)(2,1)S(1)}, bf16[16,3072]{1,0:T(8,128)(2,1)S(1)}, u32[]{:S(2)}, u32[]{:S(2)}) %collective-permute-start.2) | collective-permute-done | bytes 98336 | tf_op jit(solution)/shard_map/ppermute | solution.py:331
  43.7 0.3 shard_map.66
  43.9 0.1 convert_element_type.12
  44.0 34.0 %all-gather.6 = f16[384,4096]{1,0:T(8,128)(2,1)S(1)} all-gather(f16[48,4096]{1,0:T(8,128)(2,1)S(1)} %convert_element_type.12), channel_id=1, replica_groups=mesh['y'=8,'core'=2,'x'=4,'z'=8] {'z'}, dimensions={0}, use_global_device_ids=true | all-gather | bytes 3538944 | tf_op jit(solution)/shard_map/all_gather | solution.py:339
  78.0 0.4 convert_element_type.13.x_ref
  78.4 5.7 %all-gather.5.cloned.1.call-done = bf16[21504,128]{1,0:T(8,128)(2,1)} async-done(((bf16[1344,128]{1,0:T(8,128)(2,1)}), bf16[21504,128]{1,0:T(8,128)(2,1)}) %all-gather.5.cloned.1.call-update) | async-done | bytes 5505040 | tf_op jit(solution)/shard_map/all_gather | solution.py:336
  84.2 3.7 %shard_map.68 = (bf16[384,384]{1,0:T(8,128)(2,1)S(1)}, bf16[16,672,128]{2,1,0:T(8,128)(2,1)S(1)}) custom-call(bf16[384,4096]{1,0:T(8,128)(2,1)S(1)} %convert_element_type.13.x_ref, bf16[16,1344,128]{2,1,0:T(8,128)(2,1)} %bitcast.11), custom_call_target="tpu_custom_call" | custom-call | flops 1056964608 | bytes 5898240 | tf_op jit(solution)/shard_map/pallas_call | solution.py:213
  87.9 0.1 convert_element_type.14
  88.0 32.2 %all-gather.7 = f16[3072,384]{1,0:T(8,128)(2,1)S(1)} all-gather(f16[384,384]{1,0:T(8,128)(2,1)S(1)} %convert_element_type.14), channel_id=1, replica_groups=mesh['y'=8,'core'=2,'x'=4,'z'=8] {'z'}, dimensions={0}, use_global_device_ids=true | all-gather | bytes 2654208 | tf_op jit(solution)/shard_map/all_gather | solution.py:342
  120.1 0.4 convert_element_type.15
  120.6 1.3 shard_map.69.hid_ref
  121.9 0.0 copy-start.2
  121.9 0.0 copy-start.3
  122.0 1.3 shard_map.70
  123.3 21.1 %all_to_all.10.home_ref = bf16[32,48,128]{2,1,0:T(8,128)(2,1)S(1)} all-to-all(bf16[32,48,128]{2,1,0:T(8,128)(2,1)S(1)} %shard_map.70), channel_id=1, replica_groups=mesh['y'=8,'core'=2,'x'=4,'z'=8] {'x','z'}, dimensions={0} | all-to-all | bytes 786432 | tf_op jit(solution)/shard_map/all_to_all | solution.py:345
  144.4 0.0 copy-done.2
  144.4 0.0 copy-done.3
  144.4 1.9 %shard_map.71 = bf16[132,4096]{1,0:T(8,128)(2,1)} custom-call(s32[1]{0:T(128)} %bitcast.here_ref, s32[2,132]{1,0:T(2,128)S(1)} %bitcast.9, f32[2,132]{1,0:T(2,128)S(1)} %bitcast.10, f32[48,1]{1,0:T(8,128)S(1)} %get-tuple-element.17.shrink_ref, bf16[32,48,128]{2,1,0:T(8,128)(2,1)S(1)} %all_to_all.10.home_ref), custom_call_target="tpu_custom_call" | custom-call | tf_op jit(solution)/shard_map/pallas_call | solution.py:312
Async XLA Ops:
  8.6 27.5 %all-to-all-start = ((bf16[32,16,384]{2,1,0:T(8,128)(2,1)}), bf16[32,16,384]{2,1,0:T(8,128)(2,1)S(1)}, u32[]{:S(2)}, u32[]{:S(2)}) async-start(bf16[32,16,384]{2,1,0:T(8,128)(2,1)} %shard_map.65), calls=%async_computation | async-start | bytes 786432 | tf_op jit(solution)/shard_map/all_to_all | solution.py:327
  21.1 63.0 %all-gather.5.cloned.1.call-start = ((), (), s32[]{:S(2)}) async-start(), calls=%async_computation.2 | async-start | bytes 5849088 | tf_op jit(solution)/shard_map/all_gather | solution.py:336
  21.2 1.3 copy-start
  22.4 0.7 copy-start.1
  23.9 9.0 %collective-permute-start = (bf16[16,3072]{1,0:T(8,128)(2,1)S(1)}, bf16[16,3072]{1,0:T(8,128)(2,1)S(1)}, u32[]{:S(2)}, u32[]{:S(2)}) collective-permute-start(bf16[16,3072]{1,0:T(8,128)(2,1)S(1)} %get-tuple-element.19), channel_id=1, source_target_pairs={{0,8},{8,16},{16,24},{24,0},{1,9},{9,17},{17,25},{25,1},{2,10},{10... | collective-permute-start | bytes 294920 | tf_op jit(solution)/shard_map/ppermute | solution.py:331
  27.2 8.4 %collective-permute-start.1 = (bf16[16,3072]{1,0:T(8,128)(2,1)S(1)}, bf16[16,3072]{1,0:T(8,128)(2,1)S(1)}, u32[]{:S(2)}, u32[]{:S(2)}) collective-permute-start(bf16[16,3072]{1,0:T(8,128)(2,1)S(1)} %get-tuple-element.20), channel_id=1, source_target_pairs={{0,16},{8,24},{16,0},{24,8},{1,17},{9,25},{17,1},{25,9},{2,18},{10... | collective-permute-start | bytes 294920 | tf_op jit(solution)/shard_map/ppermute | solution.py:331
  37.2 6.5 %collective-permute-start.2 = (bf16[16,3072]{1,0:T(8,128)(2,1)S(1)}, bf16[16,3072]{1,0:T(8,128)(2,1)S(1)}, u32[]{:S(2)}, u32[]{:S(2)}) collective-permute-start(bf16[16,3072]{1,0:T(8,128)(2,1)S(1)} %get-tuple-element.23), channel_id=1, source_target_pairs={{0,24},{8,0},{16,8},{24,16},{1,25},{9,1},{17,9},{25,17},{2,26},{10... | collective-permute-start | bytes 294920 | tf_op jit(solution)/shard_map/ppermute | solution.py:331
  121.9 22.5 %copy-start.2 = (s32[132,2]{0,1:T(2,128)S(1)}, s32[132,2]{0,1:T(2,128)}, u32[]{:S(2)}) copy-start(s32[132,2]{0,1:T(2,128)} %param.7) | copy-start | bytes 3172
  121.9 22.5 %copy-start.3 = (f32[132,2]{0,1:T(2,128)S(1)}, f32[132,2]{0,1:T(2,128)}, u32[]{:S(2)}) copy-start(f32[132,2]{0,1:T(2,128)} %param.8) | copy-start | bytes 3172
Sparse Core Ops, SparseCore 0:
  37.3 46.8 all-gather.4

commit v12 on v11

--- a/solution.py
+++ b/solution.py
@@ -44,9 +44,8 @@
     return factor, power
 
 
-def dispatch_kernel(here_ref, routes_ref, tokens_ref, *refs):
-    out_refs, shrink_ref = refs[:FLIGHT], refs[FLIGHT]
-    piece = tokens_ref.shape[1] - out_refs[0].shape[1]
+def dispatch_kernel(here_ref, routes_ref, tokens_ref, out_ref, shrink_ref):
+    piece = tokens_ref.shape[1] - out_ref.shape[2]
     chunks = tokens_ref.shape[1] // piece
     taken, _, _ = place(routes_ref[...], here_ref[0])
     taken = taken.astype(F32).astype(BF16)
@@ -64,7 +63,7 @@
         for e in range(FLIGHT):
             at = e * PITCH
             tails = [rest[at + i : at + i + 1] for i in range(c, PITCH, chunks - 1)]
-            out_refs[e][:, c * piece : (c + 1) * piece] = jnp.concatenate([rows[at : at + PITCH]] + tails, axis=0).astype(BF16)
+            out_ref[e, :, c * piece : (c + 1) * piece] = jnp.concatenate([rows[at : at + PITCH]] + tails, axis=0).astype(BF16)
 
 
 def dispatch(here, routes_t, tokens):
@@ -79,25 +78,20 @@
             pl.BlockSpec(memory_space=pltpu.VMEM),
         ],
         out_shape=(
-            *[jax.ShapeDtypeStruct((SENT_ROWS, width - piece), BF16)] * FLIGHT,
+            jax.ShapeDtypeStruct((FLIGHT, SENT_ROWS, width - piece), BF16),
             jax.ShapeDtypeStruct((FLIGHT * PITCH, 1), F32),
         ),
         compiler_params=pltpu.CompilerParams(vmem_limit_bytes=VMEM_LIMIT),
     )(here, routes_t, tokens)
 
 
-def unpack_kernel(here_ref, *refs):
-    near, rows_ref = refs[:-1], refs[-1]
-    here = here_ref[0]
-    short = near[0].shape[1]
+def unpack_kernel(near_ref, rows_ref):
+    short = near_ref.shape[2]
     rest = rows_ref.shape[1] - short
     fold = short // rest
-    blocks = [ref[...].astype(F32) for ref in near]
     rows = []
-    for k in range(FLIGHT):
-        sent = blocks[(FLIGHT - 1 - k) % FLIGHT]
-        for x in range(FLIGHT - 1):
-            sent = jnp.where(here == x, blocks[(x - k) % FLIGHT], sent)
+    for e in range(FLIGHT):
+        sent = near_ref[e].astype(F32)
         tails = []
         for i in range(PITCH):
             at = PITCH + i // fold
@@ -106,21 +100,13 @@
     rows_ref[...] = jnp.concatenate(rows, axis=0).astype(BF16)
 
 
-def unpack(here, near):
-    height, short = near[0].shape
-    width = short * height // PITCH
-    whole = pl.BlockSpec((height, short), lambda i, m: (0, 0))
+def unpack(near):
+    flight, height, short = near.shape
     return pl.pallas_call(
         unpack_kernel,
-        grid_spec=pltpu.PrefetchScalarGridSpec(
-            num_scalar_prefetch=1,
-            grid=(1,),
-            in_specs=[whole] * len(near),
-            out_specs=pl.BlockSpec((len(near) * PITCH, width), lambda i, m: (0, 0)),
-        ),
-        out_shape=jax.ShapeDtypeStruct((len(near) * PITCH, width), BF16),
-        compiler_params=pltpu.CompilerParams(vmem_limit_bytes=VMEM_LIMIT),
-    )(here, *near)
+        out_shape=jax.ShapeDtypeStruct((flight * PITCH, short * height // PITCH), BF16),
+        compiler_params=pltpu.CompilerParams(vmem_limit_bytes=VMEM_LIMIT),
+    )(near)
 
 
 def split_kernel(up_ref, down_ref, out_ref):
@@ -321,20 +307,20 @@
     flight, _, total = dense_up.shape
     units = up_noise.shape[1]
     blocks = total // units
-    here = lax.axis_index("x").reshape(1)
+    here = jnp.zeros((1,), jnp.int32)
     mine = lax.axis_index("y") * lax.axis_size("core") + lax.axis_index("core")
 
     got = lax.all_to_all(split(dense_up, dense_down, blocks), ("x", "z"), 0, 0, tiled=True)
 
-    *near, shrink = dispatch(here, routes.T, tokens)
-    for s in range(1, flight):
-        near[s] = lax.ppermute(near[s], "x", [(i, (i + s) % flight) for i in range(flight)])
+    outgoing, shrink = dispatch(here, routes.T, tokens)
     span = up_noise.shape[0] // lax.axis_size(("y", "core"))
     noise = lax.dynamic_slice_in_dim(up_noise.T, mine * span, span, axis=1)
-    got, near[1], near[2], noise = lax.optimization_barrier((got, near[1], near[2], noise))
+    got, outgoing, noise = lax.optimization_barrier((got, outgoing, noise))
     shard = prepare(got, noise, total)
     weights = lax.all_gather(shard, ("y", "core"))
-    routed = unpack(here, near).astype(jnp.float16)
+    outgoing, _ = lax.optimization_barrier((outgoing, shard))
+    near = lax.all_to_all(outgoing, "x", 0, 0, tiled=True)
+    routed = unpack(near).astype(jnp.float16)
     routed, _ = lax.optimization_barrier((routed, shard))
     everyone = lax.all_gather(routed, "z", axis=0, tiled=True).astype(BF16)
 

time: 154 us -> 149 us (0.968)
  starting transfers between devices: 23.8 us -> 12.6 us
  blocking collectives: 87.3 us -> 95.6 us
    ppermute x3 -> x0, starting transfers between devices: 11.2 us -> none  [on_device(): lax.ppermute(near[s], 'x', [(i, (i + s) % flight) for i in range(flight)])]
    all_to_all x1, waiting for transfers between devices: 0.36 us -> 11.2 us  [on_device(): lax.all_to_all(split(dense_up, dense_down, blocks), ('x', 'z'), 0, 0, til...]
    all_to_all x0 -> x1, blocking collectives: none -> 9.94 us  [on_device(): near = lax.all_to_all(outgoing, 'x', 0, 0, tiled=True)]
    ppermute x3 -> x0, waiting for transfers between devices: 6.15 us -> none  [on_device(): lax.ppermute(near[s], 'x', [(i, (i + s) % flight) for i in range(flight)])]
    all_gather x1, waiting for transfers between devices: 5.74 us -> 0.02 us  [on_device(): weights = lax.all_gather(shard, ('y', 'core'))]
  transfers between devices with their start and end apart: 5 -> 2, of which waited for: 4 -> 1; matrix products, arithmetic and copies ran while one was open for 1% -> 1% of each run, Pallas kernels for 1% -> 1%
where the time goes in v12:
time: 149 us
  blocking collectives  95.6 us (64%)
  between operations  13.5 us (9%)
  starting transfers between devices  12.6 us (8%)
  Pallas kernels  12.3 us (8%)
  waiting for transfers between devices  11.3 us (8%)
  local copies, waits for them, and re-layouts  2.87 us (2%)
    all_gather x1, blocking collectives, on_device(): everyone = lax.all_gather(routed, 'z', axis=0, tiled=True).astype(BF16)  32.9 us
    all_gather x1, blocking collectives, on_device(): lax.all_gather(hidden.astype(jnp.float16), 'z', axis=0, tiled=True)  31.7 us
    all_to_all x1, blocking collectives, on_device(): home = lax.all_to_all(out, ('x', 'z'), 0, 0, tiled=True)  21.1 us
    all_to_all x1, starting transfers between devices, on_device(): lax.all_to_all(split(dense_up, dense_down, blocks), ('x', 'z'), 0, 0, til...  12.6 us
    all_to_all x1, waiting for transfers between devices, on_device(): lax.all_to_all(split(dense_up, dense_down, blocks), ('x', 'z'), 0, 0, til...  11.2 us
    all_to_all x1, blocking collectives, on_device(): near = lax.all_to_all(outgoing, 'x', 0, 0, tiled=True)  9.94 us
    pallas_call x1, Pallas kernels, up_project(): pl.pallas_call(up_kernel, in_specs=[pl.BlockSpec(memory_space=pltpu.VMEM)...  3.72 us
  transfers between devices with their start and end apart: 2, of which 1 were waited for; matrix products, arithmetic and copies ran while one was open for 1% of the time, Pallas kernels for 1%

profile of v12, /device:TPU:64, one launch (start us, length us, event | category | flops | bytes accessed | tf_op | source)
XLA Modules:
  0.0 149.1 jit_solution(4651420814759699971)
XLA Ops:
  6.5 2.0 %shard_map.65 = bf16[32,16,384]{2,1,0:T(8,128)(2,1)} custom-call(bf16[4,8,2688]{2,1,0:T(8,128)(2,1)} %up_ref.1, bf16[4,8,2688]{2,1,0:T(8,128)(2,1)} %down_ref.1), custom_call_target="tpu_custom_call" | custom-call | tf_op jit(solution)/shard_map/pallas_call | solution.py:129
  8.6 12.6 %all-to-all-start = ((bf16[32,16,384]{2,1,0:T(8,128)(2,1)}), bf16[32,16,384]{2,1,0:T(8,128)(2,1)S(1)}, u32[]{:S(2)}, u32[]{:S(2)}) async-start(bf16[32,16,384]{2,1,0:T(8,128)(2,1)} %shard_map.65), calls=%async_computation | async-start | bytes 786432 | tf_op jit(solution)/shard_map/all_to_all | solution.py:313
  21.1 0.0 all-gather.5.cloned.1.call-start
  21.2 0.0 copy-start
  21.2 1.2 copy-done
  22.4 0.0 copy-start.1
  22.5 0.7 copy-done.1
  23.1 0.7 shard_map.64
  23.9 0.9 dynamic-slice_bitcast_fusion.noise_ref
  24.8 11.2 %all-to-all-done.got_ref = bf16[32,16,384]{2,1,0:T(8,128)(2,1)S(1)} async-done(((bf16[32,16,384]{2,1,0:T(8,128)(2,1)}), bf16[32,16,384]{2,1,0:T(8,128)(2,1)S(1)}, u32[]{:S(2)}, u32[]{:S(2)}) %all-to-all-start) | async-done | bytes 393248 | tf_op jit(solution)/shard_map/all_to_all | solution.py:313
  36.0 1.1 shard_map.66
  37.1 0.0 all-gather.5.cloned.1.call-update
  37.2 9.9 %all_to_all.15.near_ref = bf16[4,16,3072]{2,1,0:T(8,128)(2,1)S(1)} all-to-all(bf16[4,16,3072]{2,1,0:T(8,128)(2,1)S(1)} %get-tuple-element.19), channel_id=1, replica_groups=mesh['y'=8,'core'=2,'x'=4,'z'=8] {'x'}, dimensions={0} | all-to-all | bytes 786432 | tf_op jit(solution)/shard_map/all_to_all | solution.py:322
  47.1 0.2 shard_map.67
  47.3 0.1 convert_element_type.12
  47.3 32.9 %all-gather.6 = f16[384,4096]{1,0:T(8,128)(2,1)S(1)} all-gather(f16[48,4096]{1,0:T(8,128)(2,1)S(1)} %convert_element_type.12), channel_id=1, replica_groups=mesh['y'=8,'core'=2,'x'=4,'z'=8] {'z'}, dimensions={0}, use_global_device_ids=true | all-gather | bytes 3538944 | tf_op jit(solution)/shard_map/all_gather | solution.py:325
  80.2 0.4 convert_element_type.13.x_ref
  80.6 0.0 all-gather.5.cloned.1.call-done
  80.6 3.7 %shard_map.68 = (bf16[384,384]{1,0:T(8,128)(2,1)S(1)}, bf16[16,672,128]{2,1,0:T(8,128)(2,1)S(1)}) custom-call(bf16[384,4096]{1,0:T(8,128)(2,1)S(1)} %convert_element_type.13.x_ref, bf16[16,1344,128]{2,1,0:T(8,128)(2,1)} %bitcast.10), custom_call_target="tpu_custom_call" | custom-call | flops 1056964608 | bytes 5898240 | tf_op jit(solution)/shard_map/pallas_call | solution.py:199
  84.4 0.1 convert_element_type.14
  84.4 31.7 %all-gather.7 = f16[3072,384]{1,0:T(8,128)(2,1)S(1)} all-gather(f16[384,384]{1,0:T(8,128)(2,1)S(1)} %convert_element_type.14), channel_id=1, replica_groups=mesh['y'=8,'core'=2,'x'=4,'z'=8] {'z'}, dimensions={0}, use_global_device_ids=true | all-gather | bytes 2654208 | tf_op jit(solution)/shard_map/all_gather | solution.py:328
  116.1 0.4 convert_element_type.15
  116.5 1.3 shard_map.69.hid_ref
  117.8 0.0 copy-start.2
  117.8 0.0 copy-start.3
  117.8 1.3 shard_map.70
  119.2 21.1 %all_to_all.16.home_ref = bf16[32,48,128]{2,1,0:T(8,128)(2,1)S(1)} all-to-all(bf16[32,48,128]{2,1,0:T(8,128)(2,1)S(1)} %shard_map.70), channel_id=1, replica_groups=mesh['y'=8,'core'=2,'x'=4,'z'=8] {'x','z'}, dimensions={0} | all-to-all | bytes 786432 | tf_op jit(solution)/shard_map/all_to_all | solution.py:331
  140.3 0.0 copy-done.2
  140.3 0.0 copy-done.3
  140.3 1.9 %shard_map.71 = bf16[132,4096]{1,0:T(8,128)(2,1)} custom-call(s32[1]{0:T(128)} %constant.4.clone.1.here_ref, s32[2,132]{1,0:T(2,128)S(1)} %bitcast.8, f32[2,132]{1,0:T(2,128)S(1)} %bitcast.9, f32[48,1]{1,0:T(8,128)S(1)} %get-tuple-element.14.shrink_ref, bf16[32,48,128]{2,1,0:T(8,128)(2,1)S(1)} %all_to_all.16.home_ref), custom_call_target="tpu_custom_call" | custom-call | tf_op jit(solution)/shard_map/pallas_call | solution.py:298
Async XLA Ops:
  8.6 27.5 %all-to-all-start = ((bf16[32,16,384]{2,1,0:T(8,128)(2,1)}), bf16[32,16,384]{2,1,0:T(8,128)(2,1)S(1)}, u32[]{:S(2)}, u32[]{:S(2)}) async-start(bf16[32,16,384]{2,1,0:T(8,128)(2,1)} %shard_map.65), calls=%async_computation | async-start | bytes 786432 | tf_op jit(solution)/shard_map/all_to_all | solution.py:313
  21.1 59.5 %all-gather.5.cloned.1.call-start = ((), (), s32[]{:S(2)}) async-start(), calls=%async_computation.3 | async-start | bytes 5849088 | tf_op jit(solution)/shard_map/all_gather | solution.py:320
  21.2 1.3 copy-start
  22.4 0.7 copy-start.1
  117.8 22.5 %copy-start.2 = (s32[132,2]{0,1:T(2,128)S(1)}, s32[132,2]{0,1:T(2,128)}, u32[]{:S(2)}) copy-start(s32[132,2]{0,1:T(2,128)} %param.7) | copy-start | bytes 3172
  117.8 22.5 %copy-start.3 = (f32[132,2]{0,1:T(2,128)S(1)}, f32[132,2]{0,1:T(2,128)}, u32[]{:S(2)}) copy-start(f32[132,2]{0,1:T(2,128)} %param.8) | copy-start | bytes 3172
Sparse Core Ops, SparseCore 0:
  37.3 42.8 all-gather.4

commit v13 on v12

--- a/solution.py
+++ b/solution.py
@@ -210,30 +210,18 @@
     )(x, w)
 
 
-def join_kernel(units, hid_ref, out_ref):
+def down_kernel(units, hid_ref, w_ref, out_ref):
     hidden = []
     for b in range(hid_ref.shape[0]):
         h = hid_ref[b].astype(F32)
         hidden.append(h[:, :units] * jnp.exp2(-h[:, units : units + 1]))
-    out_ref[...] = jnp.concatenate(hidden, axis=1).astype(BF16)
-
-
-def join(hid, units):
-    blocks, rows, _ = hid.shape
-    return pl.pallas_call(
-        lambda *r: join_kernel(units, *r),
-        out_shape=jax.ShapeDtypeStruct((rows, blocks * units), BF16),
-        compiler_params=pltpu.CompilerParams(vmem_limit_bytes=VMEM_LIMIT),
-    )(hid)
-
-
-def down_kernel(hid_ref, w_ref, out_ref):
+    hidden = jnp.concatenate(hidden, axis=1).astype(BF16)
     members, height, _ = w_ref.shape
-    tiles = hid_ref.shape[1] // LANES
+    tiles = hidden.shape[1] // LANES
     count = height // tiles
     w = [w_ref[:, q * count : (q + 1) * count].reshape(members * count, LANES) for q in range(tiles)]
     w = jnp.concatenate(w, axis=1)
-    out = lax.dot_general(hid_ref[...], w, (((1,), (1,)), ((), ())), preferred_element_type=F32)
+    out = lax.dot_general(hidden, w, (((1,), (1,)), ((), ())), preferred_element_type=F32)
     blocks = out_ref.shape[0] // FLIGHT
     for z in range(blocks):
         for x in range(FLIGHT):
@@ -242,12 +230,13 @@
             out_ref[x * blocks + z] = jnp.concatenate(tiles, axis=0).astype(BF16)
 
 
-def down_project(hid, w):
-    rows, total = hid.shape
+def down_project(hid, w, units):
+    sources, rows, _ = hid.shape
+    total = sources * units
     members, height, _ = w.shape
     cols = members * height * LANES // total
     return pl.pallas_call(
-        down_kernel,
+        lambda *r: down_kernel(units, *r),
         out_shape=jax.ShapeDtypeStruct((rows // PITCH, PITCH * cols // LANES, LANES), BF16),
         compiler_params=pltpu.CompilerParams(vmem_limit_bytes=VMEM_LIMIT),
         cost_estimate=pl.CostEstimate(flops=2 * rows * cols * total, bytes_accessed=2 * total * (cols + rows), transcendentals=0),
@@ -326,8 +315,7 @@
 
     hidden, down = up_project(everyone, weights, units)
     hidden = lax.all_gather(hidden.astype(jnp.float16), "z", axis=0, tiled=True).astype(BF16)
-    hidden = join(hidden.reshape(blocks, -1, HID_LANES), units)
-    out = down_project(hidden, down)
+    out = down_project(hidden.reshape(blocks, -1, HID_LANES), down, units)
     home = lax.all_to_all(out, ("x", "z"), 0, 0, tiled=True)
     return mix(here, routes.T, gate_values.T, shrink, home)
 

time: 149 us -> 149 us (level)
  no operation moved by 1% of the time
where the time goes in v13:
time: 149 us; the launch traced here: 148 us
  blocking collectives  95.6 us (64%)
  between operations  13.5 us (9%)
  starting transfers between devices  12.6 us (8%)
  Pallas kernels  11.5 us (8%)
  waiting for transfers between devices  11.3 us (8%)
  local copies, waits for them, and re-layouts  2.87 us (2%)
    all_gather x1, blocking collectives, on_device(): everyone = lax.all_gather(routed, 'z', axis=0, tiled=True).astype(BF16)  32.9 us
    all_gather x1, blocking collectives, on_device(): lax.all_gather(hidden.astype(jnp.float16), 'z', axis=0, tiled=True)  31.7 us
    all_to_all x1, blocking collectives, on_device(): home = lax.all_to_all(out, ('x', 'z'), 0, 0, tiled=True)  21.1 us
    all_to_all x1, starting transfers between devices, on_device(): lax.all_to_all(split(dense_up, dense_down, blocks), ('x', 'z'), 0, 0, til...  12.6 us
    all_to_all x1, waiting for transfers between devices, on_device(): lax.all_to_all(split(dense_up, dense_down, blocks), ('x', 'z'), 0, 0, til...  11.2 us
    all_to_all x1, blocking collectives, on_device(): near = lax.all_to_all(outgoing, 'x', 0, 0, tiled=True)  9.94 us
    pallas_call x1, Pallas kernels, up_project(): pl.pallas_call(up_kernel, in_specs=[pl.BlockSpec(memory_space=pltpu.VMEM)...  3.72 us
  transfers between devices with their start and end apart: 2, of which 1 were waited for; matrix products, arithmetic and copies ran while one was open for 1% of the time, Pallas kernels for 1%

profile of v13, /device:TPU:64, one launch (start us, length us, event | category | flops | bytes accessed | tf_op | source)
XLA Modules:
  0.0 148.3 jit_solution(6831972625645084577)
XLA Ops:
  6.5 2.0 %shard_map.65 = bf16[32,16,384]{2,1,0:T(8,128)(2,1)} custom-call(bf16[4,8,2688]{2,1,0:T(8,128)(2,1)} %up_ref.1, bf16[4,8,2688]{2,1,0:T(8,128)(2,1)} %down_ref.1), custom_call_target="tpu_custom_call" | custom-call | tf_op jit(solution)/shard_map/pallas_call | solution.py:129
  8.6 12.6 %all-to-all-start = ((bf16[32,16,384]{2,1,0:T(8,128)(2,1)}), bf16[32,16,384]{2,1,0:T(8,128)(2,1)S(1)}, u32[]{:S(2)}, u32[]{:S(2)}) async-start(bf16[32,16,384]{2,1,0:T(8,128)(2,1)} %shard_map.65), calls=%async_computation | async-start | bytes 786432 | tf_op jit(solution)/shard_map/all_to_all | solution.py:302
  21.1 0.0 all-gather.5.cloned.1.call-start
  21.2 0.0 copy-start
  21.2 1.2 copy-done
  22.4 0.0 copy-start.1
  22.5 0.7 copy-done.1
  23.1 0.7 shard_map.64
  23.9 0.9 dynamic-slice_bitcast_fusion.noise_ref
  24.8 11.2 %all-to-all-done.got_ref = bf16[32,16,384]{2,1,0:T(8,128)(2,1)S(1)} async-done(((bf16[32,16,384]{2,1,0:T(8,128)(2,1)}), bf16[32,16,384]{2,1,0:T(8,128)(2,1)S(1)}, u32[]{:S(2)}, u32[]{:S(2)}) %all-to-all-start) | async-done | bytes 393248 | tf_op jit(solution)/shard_map/all_to_all | solution.py:302
  36.0 1.1 shard_map.66
  37.1 0.0 all-gather.5.cloned.1.call-update
  37.2 9.9 %all_to_all.15.near_ref = bf16[4,16,3072]{2,1,0:T(8,128)(2,1)S(1)} all-to-all(bf16[4,16,3072]{2,1,0:T(8,128)(2,1)S(1)} %get-tuple-element.19), channel_id=1, replica_groups=mesh['y'=8,'core'=2,'x'=4,'z'=8] {'x'}, dimensions={0} | all-to-all | bytes 786432 | tf_op jit(solution)/shard_map/all_to_all | solution.py:311
  47.1 0.2 shard_map.67
  47.3 0.1 convert_element_type.12
  47.3 32.9 %all-gather.6 = f16[384,4096]{1,0:T(8,128)(2,1)S(1)} all-gather(f16[48,4096]{1,0:T(8,128)(2,1)S(1)} %convert_element_type.12), channel_id=1, replica_groups=mesh['y'=8,'core'=2,'x'=4,'z'=8] {'z'}, dimensions={0}, use_global_device_ids=true | all-gather | bytes 3538944 | tf_op jit(solution)/shard_map/all_gather | solution.py:314
  80.2 0.4 convert_element_type.13.x_ref
  80.6 0.0 all-gather.5.cloned.1.call-done
  80.6 3.7 %shard_map.68 = (bf16[384,384]{1,0:T(8,128)(2,1)S(1)}, bf16[16,672,128]{2,1,0:T(8,128)(2,1)S(1)}) custom-call(bf16[384,4096]{1,0:T(8,128)(2,1)S(1)} %convert_element_type.13.x_ref, bf16[16,1344,128]{2,1,0:T(8,128)(2,1)} %bitcast.10), custom_call_target="tpu_custom_call" | custom-call | flops 1056964608 | bytes 5898240 | tf_op jit(solution)/shard_map/pallas_call | solution.py:199
  84.4 0.1 convert_element_type.14
  84.4 31.7 %all-gather.7 = f16[3072,384]{1,0:T(8,128)(2,1)S(1)} all-gather(f16[384,384]{1,0:T(8,128)(2,1)S(1)} %convert_element_type.14), channel_id=1, replica_groups=mesh['y'=8,'core'=2,'x'=4,'z'=8] {'z'}, dimensions={0}, use_global_device_ids=true | all-gather | bytes 2654208 | tf_op jit(solution)/shard_map/all_gather | solution.py:317
  116.1 0.4 convert_element_type.15
  116.6 0.0 copy-start.2
  116.6 0.0 copy-start.3
  116.6 1.8 %shard_map.69 = bf16[32,48,128]{2,1,0:T(8,128)(2,1)S(1)} custom-call(bf16[8,384,384]{2,1,0:T(8,128)(2,1)S(1)} %bitcast.6, bf16[16,672,128]{2,1,0:T(8,128)(2,1)S(1)} %get-tuple-element.22.r_1_), custom_call_target="tpu_custom_call" | custom-call | flops 1056964608 | bytes 4816896 | tf_op jit(solution)/shard_map/pallas_call | solution.py:238
  118.4 21.1 %all_to_all.16.home_ref = bf16[32,48,128]{2,1,0:T(8,128)(2,1)S(1)} all-to-all(bf16[32,48,128]{2,1,0:T(8,128)(2,1)S(1)} %shard_map.69), channel_id=1, replica_groups=mesh['y'=8,'core'=2,'x'=4,'z'=8] {'x','z'}, dimensions={0} | all-to-all | bytes 786432 | tf_op jit(solution)/shard_map/all_to_all | solution.py:319
  139.5 0.0 copy-done.2
  139.5 0.0 copy-done.3
  139.5 1.9 %shard_map.70 = bf16[132,4096]{1,0:T(8,128)(2,1)} custom-call(s32[1]{0:T(128)} %constant.4.clone.1.here_ref, s32[2,132]{1,0:T(2,128)S(1)} %bitcast.8, f32[2,132]{1,0:T(2,128)S(1)} %bitcast.9, f32[48,1]{1,0:T(8,128)S(1)} %get-tuple-element.14.shrink_ref, bf16[32,48,128]{2,1,0:T(8,128)(2,1)S(1)} %all_to_all.16.home_ref), custom_call_target="tpu_custom_call" | custom-call | tf_op jit(solution)/shard_map/pallas_call | solution.py:287
Async XLA Ops:
  8.6 27.5 %all-to-all-start = ((bf16[32,16,384]{2,1,0:T(8,128)(2,1)}), bf16[32,16,384]{2,1,0:T(8,128)(2,1)S(1)}, u32[]{:S(2)}, u32[]{:S(2)}) async-start(bf16[32,16,384]{2,1,0:T(8,128)(2,1)} %shard_map.65), calls=%async_computation | async-start | bytes 786432 | tf_op jit(solution)/shard_map/all_to_all | solution.py:302
  21.1 59.5 %all-gather.5.cloned.1.call-start = ((), (), s32[]{:S(2)}) async-start(), calls=%async_computation.3 | async-start | bytes 5849088 | tf_op jit(solution)/shard_map/all_gather | solution.py:309
  21.2 1.3 copy-start
  22.4 0.7 copy-start.1
  116.6 23.0 %copy-start.2 = (s32[132,2]{0,1:T(2,128)S(1)}, s32[132,2]{0,1:T(2,128)}, u32[]{:S(2)}) copy-start(s32[132,2]{0,1:T(2,128)} %param.7) | copy-start | bytes 3172
  116.6 23.0 %copy-start.3 = (f32[132,2]{0,1:T(2,128)S(1)}, f32[132,2]{0,1:T(2,128)}, u32[]{:S(2)}) copy-start(f32[132,2]{0,1:T(2,128)} %param.8) | copy-start | bytes 3172
Sparse Core Ops, SparseCore 0:
  37.3 42.8 all-gather.4
